TPU v7x, 128 devices: a whole 4x4x4 slice. The times are simulated.
128 devices in a mesh: dp: 4 (over z_lo, core), eig: 32 (over z_hi, y, x).
Axes of the slice: x: 4, y: 4, z: 4 (z_hi: 2, z_lo: 2; z = z_hi * 2 + z_lo), core: 2. Of those that a mesh axis runs over, the one named last changes fastest.
Arguments:
- acts: bfloat16 [16, 256, 4096], P('dp', 'eig'), may hold values from -6 to 6
- grads: bfloat16 [16, 256, 11008], P('dp', 'eig'), may hold values from -0.375 to 0.375
- basis_in: bfloat16 [4096, 4096], P(None, 'eig'), may hold values from -0.09375 to 0.09375
- basis_out: bfloat16 [11008, 11008], P(None, 'eig'), may hold values from -0.0546875 to 0.0546875
Outputs:
- correction: float32 [11008, 4096], P('eig', 'dp')
All inputs are finite; a program needn't handle non-finite values.
Results may differ from a plain program's by a relative error of at most 0.002.
Values may be sent and summed in bfloat16 or wider, within the bound.
No kernel may reach another device: no remote copies, remote signals or barrier semaphores. Data moves between devices by JAX's collectives and lax.ppermute only.
A program may use at most 128 MiB of HBM per device.

v0:
```python
import jax
import jax.numpy as jnp
from jax import lax
from jax.sharding import PartitionSpec as P


def squares_sum(left, right):
    count = left.shape[0]

    def add_one(number, total):
        product = jnp.einsum(
            "si,sj->ij", left[number], right[number], preferred_element_type=jnp.float32
        )
        return total + product * product

    start = jnp.zeros((left.shape[2], right.shape[2]), jnp.float32)
    return lax.fori_loop(0, count, add_one, start)


def per_device(acts, grads, basis_in, basis_out):
    rot_grads = jnp.einsum(
        "esf,fk->esk",
        lax.all_gather(grads, "eig", axis=1, tiled=True),
        basis_out,
        preferred_element_type=jnp.float32,
    ).astype(jnp.bfloat16)
    own_cols = jnp.einsum(
        "esd,dk->esk",
        lax.all_gather(acts, "eig", axis=1, tiled=True),
        basis_in,
        preferred_element_type=jnp.float32,
    ).astype(jnp.bfloat16)
    rot_acts = lax.all_gather(own_cols, "eig", axis=2, tiled=True)
    groups = lax.axis_size("dp")
    examples = rot_grads.shape[0] * groups
    total = squares_sum(rot_grads, rot_acts)
    summed = lax.psum_scatter(total, "dp", scatter_dimension=1, tiled=True)
    return summed / examples


def solution(mesh):
    placed = (P("dp", "eig", None), P("dp", "eig", None), P(None, "eig"), P(None, "eig"))
    return jax.shard_map(
        per_device, mesh=mesh, in_specs=placed, out_specs=P("eig", "dp"), check_vma=False
    )
```

profile of v0, /device:TPU:1, one launch (start us, length us, event | category | flops | bytes accessed | tf_op | source)
XLA Modules:
  0.0 545.9 jit_solution(17641558090496222114)
XLA Ops:
  6.5 0.0 copy-start
  6.5 0.0 all-gather.6.cloned.1.call-start
  6.5 0.7 all-gather.6.cloned.1.call-update
  7.3 0.0 all-gather.4.cloned.1.call-start
  7.3 0.7 all-gather.4.cloned.1.call-update
  8.0 0.0 all-gather.8.cloned.1.call-start
  8.1 110.8 %all-gather.6.cloned.1.call-done = bf16[4,256,4096]{2,1,0:T(8,128)(2,1)} async-done(((bf16[4,8,4096]{2,1,0:T(8,128)(2,1)}), bf16[4,256,4096]{2,1,0:T(8,128)(2,1)}) %all-gather.6.cloned.1.call-update) | async-done | bytes 8388624 | tf_op jit(solution)/shard_map/all_gather | solution.py:29
  118.8 0.0 copy-done
  118.8 6.4 %convolution_convert_fusion = bf16[4,256,128]{2,1,0:T(8,128)(2,1)} fusion(bf16[4,256,4096]{2,1,0:T(8,128)(2,1)} %all-gather.6.cloned.1.call-done, bf16[4096,128]{1,0:T(8,128)(2,1)S(1)} %copy-done), kind=kOutput, calls=%fused_computation.10 | convolution fusion | flops 1073872896 | bytes 9699328 | tf_op jit(solution)/shard_map/esd,dk->esk/dot_general | solution.py:27
  125.3 0.0 all-gather.8.cloned.1.call-update
  125.3 0.0 reduce-scatter.2.cloned.1.call-start
  125.3 187.6 %all-gather.4.cloned.1.call-done = bf16[4,256,11008]{2,1,0:T(8,128)(2,1)} async-done(((bf16[4,8,11008]{2,1,0:T(8,128)(2,1)}), bf16[4,256,11008]{2,1,0:T(8,128)(2,1)}) %all-gather.4.cloned.1.call-update) | async-done | bytes 22544400 | tf_op jit(solution)/shard_map/all_gather | solution.py:23
  312.9 14.7 %fusion.8 = bf16[4,256,344]{1,2,0:T(8,128)(2,1)S(1)} fusion(bf16[4,256,11008]{2,1,0:T(8,128)(2,1)} %all-gather.4.cloned.1.call-done, bf16[11008,344]{0,1:T(8,128)(2,1)} %param.9), kind=kOutput, calls=%fused_computation.9 | convolution fusion | flops 7755620352 | bytes 30822400 | tf_op jit(solution)/shard_map/esf,fk->esk/dot_general | solution.py:21
  327.6 127.4 %all-gather.8.cloned.1.call-done = bf16[4,256,4096]{2,1,0:T(8,128)(2,1)} async-done(((bf16[4,256,128]{2,1,0:T(8,128)(2,1)}), bf16[4,256,4096]{2,1,0:T(8,128)(2,1)}) %all-gather.8.cloned.1.call-update) | async-done | bytes 8388624 | tf_op jit(solution)/shard_map/all_gather | solution.py:33
  455.0 24.6 %while.14 = (s32[]{:T(128)}, f32[344,4096]{1,0:T(8,128)}, bf16[4,256,344]{1,2,0:T(8,128)(2,1)S(1)}, bf16[4,256,4096]{2,1,0:T(8,128)(2,1)}, s32[]{:T(128)}, /*index=5*/s32[]{:T(128)}) while((s32[]{:T(128)}, f32[344,4096]{1,0:T(8,128)}, bf16[4,256,344]{1,2,0:T(8,128)(2,1)S(1)}, bf16[4,256,4096]{2,1,0:T(8,128)(2,1)}, s32[]{:T(128)}, ...), condition=%wide.region_1.0_spmd.clone, body=%wide.region_0.0_spmd.clone.sunk | while | flops 725647360 | bytes 13546575 | solution.py:17
  455.0 4.9 fusion.19
  459.9 6.6 %fusion.19 = f32[344,4096]{1,0:T(8,128)} fusion(f32[344,4096]{1,0:T(8,128)} %get-tuple-element.144, pred[]{:T(512)S(6)} %compare.3, bf16[4,256,4096]{2,1,0:T(8,128)(2,1)} %get-tuple-element.152, s32[]{:T(128)} %get-tuple-element.143, bf16[4,256,344]{1,2,0:T(8,128)(2,1)S(1)} %get-tuple-element.151), kind=kOutput, calls=%fused_computation.1.clone.1 | convolution fusion | flops 725647360 | bytes 13546497 | tf_op jit(solution)/shard_map/while/body/eval_jaxpr/si,sj->ij/dot_general | solution.py:11
  466.5 6.6 %fusion.19 = f32[344,4096]{1,0:T(8,128)} fusion(f32[344,4096]{1,0:T(8,128)} %get-tuple-element.144, pred[]{:T(512)S(6)} %compare.3, bf16[4,256,4096]{2,1,0:T(8,128)(2,1)} %get-tuple-element.152, s32[]{:T(128)} %get-tuple-element.143, bf16[4,256,344]{1,2,0:T(8,128)(2,1)S(1)} %get-tuple-element.151), kind=kOutput, calls=%fused_computation.1.clone.1 | convolution fusion | flops 725647360 | bytes 13546497 | tf_op jit(solution)/shard_map/while/body/eval_jaxpr/si,sj->ij/dot_general | solution.py:11
  473.1 6.6 %fusion.19 = f32[344,4096]{1,0:T(8,128)} fusion(f32[344,4096]{1,0:T(8,128)} %get-tuple-element.144, pred[]{:T(512)S(6)} %compare.3, bf16[4,256,4096]{2,1,0:T(8,128)(2,1)} %get-tuple-element.152, s32[]{:T(128)} %get-tuple-element.143, bf16[4,256,344]{1,2,0:T(8,128)(2,1)S(1)} %get-tuple-element.151), kind=kOutput, calls=%fused_computation.1.clone.1 | convolution fusion | flops 725647360 | bytes 13546497 | tf_op jit(solution)/shard_map/while/body/eval_jaxpr/si,sj->ij/dot_general | solution.py:11
  479.6 0.0 reduce-scatter.2.cloned.1.call-update
  479.6 57.1 %reduce-scatter.2.cloned.1.call-done = f32[344,1024]{1,0:T(8,128)} async-done(((f32[344,4096]{1,0:T(8,128)}), f32[344,1024]{1,0:T(8,128)}) %reduce-scatter.2.cloned.1.call-update) | async-done | bytes 1409040 | tf_op jit(solution)/shard_map/reduce_scatter | solution.py:37
  536.8 2.6 broadcast_multiply_fusion
  (1 shorter events, 0.0 us)
Async XLA Ops:
  6.5 112.3 %copy-start = (bf16[4096,128]{1,0:T(8,128)(2,1)S(1)}, bf16[4096,128]{1,0:T(8,128)(2,1)}, u32[]{:S(2)}) copy-start(bf16[4096,128]{1,0:T(8,128)(2,1)} %param.8) | copy-start | bytes 3145732
  6.5 112.3 %all-gather.6.cloned.1.call-start = ((), (), s32[]{:S(2)}) async-start(), calls=%async_computation.2 | async-start | bytes 8650752 | tf_op jit(solution)/shard_map/all_gather | solution.py:29
  7.3 305.6 %all-gather.4.cloned.1.call-start = ((), (), s32[]{:S(2)}) async-start(), calls=%async_computation.1 | async-start | bytes 23248896 | tf_op jit(solution)/shard_map/all_gather | solution.py:23
  8.0 447.0 %all-gather.8.cloned.1.call-start = ((), (), s32[]{:S(2)}) async-start(), calls=%async_computation.3 | async-start | bytes 8650752 | tf_op jit(solution)/shard_map/all_gather | solution.py:33
  125.3 411.5 %reduce-scatter.2.cloned.1.call-start = ((), (), s32[]{:S(2)}) async-start(), calls=%async_computation.4 | async-start | bytes 7045120 | tf_op jit(solution)/shard_map/reduce_scatter | solution.py:37
Sparse Core Ops, SparseCore 0:
  10.5 108.3 all-gather.5
  121.8 191.0 all-gather.3
  315.7 139.2 all-gather.7
  479.8 56.9 reduce-scatter.1
where the time goes:
time: 546 us
  waiting for transfers between devices  484 us (89%)
  matrix products  45.7 us (8%)
  between operations  13.1 us (2%)
    all_gather x1, waiting for transfers between devices, per_device(): lax.all_gather(grads, 'eig', axis=1, tiled=True)  188 us
    all_gather x1, waiting for transfers between devices, per_device(): rot_acts = lax.all_gather(own_cols, 'eig', axis=2, tiled=True)  127 us
    all_gather x1, waiting for transfers between devices, per_device(): lax.all_gather(acts, 'eig', axis=1, tiled=True)  111 us
    reduce_scatter x1, waiting for transfers between devices, per_device(): summed = lax.psum_scatter(total, 'dp', scatter_dimension=1, tiled=True)  57.1 us
    dot_general x4, matrix products, add_one(): jnp.einsum('si,sj->ij', left[number], right[number], preferred_element_ty...  24.6 us
    dot_general x1, matrix products, per_device(): jnp.einsum('esf,fk->esk', lax.all_gather(grads, 'eig', axis=1, tiled=True...  14.7 us
  transfers between devices with their start and end apart: 4, of which 4 were waited for; matrix products, arithmetic and copies ran while one was open for 4% of the time, Pallas kernels for 0%

commit v1 on v0

v1 whole, which is shorter than its diff:
```python
import jax
import jax.numpy as jnp
from jax import lax
from jax.experimental import pallas as pl
from jax.experimental.pallas import tpu as pltpu
from jax.sharding import Mesh
from jax.sharding import PartitionSpec as P

AXES = ("zl", "c", "zh", "y", "x")


def near_pairs(axis, step):
    masks = ((1, 3), (3, 1))
    table = [
        (core * 4 + i, core * 4 + (i ^ masks[core][step])) for core in range(2) for i in range(4)
    ]
    return lambda v: lax.ppermute(v, ("c", axis), table)


def order_of(half):
    first, second = ("x", "y") if half == 0 else ("y", "x")
    return ((first, 0), (first, 1), (second, 0), (second, 1))


def flip_zh(v):
    return lax.ppermute(v, "zh", [(0, 1), (1, 0)])


def flip_zl(v):
    return lax.ppermute(v, "zl", [(0, 1), (1, 0)])


def flip_both(v):
    return lax.ppermute(v, ("zl", "zh"), [(i, 3 - i) for i in range(4)])


def flip_core(v):
    return lax.ppermute(v, "c", [(0, 1), (1, 0)])


def turned(v, axis, core):
    size = v.shape[axis] // 2
    parts = [lax.dynamic_slice_in_dim(v, start * size, size, axis) for start in (core, 1 - core)]
    return jnp.concatenate(parts, axis)


def gather_tokens(v, half):
    for axis, step in order_of(half):
        v = jnp.concatenate([v, near_pairs(axis, step)(v)], 1)
    return v


def gather_columns(v, half):
    examples, tokens, columns = v.shape
    swapped = v.reshape(examples, tokens // 16, 2, 8, columns)[:, :, ::-1].reshape(v.shape)
    (axis, step), *rest = order_of(half)
    v = jnp.stack([v, near_pairs(axis, step)(swapped)])
    for axis, step in rest[:-1]:
        v = jnp.concatenate([v, near_pairs(axis, step)(v)], 0)
    axis, step = rest[-1]
    return v, near_pairs(axis, step)(v)


def product_kernel(place_ref, *refs):
    lefts, rights, out_ref = refs[:8], refs[8:12], refs[12]
    def left(half, group, example):
        pair = [lefts[half * 4 + group * 2 + i] for i in range(2)]
        return jnp.concatenate([r[:, example * 128 : (example + 1) * 128] for r in pair], 1)

    def right(half, piece, example):
        ref = rights[half * 2 + piece // 8]
        tiles = []
        for side in range(2):
            for u in range(8):
                row = side * 128 + (u ^ (piece >> 1)) * 16
                tiles.append(ref[piece % 8, example, row : row + 16, :])
        return jnp.concatenate(tiles, 0)

    for pair in range(8):
        sources = (2 * pair, 2 * pair + 1)
        total = None
        for half in range(2):
            pieces = [s if half == 0 else (s % 4) * 4 + s // 4 for s in sources]
            for group in range(2):
                for example in range(2):
                    rhs = jnp.concatenate(
                        [right(half, piece, group * 2 + example) for piece in pieces], 1
                    )
                    product = jnp.dot(
                        left(half, group, example), rhs, preferred_element_type=jnp.float32
                    )
                    square = product * product
                    total = square if total is None else total + square
        total = total * (1.0 / 16.0)
        for i, s in enumerate(sources):
            place = place_ref[s]
            column = pl.multiple_of(lax.rem(place, 8) * 128, 128)
            out_ref[place // 8, :, pl.ds(column, 128)] = total[:, i * 128 : (i + 1) * 128]


def product(places, lefts, rights):
    rows = lefts[0].shape[0]
    vmem = pl.BlockSpec(memory_space=pltpu.VMEM)
    return pl.pallas_call(
        product_kernel,
        out_shape=jax.ShapeDtypeStruct((2, rows, 1024), jnp.float32),
        in_specs=[pl.BlockSpec(memory_space=pltpu.SMEM)] + [vmem] * 12,
        out_specs=vmem,
        compiler_params=pltpu.CompilerParams(vmem_limit_bytes=40 * 1024 * 1024),
        cost_estimate=pl.CostEstimate(
            flops=2 * 8 * 256 * rows * 2048, bytes_accessed=14_000_000, transcendentals=0
        ),
        name="squares",
    )(places, *lefts, *rights)


def per_device(acts, grads, basis_in, basis_out):
    core, zl, zh = lax.axis_index("c"), lax.axis_index("zl"), lax.axis_index("zh")
    y, x = lax.axis_index("y"), lax.axis_index("x")

    acts = turned(acts, 2, core)
    basis_in = turned(basis_in, 0, core)
    part = flip_both(basis_in[:2048])
    other_in = jnp.concatenate([part, flip_core(part)], 0)
    own_acts = [gather_tokens(acts[2 * h : 2 * h + 2], h) for h in range(2)]

    grads = turned(grads, 2, core)
    basis_out = turned(basis_out, 0, core)
    part = flip_both(basis_out[:5504])
    other_out = jnp.concatenate([part, flip_core(part)], 0)
    own_grads = [gather_tokens(grads[2 * h : 2 * h + 2], h) for h in range(2)]

    def rotate(tokens, basis):
        return jnp.einsum(
            "esd,dk->esk", tokens, basis, preferred_element_type=jnp.float32
        ).astype(jnp.bfloat16)

    def rotate_turned(tokens, basis):
        return jnp.einsum(
            "esf,fk->kes", tokens, basis, preferred_element_type=jnp.float32
        ).astype(jnp.bfloat16).reshape(basis.shape[1], -1)

    rights = []
    for h in range(2):
        both = rotate(own_acts[h], jnp.concatenate([basis_in, other_in], 1))
        mine, theirs = both[..., :128], both[..., 128:]
        same = zh == zl
        keep, give = jnp.where(same, mine, theirs), jnp.where(same, theirs, mine)
        columns = jnp.concatenate(
            [
                jnp.concatenate([keep, flip_zh(keep)], 1),
                jnp.concatenate([flip_zl(give), flip_both(give)], 1),
            ],
            0,
        )
        rights += list(gather_columns(columns, h))

    lefts = []
    for h in range(2):
        mine = rotate_turned(own_grads[h], basis_out)
        theirs = rotate_turned(own_grads[h], other_out)
        lefts += [mine, flip_zh(theirs), flip_zl(mine), flip_both(theirs)]

    low, high = jnp.where(core == 0, 1, 3), jnp.where(core == 0, 3, 1)

    def mask(bits):
        return (low if bits & 1 else 0) ^ (high if bits & 2 else 0)

    places = jnp.stack(
        [((y ^ mask(s // 4)) * 4 + (x ^ mask(s % 4))) ^ (core * 8) for s in range(16)]
    ).astype(jnp.int32)
    sums = product(places, lefts, rights)
    return sums[0] + flip_core(sums[1])


def solution(mesh):
    fine = Mesh(mesh.devices.reshape(2, 2, 2, 4, 4), AXES)
    dp, eig = ("zl", "c"), ("zh", "y", "x")
    placed = (P(dp, eig, None), P(dp, eig, None), P(None, eig), P(None, eig))
    return jax.shard_map(
        per_device, mesh=fine, in_specs=placed, out_specs=P(eig, dp), check_vma=False
    )
```

time: 546 us -> 299 us (0.55)
  waiting for transfers between devices: 484 us -> 144 us
  starting transfers between devices: 0.12 us -> 73.8 us
  local copies, waits for them, and re-layouts: 0.01 us -> 30 us
  matrix products: 45.7 us -> 26.9 us
  other arithmetic: 2.61 us -> 16.8 us
  between operations: 13.1 us -> 0.44 us
  Pallas kernels: 0 us -> 5.71 us
    all_gather x3 -> x0, waiting for transfers between devices: 426 us -> none  [the longest x1 188 us: per_device(): lax.all_gather(grads, 'eig', axis=1, tiled=True)]
    ppermute x0 -> x41, waiting for transfers between devices: none -> 144 us  [the longest x6 79.8 us: flip_both(): return lax.ppermute(v, ('zl', 'zh'), [(i, 3 - i) for i in range(4)])]
    ppermute x0 -> x41, starting transfers between devices: none -> 73.8 us  [the longest x3 27.7 us: flip_core(): return lax.ppermute(v, 'c', [(0, 1), (1, 0)])]
    reduce_scatter x1 -> x0, waiting for transfers between devices: 57.1 us -> none  [per_device(): summed = lax.psum_scatter(total, 'dp', scatter_dimension=1, tiled=True)]
    dot_general x6, matrix products: 45.7 us -> 26.9 us  [the longest x4 23.4 us: rotate_turned(): jnp.einsum('esf,fk->kes', tokens, basis, preferred_element_type=jnp.float32)]
    unnamed x2 -> x58, local copies, waits for them, and re-layouts: 0.01 us -> 12.8 us
    dynamic_slice x0 -> x4, local copies, waits for them, and re-layouts: none -> 10 us  [turned(): lax.dynamic_slice_in_dim(v, start * size, size, axis)]
    concatenate x0 -> x16, other arithmetic: none -> 8.36 us  [the longest x12 4.48 us: gather_tokens(): v = jnp.concatenate([v, near_pairs(axis, step)(v)], 1)]
  transfers between devices with their start and end apart: 4 -> 41, of which waited for: 4 -> 16; matrix products, arithmetic and copies ran while one was open for 4% -> 22% of each run, Pallas kernels for 0% -> 0%
where the time goes in v1:
time: 299 us; the launch traced here: 298 us
  waiting for transfers between devices  144 us (48%)
  starting transfers between devices  73.8 us (25%)
  local copies, waits for them, and re-layouts  30 us (10%)
  matrix products  26.9 us (9%)
  other arithmetic  16.8 us (6%)
  Pallas kernels  5.71 us (2%)
    ppermute x6, waiting for transfers between devices, flip_both(): return lax.ppermute(v, ('zl', 'zh'), [(i, 3 - i) for i in range(4)])  79.8 us
    ppermute x24, waiting for transfers between devices, near_pairs(): return lambda v: lax.ppermute(v, ('c', axis), table)  61.7 us
    ppermute x3, starting transfers between devices, flip_core(): return lax.ppermute(v, 'c', [(0, 1), (1, 0)])  27.7 us
    ppermute x24, starting transfers between devices, near_pairs(): return lambda v: lax.ppermute(v, ('c', axis), table)  27.2 us
    dot_general x4, matrix products, rotate_turned(): jnp.einsum('esf,fk->kes', tokens, basis, preferred_element_type=jnp.float32)  23.4 us
    unnamed x58, local copies, waits for them, and re-layouts  12.8 us
    ppermute x6, starting transfers between devices, flip_both(): return lax.ppermute(v, ('zl', 'zh'), [(i, 3 - i) for i in range(4)])  10.3 us
    dynamic_slice x4, local copies, waits for them, and re-layouts, turned(): lax.dynamic_slice_in_dim(v, start * size, size, axis)  10 us
  transfers between devices with their start and end apart: 41, of which 16 were waited for; matrix products, arithmetic and copies ran while one was open for 22% of the time, Pallas kernels for 0%

profile of v1, /device:TPU:1, one launch (start us, length us, event | category | flops | bytes accessed | tf_op | source)
XLA Modules:
  0.0 298.1 jit_solution(3188178501590764977)
XLA Ops:
  2.1 3.3 %collective-permute-start = (bf16[2,8,11008]{2,1,0:T(8,128)(2,1)S(1)}, bf16[2,8,11008]{2,1,0:T(8,128)(2,1)S(1)}, u32[]{:S(2)}, u32[]{:S(2)}) collective-permute-start(bf16[2,8,11008]{2,1,0:T(8,128)(2,1)S(1)} %get-tuple-element.18), channel_id=1, source_target_pairs={{0,1},{1,0},{2,3},{3,2},{32,35},{33,34},{34,33},{35,32},{4,5},{5,4... | collective-permute-start | bytes 1056776 | tf_op jit(solution)/shard_map/ppermute | solution.py:17
  5.4 6.8 %constant_dynamic-slice_fusion.7 = (bf16[5504,344]{0,1:T(8,128)(2,1)}, bf16[5504,344]{0,1:T(8,128)(2,1)}) fusion(bf16[11008,344]{0,1:T(8,128)(2,1)} %param.7, s32[]{:T(128)S(6)} %select_n.45, s32[]{:T(128)S(6)} %select_n.46), kind=kLoop, calls=%fused_computation.83 | loop fusion | bytes 15147016 | tf_op jit(solution)/shard_map/dynamic_slice | solution.py:43
  12.2 3.8 %collective-permute-start.4 = (bf16[5504,344]{0,1:T(8,128)(2,1)}, bf16[5504,344]{0,1:T(8,128)(2,1)}, u32[]{:S(2)}, u32[]{:S(2)}) collective-permute-start(bf16[5504,344]{0,1:T(8,128)(2,1)} %get-tuple-element.13), channel_id=1, source_target_pairs={{0,80},{16,64},{64,16},{80,0},{1,81},{17,65},{65,17},{81,1},{2,82}... | collective-permute-start | bytes 11360264 | tf_op jit(solution)/shard_map/ppermute | solution.py:34
  21.7 3.2 %collective-permute-done.16 = bf16[2,8,4096]{2,1,0:T(8,128)(2,1)S(1)} collective-permute-done((bf16[2,8,4096]{2,1,0:T(8,128)(2,1)S(1)}, bf16[2,8,4096]{2,1,0:T(8,128)(2,1)S(1)}, u32[]{:S(2)}, u32[]{:S(2)}) %collective-permute-start.16) | collective-permute-done | bytes 131104 | tf_op jit(solution)/shard_map/ppermute | solution.py:17
  25.6 4.7 %collective-permute-done.29 = bf16[2,8,4096]{2,1,0:T(8,128)(2,1)S(1)} collective-permute-done((bf16[2,8,4096]{2,1,0:T(8,128)(2,1)S(1)}, bf16[2,8,4096]{2,1,0:T(8,128)(2,1)S(1)}, u32[]{:S(2)}, u32[]{:S(2)}) %collective-permute-start.29) | collective-permute-done | bytes 131104 | tf_op jit(solution)/shard_map/ppermute | solution.py:17
  36.7 72.9 %collective-permute-done.20 = bf16[2048,128]{1,0:T(8,128)(2,1)} collective-permute-done((bf16[2048,128]{1,0:T(8,128)(2,1)S(1)}, bf16[2048,128]{1,0:T(8,128)(2,1)}, u32[]{:S(2)}, u32[]{:S(2)}) %collective-permute-start.20) | collective-permute-done | bytes 524320 | tf_op jit(solution)/shard_map/ppermute | solution.py:34
  110.6 8.2 %collective-permute-done.31 = bf16[2,32,4096]{2,1,0:T(8,128)(2,1)S(1)} collective-permute-done((bf16[2,32,4096]{2,1,0:T(8,128)(2,1)S(1)}, bf16[2,32,4096]{2,1,0:T(8,128)(2,1)S(1)}, u32[]{:S(2)}, u32[]{:S(2)}) %collective-permute-start.31) | collective-permute-done | bytes 524320 | tf_op jit(solution)/shard_map/ppermute | solution.py:17
  125.6 12.7 %collective-permute-done.19 = bf16[2,64,4096]{2,1,0:T(8,128)(2,1)S(1)} collective-permute-done((bf16[2,64,4096]{2,1,0:T(8,128)(2,1)S(1)}, bf16[2,64,4096]{2,1,0:T(8,128)(2,1)S(1)}, u32[]{:S(2)}, u32[]{:S(2)}) %collective-permute-start.19) | collective-permute-done | bytes 1048608 | tf_op jit(solution)/shard_map/ppermute | solution.py:17
  140.2 3.0 %collective-permute-start.24 = (bf16[2,128,128]{2,1,0:T(8,128)(2,1)S(1)}, bf16[2,128,128]{2,1,0:T(8,128)(2,1)S(1)}, u32[]{:S(2)}, u32[]{:S(2)}) collective-permute-start(bf16[2,128,128]{2,1,0:T(8,128)(2,1)S(1)} %get-tuple-element.32), channel_id=1, source_target_pairs={{0,80},{16,64},{64,16},{80,0},{1,81},{17,65},{65,17},{81,1},{2,82}... | collective-permute-start | bytes 196616 | tf_op jit(solution)/shard_map/ppermute | solution.py:34
  159.6 5.0 %collective-permute-start.36 = (bf16[4,256,128]{2,1,0:T(8,128)(2,1)}, bf16[4,256,128]{2,1,0:T(8,128)(2,1)S(1)}, u32[]{:S(2)}, u32[]{:S(2)}) collective-permute-start(bf16[4,256,128]{2,1,0:T(8,128)(2,1)} %bitcast.96), channel_id=1, source_target_pairs={{0,4},{4,0},{8,12},{12,8},{32,44},{36,40},{40,36},{44,32},{1,5},{5... | collective-permute-start | bytes 786440 | tf_op jit(solution)/shard_map/ppermute | solution.py:17
  165.5 9.8 %collective-permute-done.25 = bf16[4,256,128]{2,1,0:T(8,128)(2,1)} collective-permute-done((bf16[4,256,128]{2,1,0:T(8,128)(2,1)}, bf16[4,256,128]{2,1,0:T(8,128)(2,1)}, u32[]{:S(2)}, u32[]{:S(2)}) %collective-permute-start.25) | collective-permute-done | bytes 262176 | tf_op jit(solution)/shard_map/ppermute | solution.py:17
  183.4 4.3 %collective-permute-done.26 = bf16[2,4,256,128]{3,2,1,0:T(8,128)(2,1)S(1)} collective-permute-done((bf16[2,4,256,128]{3,2,1,0:T(8,128)(2,1)S(1)}, bf16[2,4,256,128]{3,2,1,0:T(8,128)(2,1)S(1)}, u32[]{:S(2)}, u32[]{:S(2)}) %collective-permute-start.26) | collective-permute-done | bytes 524320 | tf_op jit(solution)/shard_map/ppermute | solution.py:17
  188.8 3.5 %collective-permute-start.27 = (bf16[4,4,256,128]{3,2,1,0:T(8,128)(2,1)S(1)}, bf16[4,4,256,128]{3,2,1,0:T(8,128)(2,1)S(1)}, u32[]{:S(2)}, u32[]{:S(2)}) collective-permute-start(bf16[4,4,256,128]{3,2,1,0:T(8,128)(2,1)S(1)} %pad_maximum_fusion.7), channel_id=1, source_target_pairs={{0,4},{4,0},{8,12},{12,8},{32,44},{36,40},{40,36},{44,32},{1,5},{5... | collective-permute-start | bytes 3145736 | tf_op jit(solution)/shard_map/ppermute | solution.py:17
  195.8 13.1 %collective-permute-start.5 = (bf16[5504,344]{0,1:T(8,128)(2,1)}, bf16[5504,344]{0,1:T(8,128)(2,1)}, u32[]{:S(2)}, u32[]{:S(2)}) collective-permute-start(bf16[5504,344]{0,1:T(8,128)(2,1)} %collective-permute-done.4), channel_id=1, source_target_pairs={{0,32},{32,0},{1,33},{33,1},{2,34},{34,2},{3,35},{35,3},{4,36},{36... | collective-permute-start | bytes 11360264 | tf_op jit(solution)/shard_map/ppermute | solution.py:38
  208.9 6.3 %collective-permute-done.27 = bf16[4,4,256,128]{3,2,1,0:T(8,128)(2,1)S(1)} collective-permute-done((bf16[4,4,256,128]{3,2,1,0:T(8,128)(2,1)S(1)}, bf16[4,4,256,128]{3,2,1,0:T(8,128)(2,1)S(1)}, u32[]{:S(2)}, u32[]{:S(2)}) %collective-permute-start.27) | collective-permute-done | bytes 1048608 | tf_op jit(solution)/shard_map/ppermute | solution.py:17
  218.6 9.4 %collective-permute-done.3 = bf16[2,64,11008]{2,1,0:T(8,128)(2,1)S(1)} collective-permute-done((bf16[2,64,11008]{2,1,0:T(8,128)(2,1)S(1)}, bf16[2,64,11008]{2,1,0:T(8,128)(2,1)S(1)}, u32[]{:S(2)}, u32[]{:S(2)}) %collective-permute-start.3) | collective-permute-done | bytes 2818080 | tf_op jit(solution)/shard_map/ppermute | solution.py:17
  230.7 6.0 %fusion.12 = bf16[2,43,8,128]{3,2,1,0:T(8,128)(2,1)S(1)} fusion(bf16[2,128,11008]{2,1,0:T(8,128)(2,1)} %copy-done.14, bf16[5504,344]{0,1:T(8,128)(2,1)S(1)} %copy-done.9, bf16[5504,344]{0,1:T(8,128)(2,1)} %get-tuple-element.13), kind=kOutput, calls=%fused_computation.25 | convolution fusion | flops 1954052096 | bytes 13385728 | tf_op jit(solution)/shard_map/esf,fk->kes/dot_general | solution.py:139
  238.8 6.2 %fusion.11 = bf16[2,43,8,128]{3,2,1,0:T(8,128)(2,1)S(1)} fusion(bf16[2,128,11008]{2,1,0:T(8,128)(2,1)} %constant_dynamic-update-slice_fusion.5, bf16[5504,344]{0,1:T(8,128)(2,1)S(1)} %copy-done.9, bf16[5504,344]{0,1:T(8,128)(2,1)} %get-tuple-element.13), kind=kOutput, calls=%fused_computation.24 | convolution fusion | flops 1954052096 | bytes 13385728 | tf_op jit(solution)/shard_map/esf,fk->kes/dot_general | solution.py:139
  246.4 5.8 %fusion.10 = bf16[2,43,8,128]{3,2,1,0:T(8,128)(2,1)S(1)} fusion(bf16[2,128,11008]{2,1,0:T(8,128)(2,1)S(1)} %bitcast.102, bf16[5504,344]{0,1:T(8,128)(2,1)} %collective-permute-done.5, bf16[5504,344]{0,1:T(8,128)(2,1)} %collective-permute-done.4), kind=kOutput, calls=%fused_computation.23 | convolution fusion | flops 1954052096 | bytes 13385728 | tf_op jit(solution)/shard_map/esf,fk->kes/dot_general | solution.py:139
  255.1 5.5 %fusion.9 = bf16[2,43,8,128]{3,2,1,0:T(8,128)(2,1)S(1)} fusion(bf16[2,128,11008]{2,1,0:T(8,128)(2,1)S(1)} %bitcast.98, bf16[5504,344]{0,1:T(8,128)(2,1)} %collective-permute-done.5, bf16[5504,344]{0,1:T(8,128)(2,1)} %collective-permute-done.4), kind=kOutput, calls=%fused_computation.22 | convolution fusion | flops 1954052096 | bytes 13385728 | tf_op jit(solution)/shard_map/esf,fk->kes/dot_general | solution.py:139
  266.0 2.9 collective-permute-done.8.refs_3_
  268.9 4.0 %collective-permute-done.15.refs_7_ = bf16[344,256]{1,0:T(8,128)(2,1)S(1)} collective-permute-done((bf16[344,256]{1,0:T(8,128)(2,1)}, bf16[344,256]{1,0:T(8,128)(2,1)S(1)}, u32[]{:S(2)}, u32[]{:S(2)}) %collective-permute-start.15) | collective-permute-done | bytes 176160 | tf_op jit(solution)/shard_map/ppermute | solution.py:34
  274.5 5.7 %squares.1 = f32[2,344,1024]{2,1,0:T(8,128)S(1)} custom-call(s32[16]{0:T(128)S(1)} %stack.85.place_ref, bf16[344,256]{1,0:T(8,128)(2,1)S(1)} %bitcast.87, bf16[344,256]{1,0:T(8,128)(2,1)S(1)} %collective-permute-done.6.refs_1_, bf16[344,256]{1,0:T(8,128)(2,1)S(1)} %collective-permute-done.7.refs_2_, bf16[344,256]{1,0:T(8,128)(2,1)S(1)} %collective-permute-done.8.refs_3_, ...), custom_call_target="tpu_custom_call" | custom-call | flops 2885681152 | bytes 14000000 | tf_op jit(solution)/shard_map/squares/pallas_call | solution.py:104
  280.3 13.7 %collective-permute-start.40 = (f32[344,1024]{1,0:T(8,128)S(1)}, f32[344,1024]{1,0:T(8,128)S(1)}, u32[]{:S(2)}, u32[]{:S(2)}) collective-permute-start(f32[344,1024]{1,0:T(8,128)S(1)} %slice_bitcast_fusion), channel_id=1, source_target_pairs={{0,32},{32,0},{1,33},{33,1},{2,34},{34,2},{3,35},{35,3},{4,36},{36... | collective-permute-start | bytes 4227080 | tf_op jit(solution)/shard_map/ppermute | solution.py:38
  (167 shorter events, 78.1 us)
Async XLA Ops:
  2.1 28.9 %collective-permute-start = (bf16[2,8,11008]{2,1,0:T(8,128)(2,1)S(1)}, bf16[2,8,11008]{2,1,0:T(8,128)(2,1)S(1)}, u32[]{:S(2)}, u32[]{:S(2)}) collective-permute-start(bf16[2,8,11008]{2,1,0:T(8,128)(2,1)S(1)} %get-tuple-element.18), channel_id=1, source_target_pairs={{0,1},{1,0},{2,3},{3,2},{32,35},{33,34},{34,33},{35,32},{4,5},{5,4... | collective-permute-start | bytes 1056776 | tf_op jit(solution)/shard_map/ppermute | solution.py:17
  12.2 183.6 %collective-permute-start.4 = (bf16[5504,344]{0,1:T(8,128)(2,1)}, bf16[5504,344]{0,1:T(8,128)(2,1)}, u32[]{:S(2)}, u32[]{:S(2)}) collective-permute-start(bf16[5504,344]{0,1:T(8,128)(2,1)} %get-tuple-element.13), channel_id=1, source_target_pairs={{0,80},{16,64},{64,16},{80,0},{1,81},{17,65},{65,17},{81,1},{2,82}... | collective-permute-start | bytes 11360264 | tf_op jit(solution)/shard_map/ppermute | solution.py:34
  15.9 15.9 %collective-permute-start.9 = (bf16[2,8,11008]{2,1,0:T(8,128)(2,1)S(1)}, bf16[2,8,11008]{2,1,0:T(8,128)(2,1)S(1)}, u32[]{:S(2)}, u32[]{:S(2)}) collective-permute-start(bf16[2,8,11008]{2,1,0:T(8,128)(2,1)S(1)} %get-tuple-element.10), channel_id=1, source_target_pairs={{0,4},{4,0},{8,12},{12,8},{32,44},{36,40},{40,36},{44,32},{1,5},{5... | collective-permute-start | bytes 1056776 | tf_op jit(solution)/shard_map/ppermute | solution.py:17
  21.7 87.9 %collective-permute-start.20 = (bf16[2048,128]{1,0:T(8,128)(2,1)S(1)}, bf16[2048,128]{1,0:T(8,128)(2,1)}, u32[]{:S(2)}, u32[]{:S(2)}) collective-permute-start(bf16[2048,128]{1,0:T(8,128)(2,1)S(1)} %get-tuple-element.16), channel_id=1, source_target_pairs={{0,80},{16,64},{64,16},{80,0},{1,81},{17,65},{65,17},{81,1},{2,82}... | collective-permute-start | bytes 1572872 | tf_op jit(solution)/shard_map/ppermute | solution.py:34
  31.9 88.4 %collective-permute-start.1 = (bf16[2,16,11008]{2,1,0:T(8,128)(2,1)S(1)}, bf16[2,16,11008]{2,1,0:T(8,128)(2,1)S(1)}, u32[]{:S(2)}, u32[]{:S(2)}) collective-permute-start(bf16[2,16,11008]{2,1,0:T(8,128)(2,1)S(1)} %pad_maximum_fusion.10), channel_id=1, source_target_pairs={{0,3},{1,2},{2,1},{3,0},{32,33},{33,32},{34,35},{35,34},{4,7},{5,6... | collective-permute-start | bytes 2113544 | tf_op jit(solution)/shard_map/ppermute | solution.py:17
  35.9 85.6 %collective-permute-start.10 = (bf16[2,16,11008]{2,1,0:T(8,128)(2,1)S(1)}, bf16[2,16,11008]{2,1,0:T(8,128)(2,1)S(1)}, u32[]{:S(2)}, u32[]{:S(2)}) collective-permute-start(bf16[2,16,11008]{2,1,0:T(8,128)(2,1)S(1)} %pad_maximum_fusion.11), channel_id=1, source_target_pairs={{0,12},{4,8},{8,4},{12,0},{32,36},{36,32},{40,44},{44,40},{1,13},{... | collective-permute-start | bytes 2113544 | tf_op jit(solution)/shard_map/ppermute | solution.py:17
  36.6 73.0 %collective-permute-start.18 = (bf16[2,32,4096]{2,1,0:T(8,128)(2,1)S(1)}, bf16[2,32,4096]{2,1,0:T(8,128)(2,1)S(1)}, u32[]{:S(2)}, u32[]{:S(2)}) collective-permute-start(bf16[2,32,4096]{2,1,0:T(8,128)(2,1)S(1)} %pad_maximum_fusion.12), channel_id=1, source_target_pairs={{0,4},{4,0},{8,12},{12,8},{32,44},{36,40},{40,36},{44,32},{1,5},{5... | collective-permute-start | bytes 1572872 | tf_op jit(solution)/shard_map/ppermute | solution.py:17
  109.6 28.8 %collective-permute-start.21 = (bf16[2048,128]{1,0:T(8,128)(2,1)}, bf16[2048,128]{1,0:T(8,128)(2,1)S(1)}, u32[]{:S(2)}, u32[]{:S(2)}) collective-permute-start(bf16[2048,128]{1,0:T(8,128)(2,1)} %collective-permute-done.20), channel_id=1, source_target_pairs={{0,32},{32,0},{1,33},{33,1},{2,34},{34,2},{3,35},{35,3},{4,36},{36... | collective-permute-start | bytes 1572872 | tf_op jit(solution)/shard_map/ppermute | solution.py:38
  118.9 19.5 %collective-permute-start.19 = (bf16[2,64,4096]{2,1,0:T(8,128)(2,1)S(1)}, bf16[2,64,4096]{2,1,0:T(8,128)(2,1)S(1)}, u32[]{:S(2)}, u32[]{:S(2)}) collective-permute-start(bf16[2,64,4096]{2,1,0:T(8,128)(2,1)S(1)} %pad_maximum_fusion.6), channel_id=1, source_target_pairs={{0,12},{4,8},{8,4},{12,0},{32,36},{36,32},{40,44},{44,40},{1,13},{... | collective-permute-start | bytes 3145736 | tf_op jit(solution)/shard_map/ppermute | solution.py:17
  120.3 22.9 %collective-permute-start.32 = (bf16[2,64,4096]{2,1,0:T(8,128)(2,1)S(1)}, bf16[2,64,4096]{2,1,0:T(8,128)(2,1)S(1)}, u32[]{:S(2)}, u32[]{:S(2)}) collective-permute-start(bf16[2,64,4096]{2,1,0:T(8,128)(2,1)S(1)} %pad_maximum_fusion.8), channel_id=1, source_target_pairs={{0,3},{1,2},{2,1},{3,0},{32,33},{33,32},{34,35},{35,34},{4,7},{5,6... | collective-permute-start | bytes 3145736 | tf_op jit(solution)/shard_map/ppermute | solution.py:17
  121.6 58.2 %collective-permute-start.2 = (bf16[2,32,11008]{2,1,0:T(8,128)(2,1)}, bf16[2,32,11008]{2,1,0:T(8,128)(2,1)S(1)}, u32[]{:S(2)}, u32[]{:S(2)}) collective-permute-start(bf16[2,32,11008]{2,1,0:T(8,128)(2,1)} %pad_maximum_fusion.4), channel_id=1, source_target_pairs={{0,4},{4,0},{8,12},{12,8},{32,44},{36,40},{40,36},{44,32},{1,5},{5... | collective-permute-start | bytes 4227080 | tf_op jit(solution)/shard_map/ppermute | solution.py:17
  153.4 26.7 %collective-permute-start.11 = (bf16[2,32,11008]{2,1,0:T(8,128)(2,1)}, bf16[2,32,11008]{2,1,0:T(8,128)(2,1)}, u32[]{:S(2)}, u32[]{:S(2)}) collective-permute-start(bf16[2,32,11008]{2,1,0:T(8,128)(2,1)} %pad_maximum_fusion.5), channel_id=1, source_target_pairs={{0,1},{1,0},{2,3},{3,2},{32,35},{33,34},{34,33},{35,32},{4,5},{5,4... | collective-permute-start | bytes 4227080 | tf_op jit(solution)/shard_map/ppermute | solution.py:17
  153.6 21.7 %collective-permute-start.25 = (bf16[4,256,128]{2,1,0:T(8,128)(2,1)}, bf16[4,256,128]{2,1,0:T(8,128)(2,1)}, u32[]{:S(2)}, u32[]{:S(2)}) collective-permute-start(bf16[4,256,128]{2,1,0:T(8,128)(2,1)} %bitcast.95), channel_id=1, source_target_pairs={{0,1},{1,0},{2,3},{3,2},{32,35},{33,34},{34,33},{35,32},{4,5},{5,4... | collective-permute-start | bytes 786440 | tf_op jit(solution)/shard_map/ppermute | solution.py:17
  159.6 16.9 %collective-permute-start.36 = (bf16[4,256,128]{2,1,0:T(8,128)(2,1)}, bf16[4,256,128]{2,1,0:T(8,128)(2,1)S(1)}, u32[]{:S(2)}, u32[]{:S(2)}) collective-permute-start(bf16[4,256,128]{2,1,0:T(8,128)(2,1)} %bitcast.96), channel_id=1, source_target_pairs={{0,4},{4,0},{8,12},{12,8},{32,44},{36,40},{40,36},{44,32},{1,5},{5... | collective-permute-start | bytes 786440 | tf_op jit(solution)/shard_map/ppermute | solution.py:17
  180.0 48.0 %collective-permute-start.3 = (bf16[2,64,11008]{2,1,0:T(8,128)(2,1)S(1)}, bf16[2,64,11008]{2,1,0:T(8,128)(2,1)S(1)}, u32[]{:S(2)}, u32[]{:S(2)}) collective-permute-start(bf16[2,64,11008]{2,1,0:T(8,128)(2,1)S(1)} %pad_maximum_fusion), channel_id=1, source_target_pairs={{0,12},{4,8},{8,4},{12,0},{32,36},{36,32},{40,44},{44,40},{1,13},{... | collective-permute-start | bytes 8454152 | tf_op jit(solution)/shard_map/ppermute | solution.py:17
  181.6 55.4 %collective-permute-start.12 = (bf16[2,64,11008]{2,1,0:T(8,128)(2,1)S(1)}, bf16[2,64,11008]{2,1,0:T(8,128)(2,1)S(1)}, u32[]{:S(2)}, u32[]{:S(2)}) collective-permute-start(bf16[2,64,11008]{2,1,0:T(8,128)(2,1)S(1)} %pad_maximum_fusion.1), channel_id=1, source_target_pairs={{0,3},{1,2},{2,1},{3,0},{32,33},{33,32},{34,35},{35,34},{4,7},{5,6... | collective-permute-start | bytes 8454152 | tf_op jit(solution)/shard_map/ppermute | solution.py:17
  188.8 26.3 %collective-permute-start.27 = (bf16[4,4,256,128]{3,2,1,0:T(8,128)(2,1)S(1)}, bf16[4,4,256,128]{3,2,1,0:T(8,128)(2,1)S(1)}, u32[]{:S(2)}, u32[]{:S(2)}) collective-permute-start(bf16[4,4,256,128]{3,2,1,0:T(8,128)(2,1)S(1)} %pad_maximum_fusion.7), channel_id=1, source_target_pairs={{0,4},{4,0},{8,12},{12,8},{32,44},{36,40},{40,36},{44,32},{1,5},{5... | collective-permute-start | bytes 3145736 | tf_op jit(solution)/shard_map/ppermute | solution.py:17
  192.4 24.7 %collective-permute-start.38 = (bf16[4,4,256,128]{3,2,1,0:T(8,128)(2,1)S(1)}, bf16[4,4,256,128]{3,2,1,0:T(8,128)(2,1)S(1)}, u32[]{:S(2)}, u32[]{:S(2)}) collective-permute-start(bf16[4,4,256,128]{3,2,1,0:T(8,128)(2,1)S(1)} %pad_maximum_fusion.9), channel_id=1, source_target_pairs={{0,1},{1,0},{2,3},{3,2},{32,35},{33,34},{34,33},{35,32},{4,5},{5,4... | collective-permute-start | bytes 3145736 | tf_op jit(solution)/shard_map/ppermute | solution.py:17
  195.8 50.6 %collective-permute-start.5 = (bf16[5504,344]{0,1:T(8,128)(2,1)}, bf16[5504,344]{0,1:T(8,128)(2,1)}, u32[]{:S(2)}, u32[]{:S(2)}) collective-permute-start(bf16[5504,344]{0,1:T(8,128)(2,1)} %collective-permute-done.4), channel_id=1, source_target_pairs={{0,32},{32,0},{1,33},{33,1},{2,34},{34,2},{3,35},{35,3},{4,36},{36... | collective-permute-start | bytes 11360264 | tf_op jit(solution)/shard_map/ppermute | solution.py:38
  216.3 47.6 %collective-permute-start.28 = (bf16[8,4,256,128]{3,2,1,0:T(8,128)(2,1)S(1)}, bf16[8,4,256,128]{3,2,1,0:T(8,128)(2,1)S(1)}, u32[]{:S(2)}, u32[]{:S(2)}) collective-permute-start(bf16[8,4,256,128]{3,2,1,0:T(8,128)(2,1)S(1)} %pad_maximum_fusion.2.refs_8_), channel_id=1, source_target_pairs={{0,12},{4,8},{8,4},{12,0},{32,36},{36,32},{40,44},{44,40},{1,13},{... | collective-permute-start | bytes 6291464 | tf_op jit(solution)/shard_map/ppermute | solution.py:17
  218.6 47.3 %collective-permute-start.39 = (bf16[8,4,256,128]{3,2,1,0:T(8,128)(2,1)}, bf16[8,4,256,128]{3,2,1,0:T(8,128)(2,1)}, u32[]{:S(2)}, u32[]{:S(2)}) collective-permute-start(bf16[8,4,256,128]{3,2,1,0:T(8,128)(2,1)} %pad_maximum_fusion.3.refs_10_), channel_id=1, source_target_pairs={{0,3},{1,2},{2,1},{3,0},{32,33},{33,32},{34,35},{35,34},{4,7},{5,6... | collective-permute-start | bytes 6291464 | tf_op jit(solution)/shard_map/ppermute | solution.py:17
  236.8 24.5 %collective-permute-start.7 = (bf16[344,256]{1,0:T(8,128)(2,1)S(1)}, bf16[344,256]{1,0:T(8,128)(2,1)S(1)}, u32[]{:S(2)}, u32[]{:S(2)}) collective-permute-start(bf16[344,256]{1,0:T(8,128)(2,1)S(1)} %bitcast.86), channel_id=1, source_target_pairs={{0,64},{64,0},{1,65},{65,1},{2,66},{66,2},{3,67},{67,3},{4,68},{68... | collective-permute-start | bytes 528392 | tf_op jit(solution)/shard_map/ppermute | solution.py:30
  245.1 16.5 %collective-permute-start.14 = (bf16[344,256]{1,0:T(8,128)(2,1)S(1)}, bf16[344,256]{1,0:T(8,128)(2,1)S(1)}, u32[]{:S(2)}, u32[]{:S(2)}) collective-permute-start(bf16[344,256]{1,0:T(8,128)(2,1)S(1)} %bitcast.88), channel_id=1, source_target_pairs={{0,64},{64,0},{1,65},{65,1},{2,66},{66,2},{3,67},{67,3},{4,68},{68... | collective-permute-start | bytes 528392 | tf_op jit(solution)/shard_map/ppermute | solution.py:30
  280.3 16.5 %collective-permute-start.40 = (f32[344,1024]{1,0:T(8,128)S(1)}, f32[344,1024]{1,0:T(8,128)S(1)}, u32[]{:S(2)}, u32[]{:S(2)}) collective-permute-start(f32[344,1024]{1,0:T(8,128)S(1)} %slice_bitcast_fusion), channel_id=1, source_target_pairs={{0,32},{32,0},{1,33},{33,1},{2,34},{34,2},{3,35},{35,3},{4,36},{36... | collective-permute-start | bytes 4227080 | tf_op jit(solution)/shard_map/ppermute | solution.py:38
  (40 other events, 428.4 us)

commit v2 on v1

v2 whole, which is shorter than its diff:
```python
import jax
import jax.numpy as jnp
from jax import lax
from jax.experimental import pallas as pl
from jax.experimental.pallas import tpu as pltpu
from jax.sharding import Mesh
from jax.sharding import PartitionSpec as P

AXES = ("zl", "c", "zh", "y", "x")
ROOM = 56 * 1024 * 1024
CUTS = ((0, 2816), (2816, 2688))


def relay(v, hops):
    table = []
    for core, hop in enumerate(hops):
        for zl in range(2):
            for zh in range(2):
                to = {"both": (1 - zl, 1 - zh), "zl": (1 - zl, zh)}.get(hop)
                if to:
                    table.append((zl * 4 + core * 2 + zh, to[0] * 4 + core * 2 + to[1]))
    return lax.ppermute(v, ("zl", "c", "zh"), table)


def near_pairs(axis, step):
    masks = ((1, 3), (3, 1))
    table = [
        (core * 4 + i, core * 4 + (i ^ masks[core][step])) for core in range(2) for i in range(4)
    ]
    return lambda v: lax.ppermute(v, ("c", axis), table)


def steps_of(half):
    first, second = ("x", "y") if half == 0 else ("y", "x")
    return [near_pairs(axis, step) for axis in (first, second) for step in range(2)]


def flip_zh(v):
    return lax.ppermute(v, "zh", [(0, 1), (1, 0)])


def flip_zl(v):
    return lax.ppermute(v, "zl", [(0, 1), (1, 0)])


def flip_both(v):
    return lax.ppermute(v, ("zl", "zh"), [(i, 3 - i) for i in range(4)])


def flip_core(v):
    return lax.ppermute(v, "c", [(0, 1), (1, 0)])


def after(v, *others):
    return lax.optimization_barrier((v, *others))[0]


def rotate_in_kernel(flag_ref, *refs):
    tokens, own, other, (keep_ref, give_ref) = refs[:4], refs[4], refs[5], refs[6:]
    total = None
    for start in range(0, 4096, 512):
        lhs = jnp.concatenate(
            [
                tokens[half * 2 + piece][example, :, start : start + 512]
                for half in range(2)
                for example in range(2)
                for piece in range(2)
            ],
            0,
        )
        rhs = jnp.concatenate([own[start : start + 512, :], other[start : start + 512, :]], 1)
        part = jnp.dot(lhs, rhs, preferred_element_type=jnp.float32)
        total = part if total is None else total + part
    total = total.astype(jnp.bfloat16)
    mine, theirs = total[:, :128], total[:, 128:]

    @pl.when(flag_ref[0] == 1)
    def _():
        keep_ref[...] = mine
        give_ref[...] = theirs

    @pl.when(flag_ref[0] == 0)
    def _():
        keep_ref[...] = theirs
        give_ref[...] = mine


def rotate_in(flag, tokens, own, other):
    vmem = pl.BlockSpec(memory_space=pltpu.VMEM)
    shape = jax.ShapeDtypeStruct((512, 128), jnp.bfloat16)
    return pl.pallas_call(
        rotate_in_kernel,
        out_shape=(shape, shape),
        in_specs=[pl.BlockSpec(memory_space=pltpu.SMEM)] + [vmem] * 6,
        out_specs=(vmem, vmem),
        compiler_params=pltpu.CompilerParams(vmem_limit_bytes=ROOM),
        cost_estimate=pl.CostEstimate(
            flops=2 * 512 * 256 * 4096, bytes_accessed=6_500_000, transcendentals=0
        ),
        name="rotate_in",
    )(flag, *tokens, own, other)


def rotate_out_kernel(place_ref, *refs):
    tokens, refs = refs[:4], refs[4:]
    (basis, out_ref, refs) = (refs[:1], refs[1], refs[2:]) if len(refs) == 7 else (refs[:4], refs[4], refs[5:])
    kept_basis, kept_tokens, sems = refs[:2], refs[2:4], refs[4]
    copies = []
    for i in range(2):
        for start, size in CUTS:
            lanes = slice(start, start + size)
            offset = pl.multiple_of(place_ref[i] + start, 128)
            if len(basis) == 1:
                source = basis[0].at[:, i * 5504 + start : i * 5504 + start + size]
                group = [(source, kept_basis[i].at[:, lanes])]
            else:
                rows = [pl.multiple_of(place_ref[2 + 2 * i + j], 16) for j in range(2)]
                group = [
                    (basis[2 * i + j].at[:, lanes], kept_basis[i].at[pl.ds(rows[j], 176), lanes])
                    for j in range(2)
                ]
            for half in range(2):
                for piece in range(2):
                    group.append(
                        (
                            tokens[half * 2 + piece].at[:, :, pl.ds(offset, size)],
                            kept_tokens[i].at[
                                half * 2 : half * 2 + 2, piece * 64 : piece * 64 + 64, lanes
                            ],
                        )
                    )
            copies.append(
                [
                    pltpu.make_async_copy(source, target, sems.at[6 * len(copies) + j])
                    for j, (source, target) in enumerate(group)
                ]
            )
    for group in copies:
        for copy in group:
            copy.start()
    total = [None, None]
    for i, group in enumerate(copies):
        for copy in group:
            copy.wait()
        start, size = CUTS[i % 2]
        lanes = slice(start, start + size)
        for half in range(2):
            part = lax.dot_general(
                kept_basis[i // 2][:, lanes],
                kept_tokens[i // 2][half * 2 : half * 2 + 2, :, lanes].reshape(256, size),
                (((1,), (1,)), ((), ())),
                preferred_element_type=jnp.float32,
            )
            total[half] = part if total[half] is None else total[half] + part
    for half in range(2):
        rows = total[half]
        if len(basis) > 1:
            swap = place_ref[6] == 0
            low, high = rows[:176], rows[176:]
            rows = jnp.concatenate(
                [jnp.where(swap, low, high), jnp.where(swap, high, low)[8:]], 0
            )
        out_ref[:, half * 256 : half * 256 + 256] = rows.astype(out_ref.dtype)


def rotate_out(places, tokens, basis, name):
    rows = 344 if len(basis) == 1 else 352
    anywhere = pl.BlockSpec(memory_space=pltpu.HBM)
    return pl.pallas_call(
        rotate_out_kernel,
        out_shape=jax.ShapeDtypeStruct((344, 512), jnp.bfloat16),
        in_specs=[pl.BlockSpec(memory_space=pltpu.SMEM)] + [anywhere] * (4 + len(basis)),
        out_specs=pl.BlockSpec(memory_space=pltpu.VMEM),
        scratch_shapes=[pltpu.VMEM((rows, 5504), jnp.bfloat16)] * 2
        + [pltpu.VMEM((4, 128, 5504), jnp.bfloat16)] * 2
        + [pltpu.SemaphoreType.DMA((24,))],
        compiler_params=pltpu.CompilerParams(vmem_limit_bytes=ROOM),
        cost_estimate=pl.CostEstimate(
            flops=2 * 512 * rows * 11008, bytes_accessed=(512 + rows) * 22016, transcendentals=0
        ),
        name=name,
    )(places, *tokens, *basis)


def product_kernel(place_ref, *refs):
    lefts, rights, (keep_ref, give_ref) = refs[:4], refs[4:12], refs[12:]

    def left(half, group, example):
        lane = (half * 2 + example) * 128
        pair = [lefts[group * 2 + i] for i in range(2)]
        return jnp.concatenate([r[:, lane : lane + 128] for r in pair], 1)

    def right(half, piece, example):
        ref = rights[half * 4 + piece // 4]
        tiles = []
        for side in range(2):
            for u in range(8):
                row = side * 128 + (u ^ (piece >> 1)) * 16
                tiles.append(ref[piece % 4, example, row : row + 16, :])
        return jnp.concatenate(tiles, 0)

    for pair in range(8):
        sources = (2 * pair, 2 * pair + 1)
        total = None
        for half in range(2):
            pieces = [s if half == 0 else (s % 4) * 4 + s // 4 for s in sources]
            for group in range(2):
                for example in range(2):
                    rhs = jnp.concatenate(
                        [right(half, piece, group * 2 + example) for piece in pieces], 1
                    )
                    product = jnp.dot(
                        left(half, group, example), rhs, preferred_element_type=jnp.float32
                    )
                    square = product * product
                    total = square if total is None else total + square
        total = total * (1.0 / 16.0)
        for i, s in enumerate(sources):
            place = place_ref[s]
            column = pl.multiple_of(lax.rem(place, 8) * 128, 128)
            part = total[:, i * 128 : (i + 1) * 128]

            @pl.when(place < 8)
            def _(part=part, column=column):
                keep_ref[:, pl.ds(column, 128)] = part

            @pl.when(place >= 8)
            def _(part=part, column=column):
                give_ref[:, pl.ds(column, 128)] = part


def product(places, lefts, rights):
    rows = lefts[0].shape[0]
    shape = jax.ShapeDtypeStruct((rows, 1024), jnp.float32)
    vmem = pl.BlockSpec(memory_space=pltpu.VMEM)
    return pl.pallas_call(
        product_kernel,
        out_shape=(shape, shape),
        in_specs=[pl.BlockSpec(memory_space=pltpu.SMEM)] + [vmem] * 12,
        out_specs=(vmem, vmem),
        compiler_params=pltpu.CompilerParams(vmem_limit_bytes=24 * 1024 * 1024),
        cost_estimate=pl.CostEstimate(
            flops=2 * 8 * 256 * rows * 2048, bytes_accessed=14_000_000, transcendentals=0
        ),
        name="squares",
    )(places, *lefts, *rights)


def per_device(acts, grads, basis_in, basis_out):
    core, zl, zh = lax.axis_index("c"), lax.axis_index("zl"), lax.axis_index("zh")
    y, x = lax.axis_index("y"), lax.axis_index("x")
    steps = [steps_of(half) for half in range(2)]
    halves = range(2)

    def moved(v, step, *others):
        return [steps[half][step](after(v[half], *others) if others else v[half]) for half in halves]

    def joined(v, w, axis):
        return [jnp.concatenate([v[half], w[half]], axis) for half in halves]

    basis_out = basis_out.T

    a0 = [acts[2 * half : 2 * half + 2] for half in halves]
    g0 = [grads[2 * half : 2 * half + 2] for half in halves]
    a1 = joined(a0, moved(a0, 0), 1)
    other_in = flip_both(basis_in)
    window = lax.dynamic_slice(basis_out, (168 * (1 - zl), 5504 * core), (176, 5504))
    g1 = joined(g0, moved(g0, 0), 1)
    a2 = joined(a1, moved(a1, 1), 1)
    first = relay(after(window, other_in), ("both", None))
    g2 = joined(g1, moved(g1, 1), 1)
    a3 = joined(a2, moved(a2, 2), 1)
    a4 = moved(a3, 3)

    flag = (zh == zl).astype(jnp.int32).reshape(1)
    acts_pieces = [a3[0], a4[0], a3[1], a4[1]]
    keep, give = rotate_in(after(flag, first, *g2), acts_pieces, basis_in, other_in)
    keep, give = keep.reshape(4, 128, 128), give.reshape(4, 128, 128)
    exchanged = flip_zh(keep), flip_zl(give), flip_both(give)
    g3 = joined(g2, moved(g2, 2), 1)
    g4 = moved(g3, 3)
    near = jnp.concatenate([keep, exchanged[0]], 1)
    far = jnp.concatenate(exchanged[1:], 1)

    c0 = [
        jnp.concatenate([near[2 * half : 2 * half + 2], far[2 * half : 2 * half + 2]], 0)
        for half in halves
    ]
    swapped = [v.reshape(4, 16, 2, 8, 128)[:, :, ::-1].reshape(4, 256, 128) for v in c0]
    c1 = [jnp.stack([c0[half], v]) for half, v in enumerate(moved(swapped, 0, *g3))]
    second = relay(after(jnp.where(core == 0, first, window), *exchanged), ("zl", "both"))
    third = relay(after(second, *c1, *g4), (None, "zl"))

    grads_pieces = [v[half] for half in halves for v in (g3, g4)]
    places = jnp.array([0, 5504], jnp.int32)
    mine = rotate_out(places, grads_pieces, [basis_out], "rotate_own")
    c2 = joined(c1, [after(v, mine) for v in moved(c1, 1, *g4)], 0)
    c3 = moved(c2, 2)
    c4 = moved(c2, 3)
    c5 = moved(c3, 3)
    rights = [v[half] for half in halves for v in (c2, c3, c4, c5)]
    outer = jnp.where(core == 0, first, third)
    places = [5504 * core, 5504 * (1 - core)]
    places += [176 * core, 176 * (1 - core), 176 * core, 176 * (1 - core), zl]
    theirs = rotate_out(
        jnp.stack(places).astype(jnp.int32),
        grads_pieces,
        [outer, second, flip_core(after(second, *c2)), flip_core(after(outer, *c3, *c4))],
        "rotate_other",
    )
    lefts = [mine, flip_zh(theirs), flip_zl(mine), flip_both(theirs)]

    low, high = jnp.where(core == 0, 1, 3), jnp.where(core == 0, 3, 1)

    def mask(bits):
        return (low if bits & 1 else 0) ^ (high if bits & 2 else 0)

    places = jnp.stack(
        [((y ^ mask(s // 4)) * 4 + (x ^ mask(s % 4))) ^ (core * 8) for s in range(16)]
    ).astype(jnp.int32)
    keep, give = product(places, lefts, rights)
    return keep + flip_core(give)


def solution(mesh):
    fine = Mesh(mesh.devices.reshape(2, 2, 2, 4, 4), AXES)
    dp, eig = ("zl", "c"), ("zh", "y", "x")
    placed = (P(dp, eig, None), P(dp, eig, None), P(None, eig), P(None, eig))
    return jax.shard_map(
        per_device, mesh=fine, in_specs=placed, out_specs=P(eig, dp), check_vma=False
    )
```

time: 299 us -> 206 us (0.69)
  waiting for transfers between devices: 144 us -> 105 us
  starting transfers between devices: 73.8 us -> 42.6 us
  matrix products: 26.9 us -> 0 us
  Pallas kernels: 5.71 us -> 31.4 us
  local copies, waits for them, and re-layouts: 30 us -> 13.7 us
  other arithmetic: 16.8 us -> 12.2 us
    ppermute x6 -> x3, waiting for transfers between devices: 79.8 us -> 9.83 us  [flip_both(): return lax.ppermute(v, ('zl', 'zh'), [(i, 3 - i) for i in range(4)])]
    dot_general x6 -> x0, matrix products: 26.9 us -> none  [the longest x4 23.4 us: rotate_turned(): jnp.einsum('esf,fk->kes', tokens, basis, preferred_element_type=jnp.float32)]
    pallas_call x1 -> x4, Pallas kernels: 5.71 us -> 31.4 us  [the longest x2 19.5 us: rotate_out(): pl.pallas_call(rotate_out_kernel, out_shape=jax.ShapeDtypeStruct((344, 51...]
    ppermute x3, starting transfers between devices: 27.7 us -> 2.72 us  [flip_core(): return lax.ppermute(v, 'c', [(0, 1), (1, 0)])]
    ppermute x0 -> x3, waiting for transfers between devices: none -> 13.3 us  [relay(): return lax.ppermute(v, ('zl', 'c', 'zh'), table)]
    ppermute x24 -> x26, waiting for transfers between devices: 61.7 us -> 71.5 us  [near_pairs(): return lambda v: lax.ppermute(v, ('c', axis), table)]
    unnamed x58 -> x35, local copies, waits for them, and re-layouts: 12.8 us -> 5.51 us
    dynamic_slice x4 -> x1, local copies, waits for them, and re-layouts: 10 us -> 2.95 us  [per_device(): lax.dynamic_slice(basis_out, (168 * (1 - zl), 5504 * core), (176, 5504))]
  transfers between devices with their start and end apart: 41 -> 39, of which waited for: 16 -> 20; matrix products, arithmetic and copies ran while one was open for 22% -> 9% of each run, Pallas kernels for 0% -> 12%
where the time goes in v2:
time: 206 us; the launch traced here: 205 us
  waiting for transfers between devices  105 us (51%)
  starting transfers between devices  42.6 us (21%)
  Pallas kernels  31.4 us (15%)
  local copies, waits for them, and re-layouts  13.7 us (7%)
  other arithmetic  12.2 us (6%)
    ppermute x26, waiting for transfers between devices, near_pairs(): return lambda v: lax.ppermute(v, ('c', axis), table)  71.5 us
    ppermute x26, starting transfers between devices, near_pairs(): return lambda v: lax.ppermute(v, ('c', axis), table)  22.9 us
    pallas_call x2, Pallas kernels, rotate_out(): pl.pallas_call(rotate_out_kernel, out_shape=jax.ShapeDtypeStruct((344, 51...  19.5 us
    ppermute x3, waiting for transfers between devices, relay(): return lax.ppermute(v, ('zl', 'c', 'zh'), table)  13.3 us
    ppermute x3, waiting for transfers between devices, flip_both(): return lax.ppermute(v, ('zl', 'zh'), [(i, 3 - i) for i in range(4)])  9.83 us
    pallas_call x1, Pallas kernels, product(): pl.pallas_call(product_kernel, out_shape=(shape, shape), in_specs=[pl.Blo...  7.09 us
    ppermute x2, waiting for transfers between devices, flip_zh(): return lax.ppermute(v, 'zh', [(0, 1), (1, 0)])  6.09 us
    ppermute x2, starting transfers between devices, flip_zh(): return lax.ppermute(v, 'zh', [(0, 1), (1, 0)])  5.58 us
  transfers between devices with their start and end apart: 39, of which 20 were waited for; matrix products, arithmetic and copies ran while one was open for 9% of the time, Pallas kernels for 12%

profile of v2, /device:TPU:1, one launch (start us, length us, event | category | flops | bytes accessed | tf_op | source)
XLA Modules:
  0.0 205.4 jit_solution(4991328914492416432)
XLA Ops:
  1.1 3.4 %collective-permute-start = (bf16[2,8,11008]{2,1,0:T(8,128)(2,1)S(1)}, bf16[2,8,11008]{2,1,0:T(8,128)(2,1)S(1)}, u32[]{:S(2)}, u32[]{:S(2)}) collective-permute-start(bf16[2,8,11008]{2,1,0:T(8,128)(2,1)S(1)} %get-tuple-element.38), channel_id=1, source_target_pairs={{0,1},{1,0},{2,3},{3,2},{32,35},{33,34},{34,33},{35,32},{4,5},{5,4... | collective-permute-start | bytes 1056776 | tf_op jit(solution)/shard_map/ppermute | solution.py:30
  4.5 2.7 %collective-permute-start.4 = (bf16[2,8,11008]{2,1,0:T(8,128)(2,1)S(1)}, bf16[2,8,11008]{2,1,0:T(8,128)(2,1)S(1)}, u32[]{:S(2)}, u32[]{:S(2)}) collective-permute-start(bf16[2,8,11008]{2,1,0:T(8,128)(2,1)S(1)} %get-tuple-element.37), channel_id=1, source_target_pairs={{0,4},{4,0},{8,12},{12,8},{32,44},{36,40},{40,36},{44,32},{1,5},{5... | collective-permute-start | bytes 1056776 | tf_op jit(solution)/shard_map/ppermute | solution.py:30
  7.3 3.8 %collective-permute-start.8 = (bf16[4096,128]{1,0:T(8,128)(2,1)}, bf16[4096,128]{1,0:T(8,128)(2,1)}, u32[]{:S(2)}, u32[]{:S(2)}) collective-permute-start(bf16[4096,128]{1,0:T(8,128)(2,1)} %refs_4_.1), channel_id=1, source_target_pairs={{0,80},{16,64},{64,16},{80,0},{1,81},{17,65},{65,17},{81,1},{2,82}... | collective-permute-start | bytes 3145736 | tf_op jit(solution)/shard_map/ppermute | solution.py:47
  12.3 3.0 %dynamic-slice_bitcast_fusion = bf16[176,5504]{1,0:T(8,128)(2,1)} fusion(bf16[11008,344]{0,1:T(8,128)(2,1)} %param.8, s32[]{:T(128)S(6)} %select_n.28, s32[]{:T(128)S(6)} %select_n.29), kind=kLoop, calls=%fused_computation.2 | loop fusion | bytes 3874824 | tf_op jit(solution)/shard_map/dynamic_slice | solution.py:267
  19.4 3.9 %collective-permute-done.11 = bf16[2,16,4096]{2,1,0:T(8,128)(2,1)S(1)} collective-permute-done((bf16[2,16,4096]{2,1,0:T(8,128)(2,1)S(1)}, bf16[2,16,4096]{2,1,0:T(8,128)(2,1)S(1)}, u32[]{:S(2)}, u32[]{:S(2)}) %collective-permute-start.11) | collective-permute-done | bytes 262176 | tf_op jit(solution)/shard_map/ppermute | solution.py:30
  24.0 2.6 %collective-permute-start.16 = (bf16[2,32,4096]{2,1,0:T(8,128)(2,1)S(1)}, bf16[2,32,4096]{2,1,0:T(8,128)(2,1)S(1)}, u32[]{:S(2)}, u32[]{:S(2)}) collective-permute-start(bf16[2,32,4096]{2,1,0:T(8,128)(2,1)S(1)} %pad_maximum_fusion.11), channel_id=1, source_target_pairs={{0,1},{1,0},{2,3},{3,2},{32,35},{33,34},{34,33},{35,32},{4,5},{5,4... | collective-permute-start | bytes 1572872 | tf_op jit(solution)/shard_map/ppermute | solution.py:30
  26.5 10.5 %collective-permute-done.12 = bf16[2,32,4096]{2,1,0:T(8,128)(2,1)S(1)} collective-permute-done((bf16[2,32,4096]{2,1,0:T(8,128)(2,1)S(1)}, bf16[2,32,4096]{2,1,0:T(8,128)(2,1)S(1)}, u32[]{:S(2)}, u32[]{:S(2)}) %collective-permute-start.12) | collective-permute-done | bytes 524320 | tf_op jit(solution)/shard_map/ppermute | solution.py:30
  37.4 2.4 %collective-permute-done.5 = bf16[2,16,11008]{2,1,0:T(8,128)(2,1)S(1)} collective-permute-done((bf16[2,16,11008]{2,1,0:T(8,128)(2,1)S(1)}, bf16[2,16,11008]{2,1,0:T(8,128)(2,1)S(1)}, u32[]{:S(2)}, u32[]{:S(2)}) %collective-permute-start.5) | collective-permute-done | bytes 704544 | tf_op jit(solution)/shard_map/ppermute | solution.py:30
  42.9 24.9 %collective-permute-done.2 = bf16[2,32,11008]{2,1,0:T(8,128)(2,1)S(1)} collective-permute-done((bf16[2,32,11008]{2,1,0:T(8,128)(2,1)S(1)}, bf16[2,32,11008]{2,1,0:T(8,128)(2,1)S(1)}, u32[]{:S(2)}, u32[]{:S(2)}) %collective-permute-start.2) | collective-permute-done | bytes 1409056 | tf_op jit(solution)/shard_map/ppermute | solution.py:30
  73.0 4.8 %rotate_in.1 = (bf16[512,128]{1,0:T(8,128)(2,1)}, bf16[512,128]{1,0:T(8,128)(2,1)}) custom-call(s32[1]{0:T(128)} %bitcast.23.flag_ref, bf16[2,64,4096]{2,1,0:T(8,128)(2,1)} %copy-done.8, bf16[2,64,4096]{2,1,0:T(8,128)(2,1)} %copy-done.15, bf16[2,64,4096]{2,1,0:T(8,128)(2,1)} %copy-done.9, bf16[2,64,4096]{2,1,0:T(8,128)(2,1)} %collective-permute-done.17.refs_3_, ...), custom_call_target="tpu_custom_call" | custom-call | flops 1073741824 | bytes 6500000 | tf_op jit(solution)/shard_map/rotate_in/pallas_call | solution.py:91
  77.8 3.2 %collective-permute-start.18 = (bf16[4,128,128]{2,1,0:T(8,128)(2,1)}, bf16[4,128,128]{2,1,0:T(8,128)(2,1)S(1)}, u32[]{:S(2)}, u32[]{:S(2)}) collective-permute-start(bf16[4,128,128]{2,1,0:T(8,128)(2,1)} %bitcast.45), channel_id=1, source_target_pairs={{0,16},{16,0},{1,17},{17,1},{2,18},{18,2},{3,19},{19,3},{4,20},{20... | collective-permute-start | bytes 393224 | tf_op jit(solution)/shard_map/ppermute | solution.py:39
  81.0 3.3 %broadcast_select_fusion.1 = bf16[176,5504]{1,0:T(8,128)(2,1)} fusion(bf16[176,5504]{1,0:T(8,128)(2,1)S(1)} %collective-permute-done.9, pred[]{:T(512)S(6)} %eq.4, bf16[11008,344]{0,1:T(8,128)(2,1)} %param.8, s32[]{:T(128)S(6)} %select_n.28, s32[]{:T(128)S(6)} %select_n.29), kind=kLoop, calls=%fused_computation.4 | loop fusion | flops 968704 | bytes 5812233 | tf_op jit(solution)/shard_map/jit(_where)/select_n | solution.py:291
  91.7 7.3 %collective-permute-done.22 = bf16[4,256,128]{2,1,0:T(8,128)(2,1)} collective-permute-done((bf16[4,256,128]{2,1,0:T(8,128)(2,1)}, bf16[4,256,128]{2,1,0:T(8,128)(2,1)}, u32[]{:S(2)}, u32[]{:S(2)}) %collective-permute-start.22) | collective-permute-done | bytes 262176 | tf_op jit(solution)/shard_map/ppermute | solution.py:30
  101.5 8.1 %collective-permute-done.21.refs_5_ = bf16[176,5504]{1,0:T(8,128)(2,1)} collective-permute-done((bf16[176,5504]{1,0:T(8,128)(2,1)}, bf16[176,5504]{1,0:T(8,128)(2,1)}, u32[]{:S(2)}, u32[]{:S(2)}) %collective-permute-start.21) | collective-permute-done | bytes 1937440 | tf_op jit(solution)/shard_map/ppermute | solution.py:22
  111.6 3.5 %collective-permute-start.25 = (bf16[2,4,256,128]{3,2,1,0:T(8,128)(2,1)S(1)}, bf16[2,4,256,128]{3,2,1,0:T(8,128)(2,1)S(1)}, u32[]{:S(2)}, u32[]{:S(2)}) collective-permute-start(bf16[2,4,256,128]{3,2,1,0:T(8,128)(2,1)S(1)} %pad_maximum_fusion.12), channel_id=1, source_target_pairs={{0,3},{1,2},{2,1},{3,0},{32,33},{33,32},{34,35},{35,34},{4,7},{5,6... | collective-permute-start | bytes 1572872 | tf_op jit(solution)/shard_map/ppermute | solution.py:30
  115.6 9.7 %rotate_own.1.refs_0_ = bf16[344,512]{1,0:T(8,128)(2,1)} custom-call(s32[2]{0:T(128)} %iota_multiply_fusion.place_ref, bf16[2,64,11008]{2,1,0:T(8,128)(2,1)} %copy-done.5, bf16[2,64,11008]{2,1,0:T(8,128)(2,1)} %collective-permute-done.3.refs_1_, bf16[2,64,11008]{2,1,0:T(8,128)(2,1)} %pad_maximum_fusion.1.refs_2_, ...), custom_call_target="tpu_custom_call" | custom-call | flops 3877634048 | bytes 18845696 | tf_op jit(solution)/shard_map/rotate_own/pallas_call | solution.py:169
  130.2 5.2 %collective-permute-done.24 = bf16[176,5504]{1,0:T(8,128)(2,1)S(1)} collective-permute-done((bf16[176,5504]{1,0:T(8,128)(2,1)}, bf16[176,5504]{1,0:T(8,128)(2,1)S(1)}, u32[]{:S(2)}, u32[]{:S(2)}) %collective-permute-start.24) | collective-permute-done | bytes 1937440 | tf_op jit(solution)/shard_map/ppermute | solution.py:22
  136.8 14.3 %collective-permute-done.28.refs_5_ = bf16[4,4,256,128]{3,2,1,0:T(8,128)(2,1)S(1)} collective-permute-done((bf16[4,4,256,128]{3,2,1,0:T(8,128)(2,1)S(1)}, bf16[4,4,256,128]{3,2,1,0:T(8,128)(2,1)S(1)}, u32[]{:S(2)}, u32[]{:S(2)}) %collective-permute-start.28) | collective-permute-done | bytes 1048608 | tf_op jit(solution)/shard_map/ppermute | solution.py:30
  161.7 9.8 %rotate_other.1 = bf16[344,512]{1,0:T(8,128)(2,1)} custom-call(s32[7]{0:T(128)} %stack.111.place_ref, bf16[2,64,11008]{2,1,0:T(8,128)(2,1)} %copy-done.5, bf16[2,64,11008]{2,1,0:T(8,128)(2,1)} %collective-permute-done.3.refs_1_, bf16[2,64,11008]{2,1,0:T(8,128)(2,1)} %pad_maximum_fusion.1.refs_2_, bf16[2,64,11008]{2,1,0:T(8,128)(2,1)} %collective-permute-done.7.refs_3_, ...), custom_call_target="tpu_custom_call" | custom-call | flops 3967811584 | bytes 19021824 | tf_op jit(solution)/shard_map/rotate_other/pallas_call | solution.py:169
  171.5 2.3 %collective-permute-start.33 = (bf16[344,512]{1,0:T(8,128)(2,1)}, bf16[344,512]{1,0:T(8,128)(2,1)}, u32[]{:S(2)}, u32[]{:S(2)}) collective-permute-start(bf16[344,512]{1,0:T(8,128)(2,1)} %rotate_other.1), channel_id=1, source_target_pairs={{0,16},{16,0},{1,17},{17,1},{2,18},{18,2},{3,19},{19,3},{4,20},{20... | collective-permute-start | bytes 1056776 | tf_op jit(solution)/shard_map/ppermute | solution.py:39
  175.6 5.8 %collective-permute-done.33.refs_1_ = bf16[344,512]{1,0:T(8,128)(2,1)} collective-permute-done((bf16[344,512]{1,0:T(8,128)(2,1)}, bf16[344,512]{1,0:T(8,128)(2,1)}, u32[]{:S(2)}, u32[]{:S(2)}) %collective-permute-start.33) | collective-permute-done | bytes 352288 | tf_op jit(solution)/shard_map/ppermute | solution.py:39
  181.4 9.7 %collective-permute-done.35.refs_3_ = bf16[344,512]{1,0:T(8,128)(2,1)} collective-permute-done((bf16[344,512]{1,0:T(8,128)(2,1)}, bf16[344,512]{1,0:T(8,128)(2,1)}, u32[]{:S(2)}, u32[]{:S(2)}) %collective-permute-start.35) | collective-permute-done | bytes 352288 | tf_op jit(solution)/shard_map/ppermute | solution.py:47
  193.6 7.1 %squares.1 = (f32[344,1024]{1,0:T(8,128)S(1)}, f32[344,1024]{1,0:T(8,128)S(1)}) custom-call(s32[16]{0:T(128)S(1)} %stack.105.place_ref, bf16[344,512]{1,0:T(8,128)(2,1)S(1)} %copy-done, bf16[344,512]{1,0:T(8,128)(2,1)} %collective-permute-done.33.refs_1_, bf16[344,512]{1,0:T(8,128)(2,1)} %collective-permute-done.34.refs_2_, ...), custom_call_target="tpu_custom_call" | custom-call | flops 2885681152 | bytes 14000000 | tf_op jit(solution)/shard_map/squares/pallas_call | solution.py:236
  201.3 2.8 %collective-permute-done.38 = f32[344,1024]{1,0:T(8,128)S(1)} collective-permute-done((f32[344,1024]{1,0:T(8,128)S(1)}, f32[344,1024]{1,0:T(8,128)S(1)}, u32[]{:S(2)}, u32[]{:S(2)}) %collective-permute-start.38) | collective-permute-done | bytes 1409056 | tf_op jit(solution)/shard_map/ppermute | solution.py:51
  (124 shorter events, 51.0 us)
Async XLA Ops:
  1.1 16.7 %collective-permute-start = (bf16[2,8,11008]{2,1,0:T(8,128)(2,1)S(1)}, bf16[2,8,11008]{2,1,0:T(8,128)(2,1)S(1)}, u32[]{:S(2)}, u32[]{:S(2)}) collective-permute-start(bf16[2,8,11008]{2,1,0:T(8,128)(2,1)S(1)} %get-tuple-element.38), channel_id=1, source_target_pairs={{0,1},{1,0},{2,3},{3,2},{32,35},{33,34},{34,33},{35,32},{4,5},{5,4... | collective-permute-start | bytes 1056776 | tf_op jit(solution)/shard_map/ppermute | solution.py:30
  4.5 19.2 %collective-permute-start.4 = (bf16[2,8,11008]{2,1,0:T(8,128)(2,1)S(1)}, bf16[2,8,11008]{2,1,0:T(8,128)(2,1)S(1)}, u32[]{:S(2)}, u32[]{:S(2)}) collective-permute-start(bf16[2,8,11008]{2,1,0:T(8,128)(2,1)S(1)} %get-tuple-element.37), channel_id=1, source_target_pairs={{0,4},{4,0},{8,12},{12,8},{32,44},{36,40},{40,36},{44,32},{1,5},{5... | collective-permute-start | bytes 1056776 | tf_op jit(solution)/shard_map/ppermute | solution.py:30
  7.3 34.7 %collective-permute-start.8 = (bf16[4096,128]{1,0:T(8,128)(2,1)}, bf16[4096,128]{1,0:T(8,128)(2,1)}, u32[]{:S(2)}, u32[]{:S(2)}) collective-permute-start(bf16[4096,128]{1,0:T(8,128)(2,1)} %refs_4_.1), channel_id=1, source_target_pairs={{0,80},{16,64},{64,16},{80,0},{1,81},{17,65},{65,17},{81,1},{2,82}... | collective-permute-start | bytes 3145736 | tf_op jit(solution)/shard_map/ppermute | solution.py:47
  17.9 19.3 %collective-permute-start.1 = (bf16[2,16,11008]{2,1,0:T(8,128)(2,1)S(1)}, bf16[2,16,11008]{2,1,0:T(8,128)(2,1)S(1)}, u32[]{:S(2)}, u32[]{:S(2)}) collective-permute-start(bf16[2,16,11008]{2,1,0:T(8,128)(2,1)S(1)} %pad_maximum_fusion.8), channel_id=1, source_target_pairs={{0,3},{1,2},{2,1},{3,0},{32,33},{33,32},{34,35},{35,34},{4,7},{5,6... | collective-permute-start | bytes 2113544 | tf_op jit(solution)/shard_map/ppermute | solution.py:30
  23.8 16.0 %collective-permute-start.5 = (bf16[2,16,11008]{2,1,0:T(8,128)(2,1)S(1)}, bf16[2,16,11008]{2,1,0:T(8,128)(2,1)S(1)}, u32[]{:S(2)}, u32[]{:S(2)}) collective-permute-start(bf16[2,16,11008]{2,1,0:T(8,128)(2,1)S(1)} %pad_maximum_fusion.9), channel_id=1, source_target_pairs={{0,12},{4,8},{8,4},{12,0},{32,36},{36,32},{40,44},{44,40},{1,13},{... | collective-permute-start | bytes 2113544 | tf_op jit(solution)/shard_map/ppermute | solution.py:30
  24.0 17.8 %collective-permute-start.16 = (bf16[2,32,4096]{2,1,0:T(8,128)(2,1)S(1)}, bf16[2,32,4096]{2,1,0:T(8,128)(2,1)S(1)}, u32[]{:S(2)}, u32[]{:S(2)}) collective-permute-start(bf16[2,32,4096]{2,1,0:T(8,128)(2,1)S(1)} %pad_maximum_fusion.11), channel_id=1, source_target_pairs={{0,1},{1,0},{2,3},{3,2},{32,35},{33,34},{34,33},{35,32},{4,5},{5,4... | collective-permute-start | bytes 1572872 | tf_op jit(solution)/shard_map/ppermute | solution.py:30
  37.1 34.9 %collective-permute-start.13 = (bf16[2,64,4096]{2,1,0:T(8,128)(2,1)S(1)}, bf16[2,64,4096]{2,1,0:T(8,128)(2,1)S(1)}, u32[]{:S(2)}, u32[]{:S(2)}) collective-permute-start(bf16[2,64,4096]{2,1,0:T(8,128)(2,1)S(1)} %pad_maximum_fusion.4.refs_0_), channel_id=1, source_target_pairs={{0,12},{4,8},{8,4},{12,0},{32,36},{36,32},{40,44},{44,40},{1,13},{... | collective-permute-start | bytes 3145736 | tf_op jit(solution)/shard_map/ppermute | solution.py:30
  37.3 30.4 %collective-permute-start.2 = (bf16[2,32,11008]{2,1,0:T(8,128)(2,1)S(1)}, bf16[2,32,11008]{2,1,0:T(8,128)(2,1)S(1)}, u32[]{:S(2)}, u32[]{:S(2)}) collective-permute-start(bf16[2,32,11008]{2,1,0:T(8,128)(2,1)S(1)} %pad_maximum_fusion.2), channel_id=1, source_target_pairs={{0,4},{4,0},{8,12},{12,8},{32,44},{36,40},{40,36},{44,32},{1,5},{5... | collective-permute-start | bytes 4227080 | tf_op jit(solution)/shard_map/ppermute | solution.py:30
  39.9 30.3 %collective-permute-start.6 = (bf16[2,32,11008]{2,1,0:T(8,128)(2,1)S(1)}, bf16[2,32,11008]{2,1,0:T(8,128)(2,1)S(1)}, u32[]{:S(2)}, u32[]{:S(2)}) collective-permute-start(bf16[2,32,11008]{2,1,0:T(8,128)(2,1)S(1)} %pad_maximum_fusion.3), channel_id=1, source_target_pairs={{0,1},{1,0},{2,3},{3,2},{32,35},{33,34},{34,33},{35,32},{4,5},{5,4... | collective-permute-start | bytes 4227080 | tf_op jit(solution)/shard_map/ppermute | solution.py:30
  41.9 31.1 %collective-permute-start.17 = (bf16[2,64,4096]{2,1,0:T(8,128)(2,1)S(1)}, bf16[2,64,4096]{2,1,0:T(8,128)(2,1)}, u32[]{:S(2)}, u32[]{:S(2)}) collective-permute-start(bf16[2,64,4096]{2,1,0:T(8,128)(2,1)S(1)} %pad_maximum_fusion.5.refs_2_), channel_id=1, source_target_pairs={{0,3},{1,2},{2,1},{3,0},{32,33},{33,32},{34,35},{35,34},{4,7},{5,6... | collective-permute-start | bytes 3145736 | tf_op jit(solution)/shard_map/ppermute | solution.py:30
  42.0 30.0 %collective-permute-start.9 = (bf16[176,5504]{1,0:T(8,128)(2,1)S(1)}, bf16[176,5504]{1,0:T(8,128)(2,1)S(1)}, u32[]{:S(2)}, u32[]{:S(2)}) collective-permute-start(bf16[176,5504]{1,0:T(8,128)(2,1)S(1)} %copy-done.14), channel_id=1, source_target_pairs={{0,80},{16,64},{64,16},{80,0},{1,81},{17,65},{65,17},{81,1},{2,82}... | collective-permute-start | bytes 5812232 | tf_op jit(solution)/shard_map/ppermute | solution.py:22
  68.0 41.6 %collective-permute-start.3 = (bf16[2,64,11008]{2,1,0:T(8,128)(2,1)S(1)}, bf16[2,64,11008]{2,1,0:T(8,128)(2,1)}, u32[]{:S(2)}, u32[]{:S(2)}) collective-permute-start(bf16[2,64,11008]{2,1,0:T(8,128)(2,1)S(1)} %pad_maximum_fusion.refs_0_), channel_id=1, source_target_pairs={{0,12},{4,8},{8,4},{12,0},{32,36},{36,32},{40,44},{44,40},{1,13},{... | collective-permute-start | bytes 8454152 | tf_op jit(solution)/shard_map/ppermute | solution.py:30
  71.9 37.8 %collective-permute-start.7 = (bf16[2,64,11008]{2,1,0:T(8,128)(2,1)}, bf16[2,64,11008]{2,1,0:T(8,128)(2,1)}, u32[]{:S(2)}, u32[]{:S(2)}) collective-permute-start(bf16[2,64,11008]{2,1,0:T(8,128)(2,1)} %pad_maximum_fusion.1.refs_2_), channel_id=1, source_target_pairs={{0,3},{1,2},{2,1},{3,0},{32,33},{33,32},{34,35},{35,34},{4,7},{5,6... | collective-permute-start | bytes 8454152 | tf_op jit(solution)/shard_map/ppermute | solution.py:30
  84.7 25.0 %collective-permute-start.21 = (bf16[176,5504]{1,0:T(8,128)(2,1)}, bf16[176,5504]{1,0:T(8,128)(2,1)}, u32[]{:S(2)}, u32[]{:S(2)}) collective-permute-start(bf16[176,5504]{1,0:T(8,128)(2,1)} %broadcast_select_fusion.1), channel_id=1, source_target_pairs={{0,64},{16,80},{64,0},{80,16},{32,112},{48,96},{96,48},{112,32},{1... | collective-permute-start | bytes 5812232 | tf_op jit(solution)/shard_map/ppermute | solution.py:22
  109.7 25.7 %collective-permute-start.24 = (bf16[176,5504]{1,0:T(8,128)(2,1)}, bf16[176,5504]{1,0:T(8,128)(2,1)S(1)}, u32[]{:S(2)}, u32[]{:S(2)}) collective-permute-start(bf16[176,5504]{1,0:T(8,128)(2,1)} %collective-permute-done.21.refs_5_), channel_id=1, source_target_pairs={{32,96},{48,112},{96,32},{112,48},{33,97},{49,113},{97,33},{113,49... | collective-permute-start | bytes 5812232 | tf_op jit(solution)/shard_map/ppermute | solution.py:22
  126.6 24.5 %collective-permute-start.28 = (bf16[4,4,256,128]{3,2,1,0:T(8,128)(2,1)S(1)}, bf16[4,4,256,128]{3,2,1,0:T(8,128)(2,1)S(1)}, u32[]{:S(2)}, u32[]{:S(2)}) collective-permute-start(bf16[4,4,256,128]{3,2,1,0:T(8,128)(2,1)S(1)} %pad_maximum_fusion.6.refs_4_), channel_id=1, source_target_pairs={{0,4},{4,0},{8,12},{12,8},{32,44},{36,40},{40,36},{44,32},{1,5},{5... | collective-permute-start | bytes 3145736 | tf_op jit(solution)/shard_map/ppermute | solution.py:30
  128.5 25.2 %collective-permute-start.30 = (bf16[4,4,256,128]{3,2,1,0:T(8,128)(2,1)S(1)}, bf16[4,4,256,128]{3,2,1,0:T(8,128)(2,1)S(1)}, u32[]{:S(2)}, u32[]{:S(2)}) collective-permute-start(bf16[4,4,256,128]{3,2,1,0:T(8,128)(2,1)S(1)} %pad_maximum_fusion.6.refs_4_), channel_id=1, source_target_pairs={{0,12},{4,8},{8,4},{12,0},{32,36},{36,32},{40,44},{44,40},{1,13},{... | collective-permute-start | bytes 3145736 | tf_op jit(solution)/shard_map/ppermute | solution.py:30
  129.5 23.7 %collective-permute-start.29 = (bf16[4,4,256,128]{3,2,1,0:T(8,128)(2,1)S(1)}, bf16[4,4,256,128]{3,2,1,0:T(8,128)(2,1)}, u32[]{:S(2)}, u32[]{:S(2)}) collective-permute-start(bf16[4,4,256,128]{3,2,1,0:T(8,128)(2,1)S(1)} %pad_maximum_fusion.7.refs_8_), channel_id=1, source_target_pairs={{0,1},{1,0},{2,3},{3,2},{32,35},{33,34},{34,33},{35,32},{4,5},{5,4... | collective-permute-start | bytes 3145736 | tf_op jit(solution)/shard_map/ppermute | solution.py:30
  130.2 24.5 %collective-permute-start.31 = (bf16[4,4,256,128]{3,2,1,0:T(8,128)(2,1)S(1)}, bf16[4,4,256,128]{3,2,1,0:T(8,128)(2,1)S(1)}, u32[]{:S(2)}, u32[]{:S(2)}) collective-permute-start(bf16[4,4,256,128]{3,2,1,0:T(8,128)(2,1)S(1)} %pad_maximum_fusion.7.refs_8_), channel_id=1, source_target_pairs={{0,3},{1,2},{2,1},{3,0},{32,33},{33,32},{34,35},{35,34},{4,7},{5,6... | collective-permute-start | bytes 3145736 | tf_op jit(solution)/shard_map/ppermute | solution.py:30
  135.3 25.0 %collective-permute-start.27 = (bf16[176,5504]{1,0:T(8,128)(2,1)}, bf16[176,5504]{1,0:T(8,128)(2,1)}, u32[]{:S(2)}, u32[]{:S(2)}) collective-permute-start(bf16[176,5504]{1,0:T(8,128)(2,1)} %collective-permute-done.21.refs_5_), channel_id=1, source_target_pairs={{0,32},{32,0},{1,33},{33,1},{2,34},{34,2},{3,35},{35,3},{4,36},{36... | collective-permute-start | bytes 5812232 | tf_op jit(solution)/shard_map/ppermute | solution.py:51
  157.8 17.7 %collective-permute-start.36 = (bf16[4,4,256,128]{3,2,1,0:T(8,128)(2,1)S(1)}, bf16[4,4,256,128]{3,2,1,0:T(8,128)(2,1)}, u32[]{:S(2)}, u32[]{:S(2)}) collective-permute-start(bf16[4,4,256,128]{3,2,1,0:T(8,128)(2,1)S(1)} %collective-permute-done.28.refs_5_), channel_id=1, source_target_pairs={{0,12},{4,8},{8,4},{12,0},{32,36},{36,32},{40,44},{44,40},{1,13},{... | collective-permute-start | bytes 3145736 | tf_op jit(solution)/shard_map/ppermute | solution.py:30
  158.3 17.3 %collective-permute-start.37 = (bf16[4,4,256,128]{3,2,1,0:T(8,128)(2,1)}, bf16[4,4,256,128]{3,2,1,0:T(8,128)(2,1)}, u32[]{:S(2)}, u32[]{:S(2)}) collective-permute-start(bf16[4,4,256,128]{3,2,1,0:T(8,128)(2,1)} %collective-permute-done.29.refs_9_), channel_id=1, source_target_pairs={{0,3},{1,2},{2,1},{3,0},{32,33},{33,32},{34,35},{35,34},{4,7},{5,6... | collective-permute-start | bytes 3145736 | tf_op jit(solution)/shard_map/ppermute | solution.py:30
  158.9 16.7 %collective-permute-start.34 = (bf16[344,512]{1,0:T(8,128)(2,1)S(1)}, bf16[344,512]{1,0:T(8,128)(2,1)}, u32[]{:S(2)}, u32[]{:S(2)}) collective-permute-start(bf16[344,512]{1,0:T(8,128)(2,1)S(1)} %copy-done), channel_id=1, source_target_pairs={{0,64},{64,0},{1,65},{65,1},{2,66},{66,2},{3,67},{67,3},{4,68},{68... | collective-permute-start | bytes 1056776 | tf_op jit(solution)/shard_map/ppermute | solution.py:43
  173.9 17.3 %collective-permute-start.35 = (bf16[344,512]{1,0:T(8,128)(2,1)}, bf16[344,512]{1,0:T(8,128)(2,1)}, u32[]{:S(2)}, u32[]{:S(2)}) collective-permute-start(bf16[344,512]{1,0:T(8,128)(2,1)} %rotate_other.1), channel_id=1, source_target_pairs={{0,80},{16,64},{64,16},{80,0},{1,81},{17,65},{65,17},{81,1},{2,82}... | collective-permute-start | bytes 1056776 | tf_op jit(solution)/shard_map/ppermute | solution.py:47
  (32 other events, 318.6 us)

commit v3 on v2

--- a/solution.py
+++ b/solution.py
@@ -56,7 +56,7 @@
 
 
 def rotate_in_kernel(flag_ref, *refs):
-    tokens, own, other, (keep_ref, give_ref) = refs[:4], refs[4], refs[5], refs[6:]
+    tokens, own, (near, far), (keep_ref, give_ref) = refs[:4], refs[4], refs[5:7], refs[7:]
     total = None
     for start in range(0, 4096, 512):
         lhs = jnp.concatenate(
@@ -68,7 +68,9 @@
             ],
             0,
         )
-        rhs = jnp.concatenate([own[start : start + 512, :], other[start : start + 512, :]], 1)
+        rows = slice(start % 2048, start % 2048 + 512)
+        other = jnp.where(flag_ref[1] == start // 2048, near[rows, :], far[rows, :])
+        rhs = jnp.concatenate([own[start : start + 512, :], other], 1)
         part = jnp.dot(lhs, rhs, preferred_element_type=jnp.float32)
         total = part if total is None else total + part
     total = total.astype(jnp.bfloat16)
@@ -91,47 +93,39 @@
     return pl.pallas_call(
         rotate_in_kernel,
         out_shape=(shape, shape),
-        in_specs=[pl.BlockSpec(memory_space=pltpu.SMEM)] + [vmem] * 6,
+        in_specs=[pl.BlockSpec(memory_space=pltpu.SMEM)] + [vmem] * 7,
         out_specs=(vmem, vmem),
         compiler_params=pltpu.CompilerParams(vmem_limit_bytes=ROOM),
         cost_estimate=pl.CostEstimate(
             flops=2 * 512 * 256 * 4096, bytes_accessed=6_500_000, transcendentals=0
         ),
         name="rotate_in",
-    )(flag, *tokens, own, other)
+    )(flag, *tokens, own, *other)
 
 
 def rotate_out_kernel(place_ref, *refs):
-    tokens, refs = refs[:4], refs[4:]
-    (basis, out_ref, refs) = (refs[:1], refs[1], refs[2:]) if len(refs) == 7 else (refs[:4], refs[4], refs[5:])
-    kept_basis, kept_tokens, sems = refs[:2], refs[2:4], refs[4]
+    tokens, own, windows, (own_ref, other_ref) = refs[:8], refs[8], refs[9:13], refs[13:15]
+    kept_own, kept_other, kept_tokens, sems = refs[15:17], refs[17:19], refs[19:21], refs[21]
     copies = []
     for i in range(2):
+        rows = [pl.multiple_of(place_ref[2 + 2 * i + j], 16) for j in range(2)]
         for start, size in CUTS:
             lanes = slice(start, start + size)
             offset = pl.multiple_of(place_ref[i] + start, 128)
-            if len(basis) == 1:
-                source = basis[0].at[:, i * 5504 + start : i * 5504 + start + size]
-                group = [(source, kept_basis[i].at[:, lanes])]
-            else:
-                rows = [pl.multiple_of(place_ref[2 + 2 * i + j], 16) for j in range(2)]
-                group = [
-                    (basis[2 * i + j].at[:, lanes], kept_basis[i].at[pl.ds(rows[j], 176), lanes])
-                    for j in range(2)
-                ]
+            group = [(own.at[:, pl.ds(offset, size)], kept_own[i].at[:, lanes])]
+            for j in range(2):
+                target = kept_other[i].at[pl.ds(rows[j], 176), lanes]
+                group.append((windows[2 * i + j].at[:, lanes], target))
             for half in range(2):
-                for piece in range(2):
-                    group.append(
-                        (
-                            tokens[half * 2 + piece].at[:, :, pl.ds(offset, size)],
-                            kept_tokens[i].at[
-                                half * 2 : half * 2 + 2, piece * 64 : piece * 64 + 64, lanes
-                            ],
-                        )
-                    )
+                for piece in range(4):
+                    target = kept_tokens[i].at[
+                        half * 2 : half * 2 + 2, piece * 32 : piece * 32 + 32, lanes
+                    ]
+                    source = tokens[half * 4 + piece].at[:, :, pl.ds(offset, size)]
+                    group.append((source, target))
             copies.append(
                 [
-                    pltpu.make_async_copy(source, target, sems.at[6 * len(copies) + j])
+                    pltpu.make_async_copy(source, target, sems.at[11 * len(copies) + j])
                     for j, (source, target) in enumerate(group)
                 ]
             )
@@ -144,46 +138,47 @@
             copy.wait()
         start, size = CUTS[i % 2]
         lanes = slice(start, start + size)
+        basis = jnp.concatenate([kept_other[i // 2][:, lanes], kept_own[i // 2][:, lanes]], 0)
         for half in range(2):
             part = lax.dot_general(
-                kept_basis[i // 2][:, lanes],
+                basis,
                 kept_tokens[i // 2][half * 2 : half * 2 + 2, :, lanes].reshape(256, size),
                 (((1,), (1,)), ((), ())),
                 preferred_element_type=jnp.float32,
             )
             total[half] = part if total[half] is None else total[half] + part
+    swap = place_ref[6] == 0
     for half in range(2):
-        rows = total[half]
-        if len(basis) > 1:
-            swap = place_ref[6] == 0
-            low, high = rows[:176], rows[176:]
-            rows = jnp.concatenate(
-                [jnp.where(swap, low, high), jnp.where(swap, high, low)[8:]], 0
-            )
-        out_ref[:, half * 256 : half * 256 + 256] = rows.astype(out_ref.dtype)
-
-
-def rotate_out(places, tokens, basis, name):
-    rows = 344 if len(basis) == 1 else 352
+        lanes = slice(half * 256, half * 256 + 256)
+        own_ref[:, lanes] = total[half][352:].astype(own_ref.dtype)
+        low, high = total[half][:176], total[half][176:352]
+        rows = jnp.concatenate([jnp.where(swap, low, high), jnp.where(swap, high, low)[8:]], 0)
+        other_ref[:, lanes] = rows.astype(other_ref.dtype)
+
+
+def rotate_out(places, tokens, own, windows):
+    shape = jax.ShapeDtypeStruct((344, 512), jnp.bfloat16)
     anywhere = pl.BlockSpec(memory_space=pltpu.HBM)
+    vmem = pl.BlockSpec(memory_space=pltpu.VMEM)
     return pl.pallas_call(
         rotate_out_kernel,
-        out_shape=jax.ShapeDtypeStruct((344, 512), jnp.bfloat16),
-        in_specs=[pl.BlockSpec(memory_space=pltpu.SMEM)] + [anywhere] * (4 + len(basis)),
-        out_specs=pl.BlockSpec(memory_space=pltpu.VMEM),
-        scratch_shapes=[pltpu.VMEM((rows, 5504), jnp.bfloat16)] * 2
+        out_shape=(shape, shape),
+        in_specs=[pl.BlockSpec(memory_space=pltpu.SMEM)] + [anywhere] * 13,
+        out_specs=(vmem, vmem),
+        scratch_shapes=[pltpu.VMEM((344, 5504), jnp.bfloat16)] * 2
+        + [pltpu.VMEM((352, 5504), jnp.bfloat16)] * 2
         + [pltpu.VMEM((4, 128, 5504), jnp.bfloat16)] * 2
-        + [pltpu.SemaphoreType.DMA((24,))],
+        + [pltpu.SemaphoreType.DMA((44,))],
         compiler_params=pltpu.CompilerParams(vmem_limit_bytes=ROOM),
         cost_estimate=pl.CostEstimate(
-            flops=2 * 512 * rows * 11008, bytes_accessed=(512 + rows) * 22016, transcendentals=0
+            flops=2 * 512 * 696 * 11008, bytes_accessed=(512 + 696) * 22016, transcendentals=0
         ),
-        name=name,
-    )(places, *tokens, *basis)
+        name="rotate_out",
+    )(places, *tokens, own, *windows)
 
 
 def product_kernel(place_ref, *refs):
-    lefts, rights, (keep_ref, give_ref) = refs[:4], refs[4:12], refs[12:]
+    lefts, rights, (keep_ref, give_ref) = refs[:4], refs[4:8], refs[8:]
 
     def left(half, group, example):
         lane = (half * 2 + example) * 128
@@ -191,12 +186,12 @@
         return jnp.concatenate([r[:, lane : lane + 128] for r in pair], 1)
 
     def right(half, piece, example):
-        ref = rights[half * 4 + piece // 4]
+        ref = rights[half * 2 + piece // 8]
         tiles = []
         for side in range(2):
             for u in range(8):
                 row = side * 128 + (u ^ (piece >> 1)) * 16
-                tiles.append(ref[piece % 4, example, row : row + 16, :])
+                tiles.append(ref[piece % 8, example, row : row + 16, :])
         return jnp.concatenate(tiles, 0)
 
     for pair in range(8):
@@ -236,7 +231,7 @@
     return pl.pallas_call(
         product_kernel,
         out_shape=(shape, shape),
-        in_specs=[pl.BlockSpec(memory_space=pltpu.SMEM)] + [vmem] * 12,
+        in_specs=[pl.BlockSpec(memory_space=pltpu.SMEM)] + [vmem] * 8,
         out_specs=(vmem, vmem),
         compiler_params=pltpu.CompilerParams(vmem_limit_bytes=24 * 1024 * 1024),
         cost_estimate=pl.CostEstimate(
@@ -263,51 +258,47 @@
     a0 = [acts[2 * half : 2 * half + 2] for half in halves]
     g0 = [grads[2 * half : 2 * half + 2] for half in halves]
     a1 = joined(a0, moved(a0, 0), 1)
-    other_in = flip_both(basis_in)
+    part = flip_both(lax.dynamic_slice_in_dim(basis_in, 2048 * (1 - zl), 2048, 0))
+    other_in = part, flip_zl(part)
     window = lax.dynamic_slice(basis_out, (168 * (1 - zl), 5504 * core), (176, 5504))
     g1 = joined(g0, moved(g0, 0), 1)
     a2 = joined(a1, moved(a1, 1), 1)
-    first = relay(after(window, other_in), ("both", None))
+    first = relay(after(window, part), ("both", None))
     g2 = joined(g1, moved(g1, 1), 1)
     a3 = joined(a2, moved(a2, 2), 1)
     a4 = moved(a3, 3)
 
-    flag = (zh == zl).astype(jnp.int32).reshape(1)
+    flag = jnp.stack([(zh == zl).astype(jnp.int32), zl.astype(jnp.int32)])
     acts_pieces = [a3[0], a4[0], a3[1], a4[1]]
     keep, give = rotate_in(after(flag, first, *g2), acts_pieces, basis_in, other_in)
     keep, give = keep.reshape(4, 128, 128), give.reshape(4, 128, 128)
     exchanged = flip_zh(keep), flip_zl(give), flip_both(give)
-    g3 = joined(g2, moved(g2, 2), 1)
-    g4 = moved(g3, 3)
-    near = jnp.concatenate([keep, exchanged[0]], 1)
-    far = jnp.concatenate(exchanged[1:], 1)
+    g3 = moved(g2, 2, *a4)
+    g4 = moved(g2, 3, *exchanged)
+    near = jnp.concatenate([after(keep, *g3), exchanged[0]], 1)
+    far = jnp.concatenate(after(exchanged[1:], *g3), 1)
 
     c0 = [
         jnp.concatenate([near[2 * half : 2 * half + 2], far[2 * half : 2 * half + 2]], 0)
         for half in halves
     ]
     swapped = [v.reshape(4, 16, 2, 8, 128)[:, :, ::-1].reshape(4, 256, 128) for v in c0]
-    c1 = [jnp.stack([c0[half], v]) for half, v in enumerate(moved(swapped, 0, *g3))]
+    c1 = [jnp.stack([c0[half], v]) for half, v in enumerate(moved(swapped, 0))]
     second = relay(after(jnp.where(core == 0, first, window), *exchanged), ("zl", "both"))
     third = relay(after(second, *c1, *g4), (None, "zl"))
 
-    grads_pieces = [v[half] for half in halves for v in (g3, g4)]
-    places = jnp.array([0, 5504], jnp.int32)
-    mine = rotate_out(places, grads_pieces, [basis_out], "rotate_own")
-    c2 = joined(c1, [after(v, mine) for v in moved(c1, 1, *g4)], 0)
-    c3 = moved(c2, 2)
-    c4 = moved(c2, 3)
-    c5 = moved(c3, 3)
-    rights = [v[half] for half in halves for v in (c2, c3, c4, c5)]
+    c2 = joined(c1, moved(c1, 1), 0)
+    g5 = moved(g3, 3, *c1, *g4)
+    grads_pieces = [v[half] for half in halves for v in (g2, g3, g4, g5)]
+    c3 = joined(c2, moved(c2, 2), 0)
+    c4 = moved(c3, 3, *g5)
     outer = jnp.where(core == 0, first, third)
     places = [5504 * core, 5504 * (1 - core)]
     places += [176 * core, 176 * (1 - core), 176 * core, 176 * (1 - core), zl]
-    theirs = rotate_out(
-        jnp.stack(places).astype(jnp.int32),
-        grads_pieces,
-        [outer, second, flip_core(after(second, *c2)), flip_core(after(outer, *c3, *c4))],
-        "rotate_other",
-    )
+    windows = [outer, second, flip_core(after(second, *c2)), flip_core(after(outer, *c2))]
+    places = after(jnp.stack(places).astype(jnp.int32), *c3)
+    mine, theirs = rotate_out(places, grads_pieces, basis_out, windows)
+    rights = [v[half] for half in halves for v in (c3, c4)]
     lefts = [mine, flip_zh(theirs), flip_zl(mine), flip_both(theirs)]
 
     low, high = jnp.where(core == 0, 1, 3), jnp.where(core == 0, 3, 1)

time: 206 us -> 189 us (0.917)
  waiting for transfers between devices: 105 us -> 87.1 us
  starting transfers between devices: 42.6 us -> 49.1 us
  Pallas kernels: 31.4 us -> 27.5 us
    ppermute x3, waiting for transfers between devices: 9.83 us -> 3.37 us  [flip_both(): return lax.ppermute(v, ('zl', 'zh'), [(i, 3 - i) for i in range(4)])]
    ppermute x26, waiting for transfers between devices: 71.5 us -> 65.6 us  [near_pairs(): return lambda v: lax.ppermute(v, ('c', axis), table)]
    pallas_call x2 -> x1, Pallas kernels: 19.5 us -> 15.2 us  [rotate_out(): pl.pallas_call(rotate_out_kernel, out_shape=(shape, shape), in_specs=[pl....]
    ppermute x3, starting transfers between devices: 2.72 us -> 6.81 us  [flip_core(): return lax.ppermute(v, 'c', [(0, 1), (1, 0)])]
    ppermute x26, starting transfers between devices: 22.9 us -> 25.9 us  [near_pairs(): return lambda v: lax.ppermute(v, ('c', axis), table)]
    ppermute x2, waiting for transfers between devices: 6.09 us -> 3.5 us  [flip_zh(): return lax.ppermute(v, 'zh', [(0, 1), (1, 0)])]
    ppermute x2, starting transfers between devices: 5.58 us -> 3.03 us  [flip_zh(): return lax.ppermute(v, 'zh', [(0, 1), (1, 0)])]
    unnamed x35 -> x30, local copies, waits for them, and re-layouts: 5.51 us -> 4.74 us
  transfers between devices with their start and end apart: 39 -> 40, of which waited for: 20 -> 21; matrix products, arithmetic and copies ran while one was open for 9% -> 9% of each run, Pallas kernels for 12% -> 11%
where the time goes in v3:
time: 189 us
  waiting for transfers between devices  87.1 us (46%)
  starting transfers between devices  49.1 us (26%)
  Pallas kernels  27.5 us (15%)
  local copies, waits for them, and re-layouts  12.5 us (7%)
  other arithmetic  12 us (6%)
    ppermute x26, waiting for transfers between devices, near_pairs(): return lambda v: lax.ppermute(v, ('c', axis), table)  65.6 us
    ppermute x26, starting transfers between devices, near_pairs(): return lambda v: lax.ppermute(v, ('c', axis), table)  25.9 us
    pallas_call x1, Pallas kernels, rotate_out(): pl.pallas_call(rotate_out_kernel, out_shape=(shape, shape), in_specs=[pl....  15.2 us
    ppermute x3, waiting for transfers between devices, relay(): return lax.ppermute(v, ('zl', 'c', 'zh'), table)  11.8 us
    pallas_call x1, Pallas kernels, product(): pl.pallas_call(product_kernel, out_shape=(shape, shape), in_specs=[pl.Blo...  7.55 us
    ppermute x3, starting transfers between devices, flip_core(): return lax.ppermute(v, 'c', [(0, 1), (1, 0)])  6.81 us
    ppermute x3, starting transfers between devices, relay(): return lax.ppermute(v, ('zl', 'c', 'zh'), table)  5.2 us
    ppermute x3, starting transfers between devices, flip_both(): return lax.ppermute(v, ('zl', 'zh'), [(i, 3 - i) for i in range(4)])  5.08 us
  transfers between devices with their start and end apart: 40, of which 21 were waited for; matrix products, arithmetic and copies ran while one was open for 9% of the time, Pallas kernels for 11%

profile of v3, /device:TPU:1, one launch (start us, length us, event | category | flops | bytes accessed | tf_op | source)
XLA Modules:
  0.0 188.6 jit_solution(9163100748567787215)
XLA Ops:
  1.0 3.6 %collective-permute-start.10 = (bf16[2,8,4096]{2,1,0:T(8,128)(2,1)S(1)}, bf16[2,8,4096]{2,1,0:T(8,128)(2,1)S(1)}, u32[]{:S(2)}, u32[]{:S(2)}) collective-permute-start(bf16[2,8,4096]{2,1,0:T(8,128)(2,1)S(1)} %get-tuple-element.63), channel_id=1, source_target_pairs={{0,4},{4,0},{8,12},{12,8},{32,44},{36,40},{40,36},{44,32},{1,5},{5... | collective-permute-start | bytes 393224 | tf_op jit(solution)/shard_map/ppermute | solution.py:30
  8.2 3.8 %collective-permute-start = (bf16[2048,128]{1,0:T(8,128)(2,1)S(1)}, bf16[2048,128]{1,0:T(8,128)(2,1)}, u32[]{:S(2)}, u32[]{:S(2)}) collective-permute-start(bf16[2048,128]{1,0:T(8,128)(2,1)S(1)} %constant_dynamic-slice_fusion), channel_id=1, source_target_pairs={{0,80},{16,64},{64,16},{80,0},{1,81},{17,65},{65,17},{81,1},{2,82}... | collective-permute-start | bytes 1572872 | tf_op jit(solution)/shard_map/ppermute | solution.py:47
  13.5 3.0 %dynamic-slice_bitcast_fusion = bf16[176,5504]{1,0:T(8,128)(2,1)} fusion(bf16[11008,344]{0,1:T(8,128)(2,1)} %param.7, s32[]{:T(128)S(6)} %select_n.30, s32[]{:T(128)S(6)} %select_n.31), kind=kLoop, calls=%fused_computation.2 | loop fusion | bytes 3874824 | tf_op jit(solution)/shard_map/dynamic_slice | solution.py:263
  17.3 3.7 %collective-permute-done.4 = bf16[2,8,11008]{2,1,0:T(8,128)(2,1)S(1)} collective-permute-done((bf16[2,8,11008]{2,1,0:T(8,128)(2,1)S(1)}, bf16[2,8,11008]{2,1,0:T(8,128)(2,1)S(1)}, u32[]{:S(2)}, u32[]{:S(2)}) %collective-permute-start.4) | collective-permute-done | bytes 352288 | tf_op jit(solution)/shard_map/ppermute | solution.py:30
  22.8 2.6 %collective-permute-start.12 = (bf16[2,32,4096]{2,1,0:T(8,128)(2,1)S(1)}, bf16[2,32,4096]{2,1,0:T(8,128)(2,1)S(1)}, u32[]{:S(2)}, u32[]{:S(2)}) collective-permute-start(bf16[2,32,4096]{2,1,0:T(8,128)(2,1)S(1)} %pad_maximum_fusion.11), channel_id=1, source_target_pairs={{0,1},{1,0},{2,3},{3,2},{32,35},{33,34},{34,33},{35,32},{4,5},{5,4... | collective-permute-start | bytes 1572872 | tf_op jit(solution)/shard_map/ppermute | solution.py:30
  25.4 2.7 %collective-permute-start.8 = (bf16[2,32,4096]{2,1,0:T(8,128)(2,1)S(1)}, bf16[2,32,4096]{2,1,0:T(8,128)(2,1)S(1)}, u32[]{:S(2)}, u32[]{:S(2)}) collective-permute-start(bf16[2,32,4096]{2,1,0:T(8,128)(2,1)S(1)} %pad_maximum_fusion.10), channel_id=1, source_target_pairs={{0,4},{4,0},{8,12},{12,8},{32,44},{36,40},{40,36},{44,32},{1,5},{5... | collective-permute-start | bytes 1572872 | tf_op jit(solution)/shard_map/ppermute | solution.py:30
  29.1 11.1 %collective-permute-done.8 = bf16[2,32,4096]{2,1,0:T(8,128)(2,1)S(1)} collective-permute-done((bf16[2,32,4096]{2,1,0:T(8,128)(2,1)S(1)}, bf16[2,32,4096]{2,1,0:T(8,128)(2,1)S(1)}, u32[]{:S(2)}, u32[]{:S(2)}) %collective-permute-start.8) | collective-permute-done | bytes 524320 | tf_op jit(solution)/shard_map/ppermute | solution.py:30
  43.4 11.0 %collective-permute-done.9.refs_1_ = bf16[2,64,4096]{2,1,0:T(8,128)(2,1)S(1)} collective-permute-done((bf16[2,64,4096]{2,1,0:T(8,128)(2,1)S(1)}, bf16[2,64,4096]{2,1,0:T(8,128)(2,1)S(1)}, u32[]{:S(2)}, u32[]{:S(2)}) %collective-permute-start.9) | collective-permute-done | bytes 1048608 | tf_op jit(solution)/shard_map/ppermute | solution.py:30
  57.4 4.8 %rotate_in.1 = (bf16[512,128]{1,0:T(8,128)(2,1)}, bf16[512,128]{1,0:T(8,128)(2,1)}) custom-call(s32[2]{0:T(128)} %pad_add_fusion.flag_ref, bf16[2,64,4096]{2,1,0:T(8,128)(2,1)} %copy-done.1, bf16[2,64,4096]{2,1,0:T(8,128)(2,1)} %copy-done.6, bf16[2,64,4096]{2,1,0:T(8,128)(2,1)} %copy-done.2, bf16[2,64,4096]{2,1,0:T(8,128)(2,1)} %copy-done.7, ...), custom_call_target="tpu_custom_call" | custom-call | flops 1073741824 | bytes 6500000 | tf_op jit(solution)/shard_map/rotate_in/pallas_call | solution.py:93
  66.0 3.3 %broadcast_select_fusion.1 = bf16[176,5504]{1,0:T(8,128)(2,1)} fusion(bf16[176,5504]{1,0:T(8,128)(2,1)S(1)} %collective-permute-done.1, pred[]{:T(512)S(6)} %eq.4, bf16[11008,344]{0,1:T(8,128)(2,1)} %param.7, s32[]{:T(128)S(6)} %select_n.30, s32[]{:T(128)S(6)} %select_n.31), kind=kLoop, calls=%fused_computation.4 | loop fusion | flops 968704 | bytes 5812233 | tf_op jit(solution)/shard_map/jit(_where)/select_n | solution.py:287
  78.7 5.7 %collective-permute-done.23 = bf16[4,256,128]{2,1,0:T(8,128)(2,1)S(1)} collective-permute-done((bf16[4,256,128]{2,1,0:T(8,128)(2,1)S(1)}, bf16[4,256,128]{2,1,0:T(8,128)(2,1)S(1)}, u32[]{:S(2)}, u32[]{:S(2)}) %collective-permute-start.23) | collective-permute-done | bytes 262176 | tf_op jit(solution)/shard_map/ppermute | solution.py:30
  84.5 2.9 %collective-permute-done.20 = bf16[4,256,128]{2,1,0:T(8,128)(2,1)S(1)} collective-permute-done((bf16[4,256,128]{2,1,0:T(8,128)(2,1)}, bf16[4,256,128]{2,1,0:T(8,128)(2,1)S(1)}, u32[]{:S(2)}, u32[]{:S(2)}) %collective-permute-start.20) | collective-permute-done | bytes 262176 | tf_op jit(solution)/shard_map/ppermute | solution.py:30
  87.4 7.1 %collective-permute-done.26.refs_2_ = bf16[2,32,11008]{2,1,0:T(8,128)(2,1)} collective-permute-done((bf16[2,32,11008]{2,1,0:T(8,128)(2,1)}, bf16[2,32,11008]{2,1,0:T(8,128)(2,1)}, u32[]{:S(2)}, u32[]{:S(2)}) %collective-permute-start.26) | collective-permute-done | bytes 1409056 | tf_op jit(solution)/shard_map/ppermute | solution.py:30
  100.0 5.4 %collective-permute-done.21 = bf16[2,4,256,128]{3,2,1,0:T(8,128)(2,1)S(1)} collective-permute-done((bf16[2,4,256,128]{3,2,1,0:T(8,128)(2,1)S(1)}, bf16[2,4,256,128]{3,2,1,0:T(8,128)(2,1)S(1)}, u32[]{:S(2)}, u32[]{:S(2)}) %collective-permute-start.21) | collective-permute-done | bytes 524320 | tf_op jit(solution)/shard_map/ppermute | solution.py:30
  106.8 2.7 %collective-permute-start.25 = (bf16[4,4,256,128]{3,2,1,0:T(8,128)(2,1)S(1)}, bf16[4,4,256,128]{3,2,1,0:T(8,128)(2,1)S(1)}, u32[]{:S(2)}, u32[]{:S(2)}) collective-permute-start(bf16[4,4,256,128]{3,2,1,0:T(8,128)(2,1)S(1)} %pad_maximum_fusion.7), channel_id=1, source_target_pairs={{0,1},{1,0},{2,3},{3,2},{32,35},{33,34},{34,33},{35,32},{4,5},{5,4... | collective-permute-start | bytes 3145736 | tf_op jit(solution)/shard_map/ppermute | solution.py:30
  109.5 11.2 %collective-permute-done.31 = bf16[176,5504]{1,0:T(8,128)(2,1)S(1)} collective-permute-done((bf16[176,5504]{1,0:T(8,128)(2,1)}, bf16[176,5504]{1,0:T(8,128)(2,1)S(1)}, u32[]{:S(2)}, u32[]{:S(2)}) %collective-permute-start.31) | collective-permute-done | bytes 1937440 | tf_op jit(solution)/shard_map/ppermute | solution.py:22
  122.3 9.8 %collective-permute-done.22 = bf16[4,4,256,128]{3,2,1,0:T(8,128)(2,1)S(1)} collective-permute-done((bf16[4,4,256,128]{3,2,1,0:T(8,128)(2,1)S(1)}, bf16[4,4,256,128]{3,2,1,0:T(8,128)(2,1)S(1)}, u32[]{:S(2)}, u32[]{:S(2)}) %collective-permute-start.22) | collective-permute-done | bytes 1048608 | tf_op jit(solution)/shard_map/ppermute | solution.py:30
  139.5 15.2 %rotate_out.1 = (bf16[344,512]{1,0:T(8,128)(2,1)}, bf16[344,512]{1,0:T(8,128)(2,1)}) custom-call(s32[7]{0:T(128)} %stack.121.place_ref, bf16[2,32,11008]{2,1,0:T(8,128)(2,1)} %pad_maximum_fusion.2.refs_0_, bf16[2,32,11008]{2,1,0:T(8,128)(2,1)} %copy-done.10, bf16[2,32,11008]{2,1,0:T(8,128)(2,1)} %collective-permute-done.26.refs_2_, ...), custom_call_target="tpu_custom_call" | custom-call | flops 7845445632 | bytes 26595328 | tf_op jit(solution)/shard_map/rotate_out/pallas_call | solution.py:163
  158.2 4.3 %collective-permute-done.37.refs_5_ = bf16[8,4,256,128]{3,2,1,0:T(8,128)(2,1)} collective-permute-done((bf16[8,4,256,128]{3,2,1,0:T(8,128)(2,1)S(1)}, bf16[8,4,256,128]{3,2,1,0:T(8,128)(2,1)}, u32[]{:S(2)}, u32[]{:S(2)}) %collective-permute-start.37) | collective-permute-done | bytes 2097184 | tf_op jit(solution)/shard_map/ppermute | solution.py:30
  163.2 3.4 %collective-permute-done.36.refs_3_ = bf16[344,512]{1,0:T(8,128)(2,1)S(1)} collective-permute-done((bf16[344,512]{1,0:T(8,128)(2,1)}, bf16[344,512]{1,0:T(8,128)(2,1)S(1)}, u32[]{:S(2)}, u32[]{:S(2)}) %collective-permute-start.36) | collective-permute-done | bytes 352288 | tf_op jit(solution)/shard_map/ppermute | solution.py:47
  166.6 2.7 %collective-permute-done.34.refs_1_ = bf16[344,512]{1,0:T(8,128)(2,1)S(1)} collective-permute-done((bf16[344,512]{1,0:T(8,128)(2,1)}, bf16[344,512]{1,0:T(8,128)(2,1)S(1)}, u32[]{:S(2)}, u32[]{:S(2)}) %collective-permute-start.34) | collective-permute-done | bytes 352288 | tf_op jit(solution)/shard_map/ppermute | solution.py:39
  170.3 7.6 %squares.1 = (f32[344,1024]{1,0:T(8,128)S(1)}, f32[344,1024]{1,0:T(8,128)S(1)}) custom-call(s32[16]{0:T(128)S(1)} %stack.115.place_ref, bf16[344,512]{1,0:T(8,128)(2,1)S(1)} %copy-done, bf16[344,512]{1,0:T(8,128)(2,1)S(1)} %collective-permute-done.34.refs_1_, bf16[344,512]{1,0:T(8,128)(2,1)S(1)} %collective-permute-done.35.refs_2_, ...), custom_call_target="tpu_custom_call" | custom-call | flops 2885681152 | bytes 14000000 | tf_op jit(solution)/shard_map/squares/pallas_call | solution.py:231
  177.8 6.6 %collective-permute-start.39 = (f32[344,1024]{1,0:T(8,128)S(1)}, f32[344,1024]{1,0:T(8,128)S(1)}, u32[]{:S(2)}, u32[]{:S(2)}) collective-permute-start(f32[344,1024]{1,0:T(8,128)S(1)} %get-tuple-element.52), channel_id=1, source_target_pairs={{0,32},{32,0},{1,33},{33,1},{2,34},{34,2},{3,35},{35,3},{4,36},{36... | collective-permute-start | bytes 4227080 | tf_op jit(solution)/shard_map/ppermute | solution.py:51
  184.4 2.8 %collective-permute-done.39 = f32[344,1024]{1,0:T(8,128)S(1)} collective-permute-done((f32[344,1024]{1,0:T(8,128)S(1)}, f32[344,1024]{1,0:T(8,128)S(1)}, u32[]{:S(2)}, u32[]{:S(2)}) %collective-permute-start.39) | collective-permute-done | bytes 1409056 | tf_op jit(solution)/shard_map/ppermute | solution.py:51
  (122 shorter events, 51.3 us)
Async XLA Ops:
  1.0 16.1 %collective-permute-start.10 = (bf16[2,8,4096]{2,1,0:T(8,128)(2,1)S(1)}, bf16[2,8,4096]{2,1,0:T(8,128)(2,1)S(1)}, u32[]{:S(2)}, u32[]{:S(2)}) collective-permute-start(bf16[2,8,4096]{2,1,0:T(8,128)(2,1)S(1)} %get-tuple-element.63), channel_id=1, source_target_pairs={{0,4},{4,0},{8,12},{12,8},{32,44},{36,40},{40,36},{44,32},{1,5},{5... | collective-permute-start | bytes 393224 | tf_op jit(solution)/shard_map/ppermute | solution.py:30
  8.2 20.0 %collective-permute-start = (bf16[2048,128]{1,0:T(8,128)(2,1)S(1)}, bf16[2048,128]{1,0:T(8,128)(2,1)}, u32[]{:S(2)}, u32[]{:S(2)}) collective-permute-start(bf16[2048,128]{1,0:T(8,128)(2,1)S(1)} %constant_dynamic-slice_fusion), channel_id=1, source_target_pairs={{0,80},{16,64},{64,16},{80,0},{1,81},{17,65},{65,17},{81,1},{2,82}... | collective-permute-start | bytes 1572872 | tf_op jit(solution)/shard_map/ppermute | solution.py:47
  13.3 14.7 %collective-permute-start.2 = (bf16[2,8,11008]{2,1,0:T(8,128)(2,1)S(1)}, bf16[2,8,11008]{2,1,0:T(8,128)(2,1)S(1)}, u32[]{:S(2)}, u32[]{:S(2)}) collective-permute-start(bf16[2,8,11008]{2,1,0:T(8,128)(2,1)S(1)} %get-tuple-element.54), channel_id=1, source_target_pairs={{0,1},{1,0},{2,3},{3,2},{32,35},{33,34},{34,33},{35,32},{4,5},{5,4... | collective-permute-start | bytes 1056776 | tf_op jit(solution)/shard_map/ppermute | solution.py:30
  21.1 19.4 %collective-permute-start.5 = (bf16[2,16,11008]{2,1,0:T(8,128)(2,1)S(1)}, bf16[2,16,11008]{2,1,0:T(8,128)(2,1)S(1)}, u32[]{:S(2)}, u32[]{:S(2)}) collective-permute-start(bf16[2,16,11008]{2,1,0:T(8,128)(2,1)S(1)} %pad_maximum_fusion.9), channel_id=1, source_target_pairs={{0,12},{4,8},{8,4},{12,0},{32,36},{36,32},{40,44},{44,40},{1,13},{... | collective-permute-start | bytes 2113544 | tf_op jit(solution)/shard_map/ppermute | solution.py:30
  22.8 17.6 %collective-permute-start.12 = (bf16[2,32,4096]{2,1,0:T(8,128)(2,1)S(1)}, bf16[2,32,4096]{2,1,0:T(8,128)(2,1)S(1)}, u32[]{:S(2)}, u32[]{:S(2)}) collective-permute-start(bf16[2,32,4096]{2,1,0:T(8,128)(2,1)S(1)} %pad_maximum_fusion.11), channel_id=1, source_target_pairs={{0,1},{1,0},{2,3},{3,2},{32,35},{33,34},{34,33},{35,32},{4,5},{5,4... | collective-permute-start | bytes 1572872 | tf_op jit(solution)/shard_map/ppermute | solution.py:30
  25.4 14.9 %collective-permute-start.8 = (bf16[2,32,4096]{2,1,0:T(8,128)(2,1)S(1)}, bf16[2,32,4096]{2,1,0:T(8,128)(2,1)S(1)}, u32[]{:S(2)}, u32[]{:S(2)}) collective-permute-start(bf16[2,32,4096]{2,1,0:T(8,128)(2,1)S(1)} %pad_maximum_fusion.10), channel_id=1, source_target_pairs={{0,4},{4,0},{8,12},{12,8},{32,44},{36,40},{40,36},{44,32},{1,5},{5... | collective-permute-start | bytes 1572872 | tf_op jit(solution)/shard_map/ppermute | solution.py:30
  28.1 14.1 %collective-permute-start.3 = (bf16[2,16,11008]{2,1,0:T(8,128)(2,1)S(1)}, bf16[2,16,11008]{2,1,0:T(8,128)(2,1)S(1)}, u32[]{:S(2)}, u32[]{:S(2)}) collective-permute-start(bf16[2,16,11008]{2,1,0:T(8,128)(2,1)S(1)} %pad_maximum_fusion.8), channel_id=1, source_target_pairs={{0,3},{1,2},{2,1},{3,0},{32,33},{33,32},{34,35},{35,34},{4,7},{5,6... | collective-permute-start | bytes 2113544 | tf_op jit(solution)/shard_map/ppermute | solution.py:30
  28.2 28.4 %collective-permute-start.1 = (bf16[176,5504]{1,0:T(8,128)(2,1)S(1)}, bf16[176,5504]{1,0:T(8,128)(2,1)S(1)}, u32[]{:S(2)}, u32[]{:S(2)}) collective-permute-start(bf16[176,5504]{1,0:T(8,128)(2,1)S(1)} %copy-done.3), channel_id=1, source_target_pairs={{0,80},{16,64},{64,16},{80,0},{1,81},{17,65},{65,17},{81,1},{2,82}... | collective-permute-start | bytes 5812232 | tf_op jit(solution)/shard_map/ppermute | solution.py:22
  40.3 16.3 %collective-permute-start.14 = (bf16[2048,128]{1,0:T(8,128)(2,1)}, bf16[2048,128]{1,0:T(8,128)(2,1)S(1)}, u32[]{:S(2)}, u32[]{:S(2)}) collective-permute-start(bf16[2048,128]{1,0:T(8,128)(2,1)} %collective-permute-done.refs_5_), channel_id=1, source_target_pairs={{0,64},{64,0},{1,65},{65,1},{2,66},{66,2},{3,67},{67,3},{4,68},{68... | collective-permute-start | bytes 1572872 | tf_op jit(solution)/shard_map/ppermute | solution.py:43
  40.4 14.0 %collective-permute-start.9 = (bf16[2,64,4096]{2,1,0:T(8,128)(2,1)S(1)}, bf16[2,64,4096]{2,1,0:T(8,128)(2,1)S(1)}, u32[]{:S(2)}, u32[]{:S(2)}) collective-permute-start(bf16[2,64,4096]{2,1,0:T(8,128)(2,1)S(1)} %pad_maximum_fusion.4.refs_0_), channel_id=1, source_target_pairs={{0,12},{4,8},{8,4},{12,0},{32,36},{36,32},{40,44},{44,40},{1,13},{... | collective-permute-start | bytes 3145736 | tf_op jit(solution)/shard_map/ppermute | solution.py:30
  40.6 14.0 %collective-permute-start.13 = (bf16[2,64,4096]{2,1,0:T(8,128)(2,1)S(1)}, bf16[2,64,4096]{2,1,0:T(8,128)(2,1)S(1)}, u32[]{:S(2)}, u32[]{:S(2)}) collective-permute-start(bf16[2,64,4096]{2,1,0:T(8,128)(2,1)S(1)} %pad_maximum_fusion.5.refs_2_), channel_id=1, source_target_pairs={{0,3},{1,2},{2,1},{3,0},{32,33},{33,32},{34,35},{35,34},{4,7},{5,6... | collective-permute-start | bytes 3145736 | tf_op jit(solution)/shard_map/ppermute | solution.py:30
  54.6 18.9 %collective-permute-start.15 = (bf16[2,32,11008]{2,1,0:T(8,128)(2,1)}, bf16[2,32,11008]{2,1,0:T(8,128)(2,1)S(1)}, u32[]{:S(2)}, u32[]{:S(2)}) collective-permute-start(bf16[2,32,11008]{2,1,0:T(8,128)(2,1)} %pad_maximum_fusion.2.refs_0_), channel_id=1, source_target_pairs={{0,4},{4,0},{8,12},{12,8},{32,44},{36,40},{40,36},{44,32},{1,5},{5... | collective-permute-start | bytes 4227080 | tf_op jit(solution)/shard_map/ppermute | solution.py:30
  54.7 19.0 %collective-permute-start.16 = (bf16[2,32,11008]{2,1,0:T(8,128)(2,1)}, bf16[2,32,11008]{2,1,0:T(8,128)(2,1)}, u32[]{:S(2)}, u32[]{:S(2)}) collective-permute-start(bf16[2,32,11008]{2,1,0:T(8,128)(2,1)} %pad_maximum_fusion.3.refs_4_), channel_id=1, source_target_pairs={{0,1},{1,0},{2,3},{3,2},{32,35},{33,34},{34,33},{35,32},{4,5},{5,4... | collective-permute-start | bytes 4227080 | tf_op jit(solution)/shard_map/ppermute | solution.py:30
  70.1 25.0 %collective-permute-start.30 = (bf16[176,5504]{1,0:T(8,128)(2,1)}, bf16[176,5504]{1,0:T(8,128)(2,1)}, u32[]{:S(2)}, u32[]{:S(2)}) collective-permute-start(bf16[176,5504]{1,0:T(8,128)(2,1)} %broadcast_select_fusion.1), channel_id=1, source_target_pairs={{0,64},{16,80},{64,0},{80,16},{32,112},{48,96},{96,48},{112,32},{1... | collective-permute-start | bytes 5812232 | tf_op jit(solution)/shard_map/ppermute | solution.py:22
  72.5 22.0 %collective-permute-start.26 = (bf16[2,32,11008]{2,1,0:T(8,128)(2,1)}, bf16[2,32,11008]{2,1,0:T(8,128)(2,1)}, u32[]{:S(2)}, u32[]{:S(2)}) collective-permute-start(bf16[2,32,11008]{2,1,0:T(8,128)(2,1)} %pad_maximum_fusion.2.refs_0_), channel_id=1, source_target_pairs={{0,12},{4,8},{8,4},{12,0},{32,36},{36,32},{40,44},{44,40},{1,13},{... | collective-permute-start | bytes 4227080 | tf_op jit(solution)/shard_map/ppermute | solution.py:30
  72.5 22.0 %collective-permute-start.27 = (bf16[2,32,11008]{2,1,0:T(8,128)(2,1)}, bf16[2,32,11008]{2,1,0:T(8,128)(2,1)}, u32[]{:S(2)}, u32[]{:S(2)}) collective-permute-start(bf16[2,32,11008]{2,1,0:T(8,128)(2,1)} %pad_maximum_fusion.3.refs_4_), channel_id=1, source_target_pairs={{0,3},{1,2},{2,1},{3,0},{32,33},{33,32},{34,35},{35,34},{4,7},{5,6... | collective-permute-start | bytes 4227080 | tf_op jit(solution)/shard_map/ppermute | solution.py:30
  95.1 25.6 %collective-permute-start.31 = (bf16[176,5504]{1,0:T(8,128)(2,1)}, bf16[176,5504]{1,0:T(8,128)(2,1)S(1)}, u32[]{:S(2)}, u32[]{:S(2)}) collective-permute-start(bf16[176,5504]{1,0:T(8,128)(2,1)} %collective-permute-done.30.refs_10_), channel_id=1, source_target_pairs={{32,96},{48,112},{96,32},{112,48},{33,97},{49,113},{97,33},{113,49... | collective-permute-start | bytes 5812232 | tf_op jit(solution)/shard_map/ppermute | solution.py:22
  98.6 36.3 %collective-permute-start.28 = (bf16[2,32,11008]{2,1,0:T(8,128)(2,1)S(1)}, bf16[2,32,11008]{2,1,0:T(8,128)(2,1)S(1)}, u32[]{:S(2)}, u32[]{:S(2)}) collective-permute-start(bf16[2,32,11008]{2,1,0:T(8,128)(2,1)S(1)} %copy-done.11), channel_id=1, source_target_pairs={{0,12},{4,8},{8,4},{12,0},{32,36},{36,32},{40,44},{44,40},{1,13},{... | collective-permute-start | bytes 4227080 | tf_op jit(solution)/shard_map/ppermute | solution.py:30
  98.7 37.4 %collective-permute-start.29 = (bf16[2,32,11008]{2,1,0:T(8,128)(2,1)}, bf16[2,32,11008]{2,1,0:T(8,128)(2,1)S(1)}, u32[]{:S(2)}, u32[]{:S(2)}) collective-permute-start(bf16[2,32,11008]{2,1,0:T(8,128)(2,1)} %collective-permute-done.16.refs_5_), channel_id=1, source_target_pairs={{0,3},{1,2},{2,1},{3,0},{32,33},{33,32},{34,35},{35,34},{4,7},{5,6... | collective-permute-start | bytes 4227080 | tf_op jit(solution)/shard_map/ppermute | solution.py:30
  105.5 26.5 %collective-permute-start.22 = (bf16[4,4,256,128]{3,2,1,0:T(8,128)(2,1)S(1)}, bf16[4,4,256,128]{3,2,1,0:T(8,128)(2,1)S(1)}, u32[]{:S(2)}, u32[]{:S(2)}) collective-permute-start(bf16[4,4,256,128]{3,2,1,0:T(8,128)(2,1)S(1)} %pad_maximum_fusion.6), channel_id=1, source_target_pairs={{0,4},{4,0},{8,12},{12,8},{32,44},{36,40},{40,36},{44,32},{1,5},{5... | collective-permute-start | bytes 3145736 | tf_op jit(solution)/shard_map/ppermute | solution.py:30
  106.8 26.6 %collective-permute-start.25 = (bf16[4,4,256,128]{3,2,1,0:T(8,128)(2,1)S(1)}, bf16[4,4,256,128]{3,2,1,0:T(8,128)(2,1)S(1)}, u32[]{:S(2)}, u32[]{:S(2)}) collective-permute-start(bf16[4,4,256,128]{3,2,1,0:T(8,128)(2,1)S(1)} %pad_maximum_fusion.7), channel_id=1, source_target_pairs={{0,1},{1,0},{2,3},{3,2},{32,35},{33,34},{34,33},{35,32},{4,5},{5,4... | collective-permute-start | bytes 3145736 | tf_op jit(solution)/shard_map/ppermute | solution.py:30
  120.7 18.8 %collective-permute-start.32 = (bf16[176,5504]{1,0:T(8,128)(2,1)}, bf16[176,5504]{1,0:T(8,128)(2,1)}, u32[]{:S(2)}, u32[]{:S(2)}) collective-permute-start(bf16[176,5504]{1,0:T(8,128)(2,1)} %collective-permute-done.30.refs_10_), channel_id=1, source_target_pairs={{0,32},{32,0},{1,33},{33,1},{2,34},{34,2},{3,35},{35,3},{4,36},{36... | collective-permute-start | bytes 5812232 | tf_op jit(solution)/shard_map/ppermute | solution.py:51
  137.2 25.3 %collective-permute-start.37 = (bf16[8,4,256,128]{3,2,1,0:T(8,128)(2,1)S(1)}, bf16[8,4,256,128]{3,2,1,0:T(8,128)(2,1)}, u32[]{:S(2)}, u32[]{:S(2)}) collective-permute-start(bf16[8,4,256,128]{3,2,1,0:T(8,128)(2,1)S(1)} %pad_maximum_fusion.refs_4_), channel_id=1, source_target_pairs={{0,12},{4,8},{8,4},{12,0},{32,36},{36,32},{40,44},{44,40},{1,13},{... | collective-permute-start | bytes 6291464 | tf_op jit(solution)/shard_map/ppermute | solution.py:30
  137.7 25.5 %collective-permute-start.38 = (bf16[8,4,256,128]{3,2,1,0:T(8,128)(2,1)}, bf16[8,4,256,128]{3,2,1,0:T(8,128)(2,1)}, u32[]{:S(2)}, u32[]{:S(2)}) collective-permute-start(bf16[8,4,256,128]{3,2,1,0:T(8,128)(2,1)} %pad_maximum_fusion.1.refs_6_), channel_id=1, source_target_pairs={{0,3},{1,2},{2,1},{3,0},{32,33},{33,32},{34,35},{35,34},{4,7},{5,6... | collective-permute-start | bytes 6291464 | tf_op jit(solution)/shard_map/ppermute | solution.py:30
  (30 other events, 211.9 us)

commit v4 on v3

--- a/solution.py
+++ b/solution.py
@@ -7,8 +7,8 @@
 from jax.sharding import PartitionSpec as P
 
 AXES = ("zl", "c", "zh", "y", "x")
-ROOM = 56 * 1024 * 1024
-CUTS = ((0, 2816), (2816, 2688))
+ROOM = 54 * 1024 * 1024
+CUTS = (((0, 1024), (1024, 1792), (2816, 2688)), ((0, 2688), (2688, 1792), (4480, 1024)))
 
 
 def relay(v, hops):
@@ -95,7 +95,7 @@
         out_shape=(shape, shape),
         in_specs=[pl.BlockSpec(memory_space=pltpu.SMEM)] + [vmem] * 7,
         out_specs=(vmem, vmem),
-        compiler_params=pltpu.CompilerParams(vmem_limit_bytes=ROOM),
+        compiler_params=pltpu.CompilerParams(vmem_limit_bytes=24 * 1024 * 1024),
         cost_estimate=pl.CostEstimate(
             flops=2 * 512 * 256 * 4096, bytes_accessed=6_500_000, transcendentals=0
         ),
@@ -109,7 +109,7 @@
     copies = []
     for i in range(2):
         rows = [pl.multiple_of(place_ref[2 + 2 * i + j], 16) for j in range(2)]
-        for start, size in CUTS:
+        for start, size in CUTS[i]:
             lanes = slice(start, start + size)
             offset = pl.multiple_of(place_ref[i] + start, 128)
             group = [(own.at[:, pl.ds(offset, size)], kept_own[i].at[:, lanes])]
@@ -124,25 +124,28 @@
                     source = tokens[half * 4 + piece].at[:, :, pl.ds(offset, size)]
                     group.append((source, target))
             copies.append(
-                [
-                    pltpu.make_async_copy(source, target, sems.at[11 * len(copies) + j])
-                    for j, (source, target) in enumerate(group)
-                ]
+                (
+                    i,
+                    lanes,
+                    [
+                        pltpu.make_async_copy(source, target, sems.at[11 * len(copies) + j])
+                        for j, (source, target) in enumerate(group)
+                    ],
+                )
             )
-    for group in copies:
+    for _, _, group in copies:
         for copy in group:
             copy.start()
     total = [None, None]
-    for i, group in enumerate(copies):
+    for i, lanes, group in copies:
         for copy in group:
             copy.wait()
-        start, size = CUTS[i % 2]
-        lanes = slice(start, start + size)
-        basis = jnp.concatenate([kept_other[i // 2][:, lanes], kept_own[i // 2][:, lanes]], 0)
+        size = lanes.stop - lanes.start
+        basis = jnp.concatenate([kept_other[i][:, lanes], kept_own[i][:, lanes]], 0)
         for half in range(2):
             part = lax.dot_general(
                 basis,
-                kept_tokens[i // 2][half * 2 : half * 2 + 2, :, lanes].reshape(256, size),
+                kept_tokens[i][half * 2 : half * 2 + 2, :, lanes].reshape(256, size),
                 (((1,), (1,)), ((), ())),
                 preferred_element_type=jnp.float32,
             )
@@ -163,12 +166,14 @@
     return pl.pallas_call(
         rotate_out_kernel,
         out_shape=(shape, shape),
-        in_specs=[pl.BlockSpec(memory_space=pltpu.SMEM)] + [anywhere] * 13,
+        in_specs=[pl.BlockSpec(memory_space=pltpu.SMEM)]
+        + ([anywhere] * 3 + [vmem]) * 2
+        + [anywhere] * 5,
         out_specs=(vmem, vmem),
         scratch_shapes=[pltpu.VMEM((344, 5504), jnp.bfloat16)] * 2
         + [pltpu.VMEM((352, 5504), jnp.bfloat16)] * 2
         + [pltpu.VMEM((4, 128, 5504), jnp.bfloat16)] * 2
-        + [pltpu.SemaphoreType.DMA((44,))],
+        + [pltpu.SemaphoreType.DMA((66,))],
         compiler_params=pltpu.CompilerParams(vmem_limit_bytes=ROOM),
         cost_estimate=pl.CostEstimate(
             flops=2 * 512 * 696 * 11008, bytes_accessed=(512 + 696) * 22016, transcendentals=0
@@ -255,8 +260,8 @@
 
     basis_out = basis_out.T
 
+    g0 = [grads[2 * half : 2 * half + 2] for half in halves]
     a0 = [acts[2 * half : 2 * half + 2] for half in halves]
-    g0 = [grads[2 * half : 2 * half + 2] for half in halves]
     a1 = joined(a0, moved(a0, 0), 1)
     part = flip_both(lax.dynamic_slice_in_dim(basis_in, 2048 * (1 - zl), 2048, 0))
     other_in = part, flip_zl(part)
@@ -274,7 +279,7 @@
     keep, give = keep.reshape(4, 128, 128), give.reshape(4, 128, 128)
     exchanged = flip_zh(keep), flip_zl(give), flip_both(give)
     g3 = moved(g2, 2, *a4)
-    g4 = moved(g2, 3, *exchanged)
+    g4 = moved(g2, 3, keep)
     near = jnp.concatenate([after(keep, *g3), exchanged[0]], 1)
     far = jnp.concatenate(after(exchanged[1:], *g3), 1)
 
@@ -288,7 +293,7 @@
     third = relay(after(second, *c1, *g4), (None, "zl"))
 
     c2 = joined(c1, moved(c1, 1), 0)
-    g5 = moved(g3, 3, *c1, *g4)
+    g5 = moved(g3, 3, *g4)
     grads_pieces = [v[half] for half in halves for v in (g2, g3, g4, g5)]
     c3 = joined(c2, moved(c2, 2), 0)
     c4 = moved(c3, 3, *g5)

time: 189 us -> 186 us (0.984)
  Pallas kernels: 27.5 us -> 24.1 us
  starting transfers between devices: 49.1 us -> 46.6 us
  waiting for transfers between devices: 87.1 us -> 89.6 us
    ppermute x3, waiting for transfers between devices: 3.37 us -> 0.01 us  [flip_both(): return lax.ppermute(v, ('zl', 'zh'), [(i, 3 - i) for i in range(4)])]
    ppermute x2, waiting for transfers between devices: 3.5 us -> 6.82 us  [flip_zh(): return lax.ppermute(v, 'zh', [(0, 1), (1, 0)])]
    ppermute x26, waiting for transfers between devices: 65.6 us -> 68.6 us  [near_pairs(): return lambda v: lax.ppermute(v, ('c', axis), table)]
    pallas_call x1, Pallas kernels: 4.76 us -> 1.82 us  [rotate_in(): pl.pallas_call(rotate_in_kernel, out_shape=(shape, shape), in_specs=[pl.B...]
    unnamed x30 -> x32, local copies, waits for them, and re-layouts: 4.74 us -> 5.17 us
  transfers between devices with their start and end apart: 40 -> 40, of which waited for: 21 -> 18; matrix products, arithmetic and copies ran while one was open for 9% -> 9% of each run, Pallas kernels for 11% -> 9%
where the time goes in v4:
time: 186 us
  waiting for transfers between devices  89.6 us (48%)
  starting transfers between devices  46.6 us (25%)
  Pallas kernels  24.1 us (13%)
  local copies, waits for them, and re-layouts  12.9 us (7%)
  other arithmetic  12.1 us (7%)
    ppermute x26, waiting for transfers between devices, near_pairs(): return lambda v: lax.ppermute(v, ('c', axis), table)  68.6 us
    ppermute x26, starting transfers between devices, near_pairs(): return lambda v: lax.ppermute(v, ('c', axis), table)  25.2 us
    pallas_call x1, Pallas kernels, rotate_out(): pl.pallas_call(rotate_out_kernel, out_shape=(shape, shape), in_specs=[pl....  14.7 us
    ppermute x3, waiting for transfers between devices, relay(): return lax.ppermute(v, ('zl', 'c', 'zh'), table)  11.3 us
    pallas_call x1, Pallas kernels, product(): pl.pallas_call(product_kernel, out_shape=(shape, shape), in_specs=[pl.Blo...  7.55 us
    ppermute x2, waiting for transfers between devices, flip_zh(): return lax.ppermute(v, 'zh', [(0, 1), (1, 0)])  6.82 us
    concatenate x14, other arithmetic, joined(): return [jnp.concatenate([v[half], w[half]], axis) for half in halves]  5.67 us
    ppermute x3, starting transfers between devices, flip_both(): return lax.ppermute(v, ('zl', 'zh'), [(i, 3 - i) for i in range(4)])  5.56 us
  transfers between devices with their start and end apart: 40, of which 18 were waited for; matrix products, arithmetic and copies ran while one was open for 9% of the time, Pallas kernels for 9%

profile of v4, /device:TPU:1, one launch (start us, length us, event | category | flops | bytes accessed | tf_op | source)
XLA Modules:
  0.0 185.6 jit_solution(13474459501137087133)
XLA Ops:
  1.0 3.6 %collective-permute-start.10 = (bf16[2,8,4096]{2,1,0:T(8,128)(2,1)S(1)}, bf16[2,8,4096]{2,1,0:T(8,128)(2,1)S(1)}, u32[]{:S(2)}, u32[]{:S(2)}) collective-permute-start(bf16[2,8,4096]{2,1,0:T(8,128)(2,1)S(1)} %get-tuple-element.63), channel_id=1, source_target_pairs={{0,4},{4,0},{8,12},{12,8},{32,44},{36,40},{40,36},{44,32},{1,5},{5... | collective-permute-start | bytes 393224 | tf_op jit(solution)/shard_map/ppermute | solution.py:30
  4.6 2.5 %collective-permute-start.6 = (bf16[2,8,4096]{2,1,0:T(8,128)(2,1)S(1)}, bf16[2,8,4096]{2,1,0:T(8,128)(2,1)S(1)}, u32[]{:S(2)}, u32[]{:S(2)}) collective-permute-start(bf16[2,8,4096]{2,1,0:T(8,128)(2,1)S(1)} %get-tuple-element.64), channel_id=1, source_target_pairs={{0,1},{1,0},{2,3},{3,2},{32,35},{33,34},{34,33},{35,32},{4,5},{5,4... | collective-permute-start | bytes 393224 | tf_op jit(solution)/shard_map/ppermute | solution.py:30
  8.2 3.8 %collective-permute-start = (bf16[2048,128]{1,0:T(8,128)(2,1)S(1)}, bf16[2048,128]{1,0:T(8,128)(2,1)S(1)}, u32[]{:S(2)}, u32[]{:S(2)}) collective-permute-start(bf16[2048,128]{1,0:T(8,128)(2,1)S(1)} %constant_dynamic-slice_fusion), channel_id=1, source_target_pairs={{0,80},{16,64},{64,16},{80,0},{1,81},{17,65},{65,17},{81,1},{2,82}... | collective-permute-start | bytes 1572872 | tf_op jit(solution)/shard_map/ppermute | solution.py:47
  13.5 2.9 %dynamic-slice_bitcast_fusion = bf16[176,5504]{1,0:T(8,128)(2,1)} fusion(bf16[11008,344]{0,1:T(8,128)(2,1)} %param.7, s32[]{:T(128)S(6)} %select_n.30, s32[]{:T(128)S(6)} %select_n.31), kind=kLoop, calls=%fused_computation.2 | loop fusion | bytes 3874824 | tf_op jit(solution)/shard_map/dynamic_slice | solution.py:268
  16.8 4.4 %collective-permute-done.4 = bf16[2,8,11008]{2,1,0:T(8,128)(2,1)S(1)} collective-permute-done((bf16[2,8,11008]{2,1,0:T(8,128)(2,1)S(1)}, bf16[2,8,11008]{2,1,0:T(8,128)(2,1)S(1)}, u32[]{:S(2)}, u32[]{:S(2)}) %collective-permute-start.4) | collective-permute-done | bytes 352288 | tf_op jit(solution)/shard_map/ppermute | solution.py:30
  22.2 2.6 %collective-permute-start.12 = (bf16[2,32,4096]{2,1,0:T(8,128)(2,1)S(1)}, bf16[2,32,4096]{2,1,0:T(8,128)(2,1)S(1)}, u32[]{:S(2)}, u32[]{:S(2)}) collective-permute-start(bf16[2,32,4096]{2,1,0:T(8,128)(2,1)S(1)} %pad_maximum_fusion.11), channel_id=1, source_target_pairs={{0,1},{1,0},{2,3},{3,2},{32,35},{33,34},{34,33},{35,32},{4,5},{5,4... | collective-permute-start | bytes 1572872 | tf_op jit(solution)/shard_map/ppermute | solution.py:30
  24.8 2.7 %collective-permute-start.8 = (bf16[2,32,4096]{2,1,0:T(8,128)(2,1)S(1)}, bf16[2,32,4096]{2,1,0:T(8,128)(2,1)S(1)}, u32[]{:S(2)}, u32[]{:S(2)}) collective-permute-start(bf16[2,32,4096]{2,1,0:T(8,128)(2,1)S(1)} %pad_maximum_fusion.10), channel_id=1, source_target_pairs={{0,4},{4,0},{8,12},{12,8},{32,44},{36,40},{40,36},{44,32},{1,5},{5... | collective-permute-start | bytes 1572872 | tf_op jit(solution)/shard_map/ppermute | solution.py:30
  29.2 10.6 %collective-permute-done.8 = bf16[2,32,4096]{2,1,0:T(8,128)(2,1)S(1)} collective-permute-done((bf16[2,32,4096]{2,1,0:T(8,128)(2,1)S(1)}, bf16[2,32,4096]{2,1,0:T(8,128)(2,1)S(1)}, u32[]{:S(2)}, u32[]{:S(2)}) %collective-permute-start.8) | collective-permute-done | bytes 524320 | tf_op jit(solution)/shard_map/ppermute | solution.py:30
  43.5 11.3 %collective-permute-done.9.refs_1_ = bf16[2,64,4096]{2,1,0:T(8,128)(2,1)S(1)} collective-permute-done((bf16[2,64,4096]{2,1,0:T(8,128)(2,1)S(1)}, bf16[2,64,4096]{2,1,0:T(8,128)(2,1)S(1)}, u32[]{:S(2)}, u32[]{:S(2)}) %collective-permute-start.9) | collective-permute-done | bytes 1048608 | tf_op jit(solution)/shard_map/ppermute | solution.py:30
  62.8 3.3 %broadcast_select_fusion.1 = bf16[176,5504]{1,0:T(8,128)(2,1)} fusion(bf16[176,5504]{1,0:T(8,128)(2,1)S(1)} %collective-permute-done.1, pred[]{:T(512)S(6)} %eq.4, bf16[11008,344]{0,1:T(8,128)(2,1)} %param.7, s32[]{:T(128)S(6)} %select_n.30, s32[]{:T(128)S(6)} %select_n.31), kind=kLoop, calls=%fused_computation.4 | loop fusion | flops 968704 | bytes 5812233 | tf_op jit(solution)/shard_map/jit(_where)/select_n | solution.py:292
  69.5 4.4 %collective-permute-done.15.refs_1_ = bf16[2,32,11008]{2,1,0:T(8,128)(2,1)S(1)} collective-permute-done((bf16[2,32,11008]{2,1,0:T(8,128)(2,1)}, bf16[2,32,11008]{2,1,0:T(8,128)(2,1)S(1)}, u32[]{:S(2)}, u32[]{:S(2)}) %collective-permute-start.15) | collective-permute-done | bytes 1409056 | tf_op jit(solution)/shard_map/ppermute | solution.py:30
  75.5 2.7 %collective-permute-start.23 = (bf16[4,256,128]{2,1,0:T(8,128)(2,1)S(1)}, bf16[4,256,128]{2,1,0:T(8,128)(2,1)S(1)}, u32[]{:S(2)}, u32[]{:S(2)}) collective-permute-start(bf16[4,256,128]{2,1,0:T(8,128)(2,1)S(1)} %bitcast.52), channel_id=1, source_target_pairs={{0,4},{4,0},{8,12},{12,8},{32,44},{36,40},{40,36},{44,32},{1,5},{5... | collective-permute-start | bytes 786440 | tf_op jit(solution)/shard_map/ppermute | solution.py:30
  79.0 6.3 %collective-permute-done.23 = bf16[4,256,128]{2,1,0:T(8,128)(2,1)S(1)} collective-permute-done((bf16[4,256,128]{2,1,0:T(8,128)(2,1)S(1)}, bf16[4,256,128]{2,1,0:T(8,128)(2,1)S(1)}, u32[]{:S(2)}, u32[]{:S(2)}) %collective-permute-start.23) | collective-permute-done | bytes 262176 | tf_op jit(solution)/shard_map/ppermute | solution.py:30
  85.4 3.5 %collective-permute-done.20 = bf16[4,256,128]{2,1,0:T(8,128)(2,1)S(1)} collective-permute-done((bf16[4,256,128]{2,1,0:T(8,128)(2,1)}, bf16[4,256,128]{2,1,0:T(8,128)(2,1)S(1)}, u32[]{:S(2)}, u32[]{:S(2)}) %collective-permute-start.20) | collective-permute-done | bytes 262176 | tf_op jit(solution)/shard_map/ppermute | solution.py:30
  89.0 5.0 %collective-permute-done.26.refs_2_ = bf16[2,32,11008]{2,1,0:T(8,128)(2,1)} collective-permute-done((bf16[2,32,11008]{2,1,0:T(8,128)(2,1)}, bf16[2,32,11008]{2,1,0:T(8,128)(2,1)}, u32[]{:S(2)}, u32[]{:S(2)}) %collective-permute-start.26) | collective-permute-done | bytes 1409056 | tf_op jit(solution)/shard_map/ppermute | solution.py:30
  99.3 5.2 %collective-permute-done.21 = bf16[2,4,256,128]{3,2,1,0:T(8,128)(2,1)S(1)} collective-permute-done((bf16[2,4,256,128]{3,2,1,0:T(8,128)(2,1)S(1)}, bf16[2,4,256,128]{3,2,1,0:T(8,128)(2,1)S(1)}, u32[]{:S(2)}, u32[]{:S(2)}) %collective-permute-start.21) | collective-permute-done | bytes 524320 | tf_op jit(solution)/shard_map/ppermute | solution.py:30
  108.2 11.3 %collective-permute-done.31 = bf16[176,5504]{1,0:T(8,128)(2,1)S(1)} collective-permute-done((bf16[176,5504]{1,0:T(8,128)(2,1)}, bf16[176,5504]{1,0:T(8,128)(2,1)S(1)}, u32[]{:S(2)}, u32[]{:S(2)}) %collective-permute-start.31) | collective-permute-done | bytes 1937440 | tf_op jit(solution)/shard_map/ppermute | solution.py:22
  121.2 9.9 %collective-permute-done.22 = bf16[4,4,256,128]{3,2,1,0:T(8,128)(2,1)S(1)} collective-permute-done((bf16[4,4,256,128]{3,2,1,0:T(8,128)(2,1)S(1)}, bf16[4,4,256,128]{3,2,1,0:T(8,128)(2,1)S(1)}, u32[]{:S(2)}, u32[]{:S(2)}) %collective-permute-start.22) | collective-permute-done | bytes 1048608 | tf_op jit(solution)/shard_map/ppermute | solution.py:30
  138.3 14.7 %rotate_out.1 = (bf16[344,512]{1,0:T(8,128)(2,1)}, bf16[344,512]{1,0:T(8,128)(2,1)}) custom-call(s32[7]{0:T(128)} %stack.121.place_ref, bf16[2,32,11008]{2,1,0:T(8,128)(2,1)} %pad_maximum_fusion.2.refs_0_, bf16[2,32,11008]{2,1,0:T(8,128)(2,1)} %copy-done.10, bf16[2,32,11008]{2,1,0:T(8,128)(2,1)} %collective-permute-done.26.refs_2_, ...), custom_call_target="tpu_custom_call" | custom-call | flops 7845445632 | bytes 26595328 | tf_op jit(solution)/shard_map/rotate_out/pallas_call | solution.py:166
  156.5 5.2 %collective-permute-done.37.refs_5_ = bf16[8,4,256,128]{3,2,1,0:T(8,128)(2,1)} collective-permute-done((bf16[8,4,256,128]{3,2,1,0:T(8,128)(2,1)S(1)}, bf16[8,4,256,128]{3,2,1,0:T(8,128)(2,1)}, u32[]{:S(2)}, u32[]{:S(2)}) %collective-permute-start.37) | collective-permute-done | bytes 2097184 | tf_op jit(solution)/shard_map/ppermute | solution.py:30
  162.6 5.4 %collective-permute-done.34.refs_1_ = bf16[344,512]{1,0:T(8,128)(2,1)S(1)} collective-permute-done((bf16[344,512]{1,0:T(8,128)(2,1)}, bf16[344,512]{1,0:T(8,128)(2,1)S(1)}, u32[]{:S(2)}, u32[]{:S(2)}) %collective-permute-start.34) | collective-permute-done | bytes 352288 | tf_op jit(solution)/shard_map/ppermute | solution.py:39
  169.0 7.6 %squares.1 = (f32[344,1024]{1,0:T(8,128)S(1)}, f32[344,1024]{1,0:T(8,128)S(1)}) custom-call(s32[16]{0:T(128)S(1)} %stack.115.place_ref, bf16[344,512]{1,0:T(8,128)(2,1)S(1)} %copy-done.1, bf16[344,512]{1,0:T(8,128)(2,1)S(1)} %collective-permute-done.34.refs_1_, bf16[344,512]{1,0:T(8,128)(2,1)S(1)} %collective-permute-done.35.refs_2_, ...), custom_call_target="tpu_custom_call" | custom-call | flops 2885681152 | bytes 14000000 | tf_op jit(solution)/shard_map/squares/pallas_call | solution.py:236
  176.6 4.9 %collective-permute-start.39 = (f32[344,1024]{1,0:T(8,128)S(1)}, f32[344,1024]{1,0:T(8,128)S(1)}, u32[]{:S(2)}, u32[]{:S(2)}) collective-permute-start(f32[344,1024]{1,0:T(8,128)S(1)} %get-tuple-element.52), channel_id=1, source_target_pairs={{0,32},{32,0},{1,33},{33,1},{2,34},{34,2},{3,35},{35,3},{4,36},{36... | collective-permute-start | bytes 4227080 | tf_op jit(solution)/shard_map/ppermute | solution.py:51
  181.5 2.8 %collective-permute-done.39 = f32[344,1024]{1,0:T(8,128)S(1)} collective-permute-done((f32[344,1024]{1,0:T(8,128)S(1)}, f32[344,1024]{1,0:T(8,128)S(1)}, u32[]{:S(2)}, u32[]{:S(2)}) %collective-permute-start.39) | collective-permute-done | bytes 1409056 | tf_op jit(solution)/shard_map/ppermute | solution.py:51
  (124 shorter events, 48.5 us)
Async XLA Ops:
  1.0 15.6 %collective-permute-start.10 = (bf16[2,8,4096]{2,1,0:T(8,128)(2,1)S(1)}, bf16[2,8,4096]{2,1,0:T(8,128)(2,1)S(1)}, u32[]{:S(2)}, u32[]{:S(2)}) collective-permute-start(bf16[2,8,4096]{2,1,0:T(8,128)(2,1)S(1)} %get-tuple-element.63), channel_id=1, source_target_pairs={{0,4},{4,0},{8,12},{12,8},{32,44},{36,40},{40,36},{44,32},{1,5},{5... | collective-permute-start | bytes 393224 | tf_op jit(solution)/shard_map/ppermute | solution.py:30
  8.2 20.1 %collective-permute-start = (bf16[2048,128]{1,0:T(8,128)(2,1)S(1)}, bf16[2048,128]{1,0:T(8,128)(2,1)S(1)}, u32[]{:S(2)}, u32[]{:S(2)}) collective-permute-start(bf16[2048,128]{1,0:T(8,128)(2,1)S(1)} %constant_dynamic-slice_fusion), channel_id=1, source_target_pairs={{0,80},{16,64},{64,16},{80,0},{1,81},{17,65},{65,17},{81,1},{2,82}... | collective-permute-start | bytes 1572872 | tf_op jit(solution)/shard_map/ppermute | solution.py:47
  13.3 14.2 %collective-permute-start.2 = (bf16[2,8,11008]{2,1,0:T(8,128)(2,1)S(1)}, bf16[2,8,11008]{2,1,0:T(8,128)(2,1)S(1)}, u32[]{:S(2)}, u32[]{:S(2)}) collective-permute-start(bf16[2,8,11008]{2,1,0:T(8,128)(2,1)S(1)} %get-tuple-element.54), channel_id=1, source_target_pairs={{0,1},{1,0},{2,3},{3,2},{32,35},{33,34},{34,33},{35,32},{4,5},{5,4... | collective-permute-start | bytes 1056776 | tf_op jit(solution)/shard_map/ppermute | solution.py:30
  21.3 19.7 %collective-permute-start.5 = (bf16[2,16,11008]{2,1,0:T(8,128)(2,1)S(1)}, bf16[2,16,11008]{2,1,0:T(8,128)(2,1)S(1)}, u32[]{:S(2)}, u32[]{:S(2)}) collective-permute-start(bf16[2,16,11008]{2,1,0:T(8,128)(2,1)S(1)} %pad_maximum_fusion.9), channel_id=1, source_target_pairs={{0,12},{4,8},{8,4},{12,0},{32,36},{36,32},{40,44},{44,40},{1,13},{... | collective-permute-start | bytes 2113544 | tf_op jit(solution)/shard_map/ppermute | solution.py:30
  22.2 18.5 %collective-permute-start.12 = (bf16[2,32,4096]{2,1,0:T(8,128)(2,1)S(1)}, bf16[2,32,4096]{2,1,0:T(8,128)(2,1)S(1)}, u32[]{:S(2)}, u32[]{:S(2)}) collective-permute-start(bf16[2,32,4096]{2,1,0:T(8,128)(2,1)S(1)} %pad_maximum_fusion.11), channel_id=1, source_target_pairs={{0,1},{1,0},{2,3},{3,2},{32,35},{33,34},{34,33},{35,32},{4,5},{5,4... | collective-permute-start | bytes 1572872 | tf_op jit(solution)/shard_map/ppermute | solution.py:30
  24.8 14.9 %collective-permute-start.8 = (bf16[2,32,4096]{2,1,0:T(8,128)(2,1)S(1)}, bf16[2,32,4096]{2,1,0:T(8,128)(2,1)S(1)}, u32[]{:S(2)}, u32[]{:S(2)}) collective-permute-start(bf16[2,32,4096]{2,1,0:T(8,128)(2,1)S(1)} %pad_maximum_fusion.10), channel_id=1, source_target_pairs={{0,4},{4,0},{8,12},{12,8},{32,44},{36,40},{40,36},{44,32},{1,5},{5... | collective-permute-start | bytes 1572872 | tf_op jit(solution)/shard_map/ppermute | solution.py:30
  27.6 14.7 %collective-permute-start.3 = (bf16[2,16,11008]{2,1,0:T(8,128)(2,1)S(1)}, bf16[2,16,11008]{2,1,0:T(8,128)(2,1)S(1)}, u32[]{:S(2)}, u32[]{:S(2)}) collective-permute-start(bf16[2,16,11008]{2,1,0:T(8,128)(2,1)S(1)} %pad_maximum_fusion.8), channel_id=1, source_target_pairs={{0,3},{1,2},{2,1},{3,0},{32,33},{33,32},{34,35},{35,34},{4,7},{5,6... | collective-permute-start | bytes 2113544 | tf_op jit(solution)/shard_map/ppermute | solution.py:30
  28.2 28.8 %collective-permute-start.1 = (bf16[176,5504]{1,0:T(8,128)(2,1)S(1)}, bf16[176,5504]{1,0:T(8,128)(2,1)S(1)}, u32[]{:S(2)}, u32[]{:S(2)}) collective-permute-start(bf16[176,5504]{1,0:T(8,128)(2,1)S(1)} %copy-done.2), channel_id=1, source_target_pairs={{0,80},{16,64},{64,16},{80,0},{1,81},{17,65},{65,17},{81,1},{2,82}... | collective-permute-start | bytes 5812232 | tf_op jit(solution)/shard_map/ppermute | solution.py:22
  39.7 17.3 %collective-permute-start.14 = (bf16[2048,128]{1,0:T(8,128)(2,1)S(1)}, bf16[2048,128]{1,0:T(8,128)(2,1)S(1)}, u32[]{:S(2)}, u32[]{:S(2)}) collective-permute-start(bf16[2048,128]{1,0:T(8,128)(2,1)S(1)} %collective-permute-done.refs_5_), channel_id=1, source_target_pairs={{0,64},{64,0},{1,65},{65,1},{2,66},{66,2},{3,67},{67,3},{4,68},{68... | collective-permute-start | bytes 1572872 | tf_op jit(solution)/shard_map/ppermute | solution.py:43
  40.8 14.0 %collective-permute-start.9 = (bf16[2,64,4096]{2,1,0:T(8,128)(2,1)S(1)}, bf16[2,64,4096]{2,1,0:T(8,128)(2,1)S(1)}, u32[]{:S(2)}, u32[]{:S(2)}) collective-permute-start(bf16[2,64,4096]{2,1,0:T(8,128)(2,1)S(1)} %pad_maximum_fusion.4.refs_0_), channel_id=1, source_target_pairs={{0,12},{4,8},{8,4},{12,0},{32,36},{36,32},{40,44},{44,40},{1,13},{... | collective-permute-start | bytes 3145736 | tf_op jit(solution)/shard_map/ppermute | solution.py:30
  41.0 14.0 %collective-permute-start.13 = (bf16[2,64,4096]{2,1,0:T(8,128)(2,1)S(1)}, bf16[2,64,4096]{2,1,0:T(8,128)(2,1)S(1)}, u32[]{:S(2)}, u32[]{:S(2)}) collective-permute-start(bf16[2,64,4096]{2,1,0:T(8,128)(2,1)S(1)} %pad_maximum_fusion.5.refs_2_), channel_id=1, source_target_pairs={{0,3},{1,2},{2,1},{3,0},{32,33},{33,32},{34,35},{35,34},{4,7},{5,6... | collective-permute-start | bytes 3145736 | tf_op jit(solution)/shard_map/ppermute | solution.py:30
  55.0 18.9 %collective-permute-start.15 = (bf16[2,32,11008]{2,1,0:T(8,128)(2,1)}, bf16[2,32,11008]{2,1,0:T(8,128)(2,1)S(1)}, u32[]{:S(2)}, u32[]{:S(2)}) collective-permute-start(bf16[2,32,11008]{2,1,0:T(8,128)(2,1)} %pad_maximum_fusion.2.refs_0_), channel_id=1, source_target_pairs={{0,4},{4,0},{8,12},{12,8},{32,44},{36,40},{40,36},{44,32},{1,5},{5... | collective-permute-start | bytes 4227080 | tf_op jit(solution)/shard_map/ppermute | solution.py:30
  55.0 18.9 %collective-permute-start.16 = (bf16[2,32,11008]{2,1,0:T(8,128)(2,1)}, bf16[2,32,11008]{2,1,0:T(8,128)(2,1)S(1)}, u32[]{:S(2)}, u32[]{:S(2)}) collective-permute-start(bf16[2,32,11008]{2,1,0:T(8,128)(2,1)} %pad_maximum_fusion.3.refs_4_), channel_id=1, source_target_pairs={{0,1},{1,0},{2,3},{3,2},{32,35},{33,34},{34,33},{35,32},{4,5},{5,4... | collective-permute-start | bytes 4227080 | tf_op jit(solution)/shard_map/ppermute | solution.py:30
  67.4 26.5 %collective-permute-start.30 = (bf16[176,5504]{1,0:T(8,128)(2,1)}, bf16[176,5504]{1,0:T(8,128)(2,1)}, u32[]{:S(2)}, u32[]{:S(2)}) collective-permute-start(bf16[176,5504]{1,0:T(8,128)(2,1)} %broadcast_select_fusion.1), channel_id=1, source_target_pairs={{0,64},{16,80},{64,0},{80,16},{32,112},{48,96},{96,48},{112,32},{1... | collective-permute-start | bytes 5812232 | tf_op jit(solution)/shard_map/ppermute | solution.py:22
  69.3 24.6 %collective-permute-start.26 = (bf16[2,32,11008]{2,1,0:T(8,128)(2,1)}, bf16[2,32,11008]{2,1,0:T(8,128)(2,1)}, u32[]{:S(2)}, u32[]{:S(2)}) collective-permute-start(bf16[2,32,11008]{2,1,0:T(8,128)(2,1)} %pad_maximum_fusion.2.refs_0_), channel_id=1, source_target_pairs={{0,12},{4,8},{8,4},{12,0},{32,36},{36,32},{40,44},{44,40},{1,13},{... | collective-permute-start | bytes 4227080 | tf_op jit(solution)/shard_map/ppermute | solution.py:30
  69.5 24.4 %collective-permute-start.27 = (bf16[2,32,11008]{2,1,0:T(8,128)(2,1)}, bf16[2,32,11008]{2,1,0:T(8,128)(2,1)}, u32[]{:S(2)}, u32[]{:S(2)}) collective-permute-start(bf16[2,32,11008]{2,1,0:T(8,128)(2,1)} %pad_maximum_fusion.3.refs_4_), channel_id=1, source_target_pairs={{0,3},{1,2},{2,1},{3,0},{32,33},{33,32},{34,35},{35,34},{4,7},{5,6... | collective-permute-start | bytes 4227080 | tf_op jit(solution)/shard_map/ppermute | solution.py:30
  94.0 25.6 %collective-permute-start.31 = (bf16[176,5504]{1,0:T(8,128)(2,1)}, bf16[176,5504]{1,0:T(8,128)(2,1)S(1)}, u32[]{:S(2)}, u32[]{:S(2)}) collective-permute-start(bf16[176,5504]{1,0:T(8,128)(2,1)} %collective-permute-done.30.refs_10_), channel_id=1, source_target_pairs={{32,96},{48,112},{96,32},{112,48},{33,97},{49,113},{97,33},{113,49... | collective-permute-start | bytes 5812232 | tf_op jit(solution)/shard_map/ppermute | solution.py:22
  98.0 36.1 %collective-permute-start.28 = (bf16[2,32,11008]{2,1,0:T(8,128)(2,1)S(1)}, bf16[2,32,11008]{2,1,0:T(8,128)(2,1)S(1)}, u32[]{:S(2)}, u32[]{:S(2)}) collective-permute-start(bf16[2,32,11008]{2,1,0:T(8,128)(2,1)S(1)} %copy-done.11), channel_id=1, source_target_pairs={{0,12},{4,8},{8,4},{12,0},{32,36},{36,32},{40,44},{44,40},{1,13},{... | collective-permute-start | bytes 4227080 | tf_op jit(solution)/shard_map/ppermute | solution.py:30
  98.1 37.2 %collective-permute-start.29 = (bf16[2,32,11008]{2,1,0:T(8,128)(2,1)}, bf16[2,32,11008]{2,1,0:T(8,128)(2,1)S(1)}, u32[]{:S(2)}, u32[]{:S(2)}) collective-permute-start(bf16[2,32,11008]{2,1,0:T(8,128)(2,1)} %copy-done.12), channel_id=1, source_target_pairs={{0,3},{1,2},{2,1},{3,0},{32,33},{33,32},{34,35},{35,34},{4,7},{5,6... | collective-permute-start | bytes 4227080 | tf_op jit(solution)/shard_map/ppermute | solution.py:30
  104.6 26.5 %collective-permute-start.22 = (bf16[4,4,256,128]{3,2,1,0:T(8,128)(2,1)S(1)}, bf16[4,4,256,128]{3,2,1,0:T(8,128)(2,1)S(1)}, u32[]{:S(2)}, u32[]{:S(2)}) collective-permute-start(bf16[4,4,256,128]{3,2,1,0:T(8,128)(2,1)S(1)} %pad_maximum_fusion.6), channel_id=1, source_target_pairs={{0,4},{4,0},{8,12},{12,8},{32,44},{36,40},{40,36},{44,32},{1,5},{5... | collective-permute-start | bytes 3145736 | tf_op jit(solution)/shard_map/ppermute | solution.py:30
  106.8 25.8 %collective-permute-start.25 = (bf16[4,4,256,128]{3,2,1,0:T(8,128)(2,1)S(1)}, bf16[4,4,256,128]{3,2,1,0:T(8,128)(2,1)S(1)}, u32[]{:S(2)}, u32[]{:S(2)}) collective-permute-start(bf16[4,4,256,128]{3,2,1,0:T(8,128)(2,1)S(1)} %pad_maximum_fusion.7), channel_id=1, source_target_pairs={{0,1},{1,0},{2,3},{3,2},{32,35},{33,34},{34,33},{35,32},{4,5},{5,4... | collective-permute-start | bytes 3145736 | tf_op jit(solution)/shard_map/ppermute | solution.py:30
  119.5 18.7 %collective-permute-start.32 = (bf16[176,5504]{1,0:T(8,128)(2,1)}, bf16[176,5504]{1,0:T(8,128)(2,1)}, u32[]{:S(2)}, u32[]{:S(2)}) collective-permute-start(bf16[176,5504]{1,0:T(8,128)(2,1)} %collective-permute-done.30.refs_10_), channel_id=1, source_target_pairs={{0,32},{32,0},{1,33},{33,1},{2,34},{34,2},{3,35},{35,3},{4,36},{36... | collective-permute-start | bytes 5812232 | tf_op jit(solution)/shard_map/ppermute | solution.py:51
  136.4 25.3 %collective-permute-start.37 = (bf16[8,4,256,128]{3,2,1,0:T(8,128)(2,1)S(1)}, bf16[8,4,256,128]{3,2,1,0:T(8,128)(2,1)}, u32[]{:S(2)}, u32[]{:S(2)}) collective-permute-start(bf16[8,4,256,128]{3,2,1,0:T(8,128)(2,1)S(1)} %pad_maximum_fusion.refs_4_), channel_id=1, source_target_pairs={{0,12},{4,8},{8,4},{12,0},{32,36},{36,32},{40,44},{44,40},{1,13},{... | collective-permute-start | bytes 6291464 | tf_op jit(solution)/shard_map/ppermute | solution.py:30
  137.1 25.5 %collective-permute-start.38 = (bf16[8,4,256,128]{3,2,1,0:T(8,128)(2,1)}, bf16[8,4,256,128]{3,2,1,0:T(8,128)(2,1)}, u32[]{:S(2)}, u32[]{:S(2)}) collective-permute-start(bf16[8,4,256,128]{3,2,1,0:T(8,128)(2,1)} %pad_maximum_fusion.1.refs_6_), channel_id=1, source_target_pairs={{0,3},{1,2},{2,1},{3,0},{32,33},{33,32},{34,35},{35,34},{4,7},{5,6... | collective-permute-start | bytes 6291464 | tf_op jit(solution)/shard_map/ppermute | solution.py:30
  (31 other events, 241.1 us)

commit v5 on v4

--- a/solution.py
+++ b/solution.py
@@ -183,7 +183,11 @@
 
 
 def product_kernel(place_ref, *refs):
-    lefts, rights, (keep_ref, give_ref) = refs[:4], refs[4:8], refs[8:]
+    lefts, sources, (keep_ref, give_ref) = refs[:4], refs[4:8], refs[8:10]
+    rights, sems = refs[10:14], refs[14]
+    copies = [pltpu.make_async_copy(sources[i], rights[i], sems.at[i]) for i in range(4)]
+    for i in (0, 2, 1, 3):
+        copies[i].start()
 
     def left(half, group, example):
         lane = (half * 2 + example) * 128
@@ -199,11 +203,13 @@
                 tiles.append(ref[piece % 8, example, row : row + 16, :])
         return jnp.concatenate(tiles, 0)
 
-    for pair in range(8):
-        sources = (2 * pair, 2 * pair + 1)
+    for first, arrived in ((0, (0, 2)), (8, (1,)), (2, (3,)), (10, ())):
+        for i in arrived:
+            copies[i].wait()
+        blocks = (first, first + 1, first + 4, first + 5)
         total = None
         for half in range(2):
-            pieces = [s if half == 0 else (s % 4) * 4 + s // 4 for s in sources]
+            pieces = [s if half == 0 else (s % 4) * 4 + s // 4 for s in blocks]
             for group in range(2):
                 for example in range(2):
                     rhs = jnp.concatenate(
@@ -215,7 +221,7 @@
                     square = product * product
                     total = square if total is None else total + square
         total = total * (1.0 / 16.0)
-        for i, s in enumerate(sources):
+        for i, s in enumerate(blocks):
             place = place_ref[s]
             column = pl.multiple_of(lax.rem(place, 8) * 128, 128)
             part = total[:, i * 128 : (i + 1) * 128]
@@ -236,8 +242,10 @@
     return pl.pallas_call(
         product_kernel,
         out_shape=(shape, shape),
-        in_specs=[pl.BlockSpec(memory_space=pltpu.SMEM)] + [vmem] * 8,
+        in_specs=[pl.BlockSpec(memory_space=pltpu.SMEM)] + [vmem] * 4 + [pl.BlockSpec(memory_space=pl.ANY)] * 4,
         out_specs=(vmem, vmem),
+        scratch_shapes=[pltpu.VMEM(rights[0].shape, jnp.bfloat16)] * 4
+        + [pltpu.SemaphoreType.DMA((4,))],
         compiler_params=pltpu.CompilerParams(vmem_limit_bytes=24 * 1024 * 1024),
         cost_estimate=pl.CostEstimate(
             flops=2 * 8 * 256 * rows * 2048, bytes_accessed=14_000_000, transcendentals=0

time: 186 us -> 185 us (level)
  transfers between devices with their start and end apart: 40 -> 40, of which waited for: 18 -> 18; matrix products, arithmetic and copies ran while one was open for 9% -> 10% of each run, Pallas kernels for 9% -> 9%
where the time goes in v5:
time: 185 us; the launch traced here: 184 us
  waiting for transfers between devices  89.6 us (48%)
  starting transfers between devices  46.6 us (25%)
  Pallas kernels  23 us (12%)
  local copies, waits for them, and re-layouts  12.9 us (7%)
  other arithmetic  12.1 us (7%)
    ppermute x26, waiting for transfers between devices, near_pairs(): return lambda v: lax.ppermute(v, ('c', axis), table)  68.6 us
    ppermute x26, starting transfers between devices, near_pairs(): return lambda v: lax.ppermute(v, ('c', axis), table)  25.2 us
    pallas_call x1, Pallas kernels, rotate_out(): pl.pallas_call(rotate_out_kernel, out_shape=(shape, shape), in_specs=[pl....  14.7 us
    ppermute x3, waiting for transfers between devices, relay(): return lax.ppermute(v, ('zl', 'c', 'zh'), table)  11.3 us
    ppermute x2, waiting for transfers between devices, flip_zh(): return lax.ppermute(v, 'zh', [(0, 1), (1, 0)])  6.82 us
    pallas_call x1, Pallas kernels, product(): pl.pallas_call(product_kernel, out_shape=(shape, shape), in_specs=[pl.Blo...  6.4 us
    concatenate x14, other arithmetic, joined(): return [jnp.concatenate([v[half], w[half]], axis) for half in halves]  5.67 us
    ppermute x3, starting transfers between devices, flip_both(): return lax.ppermute(v, ('zl', 'zh'), [(i, 3 - i) for i in range(4)])  5.56 us
  transfers between devices with their start and end apart: 40, of which 18 were waited for; matrix products, arithmetic and copies ran while one was open for 10% of the time, Pallas kernels for 9%

profile of v5, /device:TPU:1, one launch (start us, length us, event | category | flops | bytes accessed | tf_op | source)
XLA Modules:
  0.0 184.5 jit_solution(14430990317551455474)
XLA Ops:
  1.0 3.6 %collective-permute-start.10 = (bf16[2,8,4096]{2,1,0:T(8,128)(2,1)S(1)}, bf16[2,8,4096]{2,1,0:T(8,128)(2,1)S(1)}, u32[]{:S(2)}, u32[]{:S(2)}) collective-permute-start(bf16[2,8,4096]{2,1,0:T(8,128)(2,1)S(1)} %get-tuple-element.63), channel_id=1, source_target_pairs={{0,4},{4,0},{8,12},{12,8},{32,44},{36,40},{40,36},{44,32},{1,5},{5... | collective-permute-start | bytes 393224 | tf_op jit(solution)/shard_map/ppermute | solution.py:30
  4.6 2.5 %collective-permute-start.6 = (bf16[2,8,4096]{2,1,0:T(8,128)(2,1)S(1)}, bf16[2,8,4096]{2,1,0:T(8,128)(2,1)S(1)}, u32[]{:S(2)}, u32[]{:S(2)}) collective-permute-start(bf16[2,8,4096]{2,1,0:T(8,128)(2,1)S(1)} %get-tuple-element.64), channel_id=1, source_target_pairs={{0,1},{1,0},{2,3},{3,2},{32,35},{33,34},{34,33},{35,32},{4,5},{5,4... | collective-permute-start | bytes 393224 | tf_op jit(solution)/shard_map/ppermute | solution.py:30
  8.2 3.8 %collective-permute-start = (bf16[2048,128]{1,0:T(8,128)(2,1)S(1)}, bf16[2048,128]{1,0:T(8,128)(2,1)S(1)}, u32[]{:S(2)}, u32[]{:S(2)}) collective-permute-start(bf16[2048,128]{1,0:T(8,128)(2,1)S(1)} %constant_dynamic-slice_fusion), channel_id=1, source_target_pairs={{0,80},{16,64},{64,16},{80,0},{1,81},{17,65},{65,17},{81,1},{2,82}... | collective-permute-start | bytes 1572872 | tf_op jit(solution)/shard_map/ppermute | solution.py:47
  13.5 2.9 %dynamic-slice_bitcast_fusion = bf16[176,5504]{1,0:T(8,128)(2,1)} fusion(bf16[11008,344]{0,1:T(8,128)(2,1)} %param.7, s32[]{:T(128)S(6)} %select_n.30, s32[]{:T(128)S(6)} %select_n.31), kind=kLoop, calls=%fused_computation.2 | loop fusion | bytes 3874824 | tf_op jit(solution)/shard_map/dynamic_slice | solution.py:276
  16.8 4.4 %collective-permute-done.4 = bf16[2,8,11008]{2,1,0:T(8,128)(2,1)S(1)} collective-permute-done((bf16[2,8,11008]{2,1,0:T(8,128)(2,1)S(1)}, bf16[2,8,11008]{2,1,0:T(8,128)(2,1)S(1)}, u32[]{:S(2)}, u32[]{:S(2)}) %collective-permute-start.4) | collective-permute-done | bytes 352288 | tf_op jit(solution)/shard_map/ppermute | solution.py:30
  22.2 2.6 %collective-permute-start.12 = (bf16[2,32,4096]{2,1,0:T(8,128)(2,1)S(1)}, bf16[2,32,4096]{2,1,0:T(8,128)(2,1)S(1)}, u32[]{:S(2)}, u32[]{:S(2)}) collective-permute-start(bf16[2,32,4096]{2,1,0:T(8,128)(2,1)S(1)} %pad_maximum_fusion.11), channel_id=1, source_target_pairs={{0,1},{1,0},{2,3},{3,2},{32,35},{33,34},{34,33},{35,32},{4,5},{5,4... | collective-permute-start | bytes 1572872 | tf_op jit(solution)/shard_map/ppermute | solution.py:30
  24.8 2.7 %collective-permute-start.8 = (bf16[2,32,4096]{2,1,0:T(8,128)(2,1)S(1)}, bf16[2,32,4096]{2,1,0:T(8,128)(2,1)S(1)}, u32[]{:S(2)}, u32[]{:S(2)}) collective-permute-start(bf16[2,32,4096]{2,1,0:T(8,128)(2,1)S(1)} %pad_maximum_fusion.10), channel_id=1, source_target_pairs={{0,4},{4,0},{8,12},{12,8},{32,44},{36,40},{40,36},{44,32},{1,5},{5... | collective-permute-start | bytes 1572872 | tf_op jit(solution)/shard_map/ppermute | solution.py:30
  29.2 10.6 %collective-permute-done.8 = bf16[2,32,4096]{2,1,0:T(8,128)(2,1)S(1)} collective-permute-done((bf16[2,32,4096]{2,1,0:T(8,128)(2,1)S(1)}, bf16[2,32,4096]{2,1,0:T(8,128)(2,1)S(1)}, u32[]{:S(2)}, u32[]{:S(2)}) %collective-permute-start.8) | collective-permute-done | bytes 524320 | tf_op jit(solution)/shard_map/ppermute | solution.py:30
  43.5 11.3 %collective-permute-done.9.refs_1_ = bf16[2,64,4096]{2,1,0:T(8,128)(2,1)S(1)} collective-permute-done((bf16[2,64,4096]{2,1,0:T(8,128)(2,1)S(1)}, bf16[2,64,4096]{2,1,0:T(8,128)(2,1)S(1)}, u32[]{:S(2)}, u32[]{:S(2)}) %collective-permute-start.9) | collective-permute-done | bytes 1048608 | tf_op jit(solution)/shard_map/ppermute | solution.py:30
  62.8 3.3 %broadcast_select_fusion.1 = bf16[176,5504]{1,0:T(8,128)(2,1)} fusion(bf16[176,5504]{1,0:T(8,128)(2,1)S(1)} %collective-permute-done.1, pred[]{:T(512)S(6)} %eq.4, bf16[11008,344]{0,1:T(8,128)(2,1)} %param.7, s32[]{:T(128)S(6)} %select_n.30, s32[]{:T(128)S(6)} %select_n.31), kind=kLoop, calls=%fused_computation.4 | loop fusion | flops 968704 | bytes 5812233 | tf_op jit(solution)/shard_map/jit(_where)/select_n | solution.py:300
  69.5 4.4 %collective-permute-done.15.refs_1_ = bf16[2,32,11008]{2,1,0:T(8,128)(2,1)S(1)} collective-permute-done((bf16[2,32,11008]{2,1,0:T(8,128)(2,1)}, bf16[2,32,11008]{2,1,0:T(8,128)(2,1)S(1)}, u32[]{:S(2)}, u32[]{:S(2)}) %collective-permute-start.15) | collective-permute-done | bytes 1409056 | tf_op jit(solution)/shard_map/ppermute | solution.py:30
  75.5 2.7 %collective-permute-start.23 = (bf16[4,256,128]{2,1,0:T(8,128)(2,1)S(1)}, bf16[4,256,128]{2,1,0:T(8,128)(2,1)S(1)}, u32[]{:S(2)}, u32[]{:S(2)}) collective-permute-start(bf16[4,256,128]{2,1,0:T(8,128)(2,1)S(1)} %bitcast.52), channel_id=1, source_target_pairs={{0,4},{4,0},{8,12},{12,8},{32,44},{36,40},{40,36},{44,32},{1,5},{5... | collective-permute-start | bytes 786440 | tf_op jit(solution)/shard_map/ppermute | solution.py:30
  79.0 6.3 %collective-permute-done.23 = bf16[4,256,128]{2,1,0:T(8,128)(2,1)S(1)} collective-permute-done((bf16[4,256,128]{2,1,0:T(8,128)(2,1)S(1)}, bf16[4,256,128]{2,1,0:T(8,128)(2,1)S(1)}, u32[]{:S(2)}, u32[]{:S(2)}) %collective-permute-start.23) | collective-permute-done | bytes 262176 | tf_op jit(solution)/shard_map/ppermute | solution.py:30
  85.4 3.5 %collective-permute-done.20 = bf16[4,256,128]{2,1,0:T(8,128)(2,1)S(1)} collective-permute-done((bf16[4,256,128]{2,1,0:T(8,128)(2,1)}, bf16[4,256,128]{2,1,0:T(8,128)(2,1)S(1)}, u32[]{:S(2)}, u32[]{:S(2)}) %collective-permute-start.20) | collective-permute-done | bytes 262176 | tf_op jit(solution)/shard_map/ppermute | solution.py:30
  89.0 5.0 %collective-permute-done.26.refs_2_ = bf16[2,32,11008]{2,1,0:T(8,128)(2,1)} collective-permute-done((bf16[2,32,11008]{2,1,0:T(8,128)(2,1)}, bf16[2,32,11008]{2,1,0:T(8,128)(2,1)}, u32[]{:S(2)}, u32[]{:S(2)}) %collective-permute-start.26) | collective-permute-done | bytes 1409056 | tf_op jit(solution)/shard_map/ppermute | solution.py:30
  99.3 5.2 %collective-permute-done.21 = bf16[2,4,256,128]{3,2,1,0:T(8,128)(2,1)S(1)} collective-permute-done((bf16[2,4,256,128]{3,2,1,0:T(8,128)(2,1)S(1)}, bf16[2,4,256,128]{3,2,1,0:T(8,128)(2,1)S(1)}, u32[]{:S(2)}, u32[]{:S(2)}) %collective-permute-start.21) | collective-permute-done | bytes 524320 | tf_op jit(solution)/shard_map/ppermute | solution.py:30
  108.2 11.3 %collective-permute-done.31 = bf16[176,5504]{1,0:T(8,128)(2,1)S(1)} collective-permute-done((bf16[176,5504]{1,0:T(8,128)(2,1)}, bf16[176,5504]{1,0:T(8,128)(2,1)S(1)}, u32[]{:S(2)}, u32[]{:S(2)}) %collective-permute-start.31) | collective-permute-done | bytes 1937440 | tf_op jit(solution)/shard_map/ppermute | solution.py:22
  121.2 9.9 %collective-permute-done.22 = bf16[4,4,256,128]{3,2,1,0:T(8,128)(2,1)S(1)} collective-permute-done((bf16[4,4,256,128]{3,2,1,0:T(8,128)(2,1)S(1)}, bf16[4,4,256,128]{3,2,1,0:T(8,128)(2,1)S(1)}, u32[]{:S(2)}, u32[]{:S(2)}) %collective-permute-start.22) | collective-permute-done | bytes 1048608 | tf_op jit(solution)/shard_map/ppermute | solution.py:30
  138.3 14.7 %rotate_out.1 = (bf16[344,512]{1,0:T(8,128)(2,1)}, bf16[344,512]{1,0:T(8,128)(2,1)}) custom-call(s32[7]{0:T(128)} %stack.121.place_ref, bf16[2,32,11008]{2,1,0:T(8,128)(2,1)} %pad_maximum_fusion.2.refs_0_, bf16[2,32,11008]{2,1,0:T(8,128)(2,1)} %copy-done.10, bf16[2,32,11008]{2,1,0:T(8,128)(2,1)} %collective-permute-done.26.refs_2_, ...), custom_call_target="tpu_custom_call" | custom-call | flops 7845445632 | bytes 26595328 | tf_op jit(solution)/shard_map/rotate_out/pallas_call | solution.py:166
  156.5 5.2 %collective-permute-done.37.refs_5_ = bf16[8,4,256,128]{3,2,1,0:T(8,128)(2,1)} collective-permute-done((bf16[8,4,256,128]{3,2,1,0:T(8,128)(2,1)S(1)}, bf16[8,4,256,128]{3,2,1,0:T(8,128)(2,1)}, u32[]{:S(2)}, u32[]{:S(2)}) %collective-permute-start.37) | collective-permute-done | bytes 2097184 | tf_op jit(solution)/shard_map/ppermute | solution.py:30
  162.6 5.4 %collective-permute-done.34.refs_1_ = bf16[344,512]{1,0:T(8,128)(2,1)S(1)} collective-permute-done((bf16[344,512]{1,0:T(8,128)(2,1)}, bf16[344,512]{1,0:T(8,128)(2,1)S(1)}, u32[]{:S(2)}, u32[]{:S(2)}) %collective-permute-start.34) | collective-permute-done | bytes 352288 | tf_op jit(solution)/shard_map/ppermute | solution.py:39
  169.0 6.4 %squares.1 = (f32[344,1024]{1,0:T(8,128)S(1)}, f32[344,1024]{1,0:T(8,128)S(1)}) custom-call(s32[16]{0:T(128)S(1)} %stack.115.place_ref, bf16[344,512]{1,0:T(8,128)(2,1)S(1)} %copy-done.1, bf16[344,512]{1,0:T(8,128)(2,1)S(1)} %collective-permute-done.34.refs_1_, bf16[344,512]{1,0:T(8,128)(2,1)S(1)} %collective-permute-done.35.refs_2_, ...), custom_call_target="tpu_custom_call" | custom-call | flops 2885681152 | bytes 14000000 | tf_op jit(solution)/shard_map/squares/pallas_call | solution.py:242
  175.5 4.9 %collective-permute-start.39 = (f32[344,1024]{1,0:T(8,128)S(1)}, f32[344,1024]{1,0:T(8,128)S(1)}, u32[]{:S(2)}, u32[]{:S(2)}) collective-permute-start(f32[344,1024]{1,0:T(8,128)S(1)} %get-tuple-element.52), channel_id=1, source_target_pairs={{0,32},{32,0},{1,33},{33,1},{2,34},{34,2},{3,35},{35,3},{4,36},{36... | collective-permute-start | bytes 4227080 | tf_op jit(solution)/shard_map/ppermute | solution.py:51
  180.4 2.8 %collective-permute-done.39 = f32[344,1024]{1,0:T(8,128)S(1)} collective-permute-done((f32[344,1024]{1,0:T(8,128)S(1)}, f32[344,1024]{1,0:T(8,128)S(1)}, u32[]{:S(2)}, u32[]{:S(2)}) %collective-permute-start.39) | collective-permute-done | bytes 1409056 | tf_op jit(solution)/shard_map/ppermute | solution.py:51
  (124 shorter events, 48.5 us)
Async XLA Ops:
  1.0 15.6 %collective-permute-start.10 = (bf16[2,8,4096]{2,1,0:T(8,128)(2,1)S(1)}, bf16[2,8,4096]{2,1,0:T(8,128)(2,1)S(1)}, u32[]{:S(2)}, u32[]{:S(2)}) collective-permute-start(bf16[2,8,4096]{2,1,0:T(8,128)(2,1)S(1)} %get-tuple-element.63), channel_id=1, source_target_pairs={{0,4},{4,0},{8,12},{12,8},{32,44},{36,40},{40,36},{44,32},{1,5},{5... | collective-permute-start | bytes 393224 | tf_op jit(solution)/shard_map/ppermute | solution.py:30
  8.2 20.1 %collective-permute-start = (bf16[2048,128]{1,0:T(8,128)(2,1)S(1)}, bf16[2048,128]{1,0:T(8,128)(2,1)S(1)}, u32[]{:S(2)}, u32[]{:S(2)}) collective-permute-start(bf16[2048,128]{1,0:T(8,128)(2,1)S(1)} %constant_dynamic-slice_fusion), channel_id=1, source_target_pairs={{0,80},{16,64},{64,16},{80,0},{1,81},{17,65},{65,17},{81,1},{2,82}... | collective-permute-start | bytes 1572872 | tf_op jit(solution)/shard_map/ppermute | solution.py:47
  13.3 14.2 %collective-permute-start.2 = (bf16[2,8,11008]{2,1,0:T(8,128)(2,1)S(1)}, bf16[2,8,11008]{2,1,0:T(8,128)(2,1)S(1)}, u32[]{:S(2)}, u32[]{:S(2)}) collective-permute-start(bf16[2,8,11008]{2,1,0:T(8,128)(2,1)S(1)} %get-tuple-element.54), channel_id=1, source_target_pairs={{0,1},{1,0},{2,3},{3,2},{32,35},{33,34},{34,33},{35,32},{4,5},{5,4... | collective-permute-start | bytes 1056776 | tf_op jit(solution)/shard_map/ppermute | solution.py:30
  21.3 19.7 %collective-permute-start.5 = (bf16[2,16,11008]{2,1,0:T(8,128)(2,1)S(1)}, bf16[2,16,11008]{2,1,0:T(8,128)(2,1)S(1)}, u32[]{:S(2)}, u32[]{:S(2)}) collective-permute-start(bf16[2,16,11008]{2,1,0:T(8,128)(2,1)S(1)} %pad_maximum_fusion.9), channel_id=1, source_target_pairs={{0,12},{4,8},{8,4},{12,0},{32,36},{36,32},{40,44},{44,40},{1,13},{... | collective-permute-start | bytes 2113544 | tf_op jit(solution)/shard_map/ppermute | solution.py:30
  22.2 18.5 %collective-permute-start.12 = (bf16[2,32,4096]{2,1,0:T(8,128)(2,1)S(1)}, bf16[2,32,4096]{2,1,0:T(8,128)(2,1)S(1)}, u32[]{:S(2)}, u32[]{:S(2)}) collective-permute-start(bf16[2,32,4096]{2,1,0:T(8,128)(2,1)S(1)} %pad_maximum_fusion.11), channel_id=1, source_target_pairs={{0,1},{1,0},{2,3},{3,2},{32,35},{33,34},{34,33},{35,32},{4,5},{5,4... | collective-permute-start | bytes 1572872 | tf_op jit(solution)/shard_map/ppermute | solution.py:30
  24.8 14.9 %collective-permute-start.8 = (bf16[2,32,4096]{2,1,0:T(8,128)(2,1)S(1)}, bf16[2,32,4096]{2,1,0:T(8,128)(2,1)S(1)}, u32[]{:S(2)}, u32[]{:S(2)}) collective-permute-start(bf16[2,32,4096]{2,1,0:T(8,128)(2,1)S(1)} %pad_maximum_fusion.10), channel_id=1, source_target_pairs={{0,4},{4,0},{8,12},{12,8},{32,44},{36,40},{40,36},{44,32},{1,5},{5... | collective-permute-start | bytes 1572872 | tf_op jit(solution)/shard_map/ppermute | solution.py:30
  27.6 14.7 %collective-permute-start.3 = (bf16[2,16,11008]{2,1,0:T(8,128)(2,1)S(1)}, bf16[2,16,11008]{2,1,0:T(8,128)(2,1)S(1)}, u32[]{:S(2)}, u32[]{:S(2)}) collective-permute-start(bf16[2,16,11008]{2,1,0:T(8,128)(2,1)S(1)} %pad_maximum_fusion.8), channel_id=1, source_target_pairs={{0,3},{1,2},{2,1},{3,0},{32,33},{33,32},{34,35},{35,34},{4,7},{5,6... | collective-permute-start | bytes 2113544 | tf_op jit(solution)/shard_map/ppermute | solution.py:30
  28.2 28.8 %collective-permute-start.1 = (bf16[176,5504]{1,0:T(8,128)(2,1)S(1)}, bf16[176,5504]{1,0:T(8,128)(2,1)S(1)}, u32[]{:S(2)}, u32[]{:S(2)}) collective-permute-start(bf16[176,5504]{1,0:T(8,128)(2,1)S(1)} %copy-done.2), channel_id=1, source_target_pairs={{0,80},{16,64},{64,16},{80,0},{1,81},{17,65},{65,17},{81,1},{2,82}... | collective-permute-start | bytes 5812232 | tf_op jit(solution)/shard_map/ppermute | solution.py:22
  39.7 17.3 %collective-permute-start.14 = (bf16[2048,128]{1,0:T(8,128)(2,1)S(1)}, bf16[2048,128]{1,0:T(8,128)(2,1)S(1)}, u32[]{:S(2)}, u32[]{:S(2)}) collective-permute-start(bf16[2048,128]{1,0:T(8,128)(2,1)S(1)} %collective-permute-done.refs_5_), channel_id=1, source_target_pairs={{0,64},{64,0},{1,65},{65,1},{2,66},{66,2},{3,67},{67,3},{4,68},{68... | collective-permute-start | bytes 1572872 | tf_op jit(solution)/shard_map/ppermute | solution.py:43
  40.8 14.0 %collective-permute-start.9 = (bf16[2,64,4096]{2,1,0:T(8,128)(2,1)S(1)}, bf16[2,64,4096]{2,1,0:T(8,128)(2,1)S(1)}, u32[]{:S(2)}, u32[]{:S(2)}) collective-permute-start(bf16[2,64,4096]{2,1,0:T(8,128)(2,1)S(1)} %pad_maximum_fusion.4.refs_0_), channel_id=1, source_target_pairs={{0,12},{4,8},{8,4},{12,0},{32,36},{36,32},{40,44},{44,40},{1,13},{... | collective-permute-start | bytes 3145736 | tf_op jit(solution)/shard_map/ppermute | solution.py:30
  41.0 14.0 %collective-permute-start.13 = (bf16[2,64,4096]{2,1,0:T(8,128)(2,1)S(1)}, bf16[2,64,4096]{2,1,0:T(8,128)(2,1)S(1)}, u32[]{:S(2)}, u32[]{:S(2)}) collective-permute-start(bf16[2,64,4096]{2,1,0:T(8,128)(2,1)S(1)} %pad_maximum_fusion.5.refs_2_), channel_id=1, source_target_pairs={{0,3},{1,2},{2,1},{3,0},{32,33},{33,32},{34,35},{35,34},{4,7},{5,6... | collective-permute-start | bytes 3145736 | tf_op jit(solution)/shard_map/ppermute | solution.py:30
  55.0 18.9 %collective-permute-start.15 = (bf16[2,32,11008]{2,1,0:T(8,128)(2,1)}, bf16[2,32,11008]{2,1,0:T(8,128)(2,1)S(1)}, u32[]{:S(2)}, u32[]{:S(2)}) collective-permute-start(bf16[2,32,11008]{2,1,0:T(8,128)(2,1)} %pad_maximum_fusion.2.refs_0_), channel_id=1, source_target_pairs={{0,4},{4,0},{8,12},{12,8},{32,44},{36,40},{40,36},{44,32},{1,5},{5... | collective-permute-start | bytes 4227080 | tf_op jit(solution)/shard_map/ppermute | solution.py:30
  55.0 18.9 %collective-permute-start.16 = (bf16[2,32,11008]{2,1,0:T(8,128)(2,1)}, bf16[2,32,11008]{2,1,0:T(8,128)(2,1)S(1)}, u32[]{:S(2)}, u32[]{:S(2)}) collective-permute-start(bf16[2,32,11008]{2,1,0:T(8,128)(2,1)} %pad_maximum_fusion.3.refs_4_), channel_id=1, source_target_pairs={{0,1},{1,0},{2,3},{3,2},{32,35},{33,34},{34,33},{35,32},{4,5},{5,4... | collective-permute-start | bytes 4227080 | tf_op jit(solution)/shard_map/ppermute | solution.py:30
  67.4 26.5 %collective-permute-start.30 = (bf16[176,5504]{1,0:T(8,128)(2,1)}, bf16[176,5504]{1,0:T(8,128)(2,1)}, u32[]{:S(2)}, u32[]{:S(2)}) collective-permute-start(bf16[176,5504]{1,0:T(8,128)(2,1)} %broadcast_select_fusion.1), channel_id=1, source_target_pairs={{0,64},{16,80},{64,0},{80,16},{32,112},{48,96},{96,48},{112,32},{1... | collective-permute-start | bytes 5812232 | tf_op jit(solution)/shard_map/ppermute | solution.py:22
  69.3 24.6 %collective-permute-start.26 = (bf16[2,32,11008]{2,1,0:T(8,128)(2,1)}, bf16[2,32,11008]{2,1,0:T(8,128)(2,1)}, u32[]{:S(2)}, u32[]{:S(2)}) collective-permute-start(bf16[2,32,11008]{2,1,0:T(8,128)(2,1)} %pad_maximum_fusion.2.refs_0_), channel_id=1, source_target_pairs={{0,12},{4,8},{8,4},{12,0},{32,36},{36,32},{40,44},{44,40},{1,13},{... | collective-permute-start | bytes 4227080 | tf_op jit(solution)/shard_map/ppermute | solution.py:30
  69.5 24.4 %collective-permute-start.27 = (bf16[2,32,11008]{2,1,0:T(8,128)(2,1)}, bf16[2,32,11008]{2,1,0:T(8,128)(2,1)}, u32[]{:S(2)}, u32[]{:S(2)}) collective-permute-start(bf16[2,32,11008]{2,1,0:T(8,128)(2,1)} %pad_maximum_fusion.3.refs_4_), channel_id=1, source_target_pairs={{0,3},{1,2},{2,1},{3,0},{32,33},{33,32},{34,35},{35,34},{4,7},{5,6... | collective-permute-start | bytes 4227080 | tf_op jit(solution)/shard_map/ppermute | solution.py:30
  94.0 25.6 %collective-permute-start.31 = (bf16[176,5504]{1,0:T(8,128)(2,1)}, bf16[176,5504]{1,0:T(8,128)(2,1)S(1)}, u32[]{:S(2)}, u32[]{:S(2)}) collective-permute-start(bf16[176,5504]{1,0:T(8,128)(2,1)} %collective-permute-done.30.refs_10_), channel_id=1, source_target_pairs={{32,96},{48,112},{96,32},{112,48},{33,97},{49,113},{97,33},{113,49... | collective-permute-start | bytes 5812232 | tf_op jit(solution)/shard_map/ppermute | solution.py:22
  98.0 36.1 %collective-permute-start.28 = (bf16[2,32,11008]{2,1,0:T(8,128)(2,1)S(1)}, bf16[2,32,11008]{2,1,0:T(8,128)(2,1)S(1)}, u32[]{:S(2)}, u32[]{:S(2)}) collective-permute-start(bf16[2,32,11008]{2,1,0:T(8,128)(2,1)S(1)} %copy-done.11), channel_id=1, source_target_pairs={{0,12},{4,8},{8,4},{12,0},{32,36},{36,32},{40,44},{44,40},{1,13},{... | collective-permute-start | bytes 4227080 | tf_op jit(solution)/shard_map/ppermute | solution.py:30
  98.1 37.2 %collective-permute-start.29 = (bf16[2,32,11008]{2,1,0:T(8,128)(2,1)}, bf16[2,32,11008]{2,1,0:T(8,128)(2,1)S(1)}, u32[]{:S(2)}, u32[]{:S(2)}) collective-permute-start(bf16[2,32,11008]{2,1,0:T(8,128)(2,1)} %copy-done.12), channel_id=1, source_target_pairs={{0,3},{1,2},{2,1},{3,0},{32,33},{33,32},{34,35},{35,34},{4,7},{5,6... | collective-permute-start | bytes 4227080 | tf_op jit(solution)/shard_map/ppermute | solution.py:30
  104.6 26.5 %collective-permute-start.22 = (bf16[4,4,256,128]{3,2,1,0:T(8,128)(2,1)S(1)}, bf16[4,4,256,128]{3,2,1,0:T(8,128)(2,1)S(1)}, u32[]{:S(2)}, u32[]{:S(2)}) collective-permute-start(bf16[4,4,256,128]{3,2,1,0:T(8,128)(2,1)S(1)} %pad_maximum_fusion.6), channel_id=1, source_target_pairs={{0,4},{4,0},{8,12},{12,8},{32,44},{36,40},{40,36},{44,32},{1,5},{5... | collective-permute-start | bytes 3145736 | tf_op jit(solution)/shard_map/ppermute | solution.py:30
  106.8 25.8 %collective-permute-start.25 = (bf16[4,4,256,128]{3,2,1,0:T(8,128)(2,1)S(1)}, bf16[4,4,256,128]{3,2,1,0:T(8,128)(2,1)S(1)}, u32[]{:S(2)}, u32[]{:S(2)}) collective-permute-start(bf16[4,4,256,128]{3,2,1,0:T(8,128)(2,1)S(1)} %pad_maximum_fusion.7), channel_id=1, source_target_pairs={{0,1},{1,0},{2,3},{3,2},{32,35},{33,34},{34,33},{35,32},{4,5},{5,4... | collective-permute-start | bytes 3145736 | tf_op jit(solution)/shard_map/ppermute | solution.py:30
  119.5 18.7 %collective-permute-start.32 = (bf16[176,5504]{1,0:T(8,128)(2,1)}, bf16[176,5504]{1,0:T(8,128)(2,1)}, u32[]{:S(2)}, u32[]{:S(2)}) collective-permute-start(bf16[176,5504]{1,0:T(8,128)(2,1)} %collective-permute-done.30.refs_10_), channel_id=1, source_target_pairs={{0,32},{32,0},{1,33},{33,1},{2,34},{34,2},{3,35},{35,3},{4,36},{36... | collective-permute-start | bytes 5812232 | tf_op jit(solution)/shard_map/ppermute | solution.py:51
  136.4 25.3 %collective-permute-start.37 = (bf16[8,4,256,128]{3,2,1,0:T(8,128)(2,1)S(1)}, bf16[8,4,256,128]{3,2,1,0:T(8,128)(2,1)}, u32[]{:S(2)}, u32[]{:S(2)}) collective-permute-start(bf16[8,4,256,128]{3,2,1,0:T(8,128)(2,1)S(1)} %pad_maximum_fusion.refs_4_), channel_id=1, source_target_pairs={{0,12},{4,8},{8,4},{12,0},{32,36},{36,32},{40,44},{44,40},{1,13},{... | collective-permute-start | bytes 6291464 | tf_op jit(solution)/shard_map/ppermute | solution.py:30
  137.1 25.5 %collective-permute-start.38 = (bf16[8,4,256,128]{3,2,1,0:T(8,128)(2,1)}, bf16[8,4,256,128]{3,2,1,0:T(8,128)(2,1)}, u32[]{:S(2)}, u32[]{:S(2)}) collective-permute-start(bf16[8,4,256,128]{3,2,1,0:T(8,128)(2,1)} %pad_maximum_fusion.1.refs_6_), channel_id=1, source_target_pairs={{0,3},{1,2},{2,1},{3,0},{32,33},{33,32},{34,35},{35,34},{4,7},{5,6... | collective-permute-start | bytes 6291464 | tf_op jit(solution)/shard_map/ppermute | solution.py:30
  (31 other events, 241.1 us)

commit v6 on v5

--- a/solution.py
+++ b/solution.py
@@ -286,8 +286,8 @@
     keep, give = rotate_in(after(flag, first, *g2), acts_pieces, basis_in, other_in)
     keep, give = keep.reshape(4, 128, 128), give.reshape(4, 128, 128)
     exchanged = flip_zh(keep), flip_zl(give), flip_both(give)
-    g3 = moved(g2, 2, *a4)
-    g4 = moved(g2, 3, keep)
+    g3 = moved(g2, 2, a4[0])
+    g4 = moved(g2, 3)
     near = jnp.concatenate([after(keep, *g3), exchanged[0]], 1)
     far = jnp.concatenate(after(exchanged[1:], *g3), 1)
 

time: 185 us -> 182 us (0.984)
  waiting for transfers between devices: 89.6 us -> 85.4 us
  starting transfers between devices: 46.6 us -> 50 us
  local copies, waits for them, and re-layouts: 12.9 us -> 10.7 us
    ppermute x2, waiting for transfers between devices: 6.82 us -> 1.96 us  [flip_zh(): return lax.ppermute(v, 'zh', [(0, 1), (1, 0)])]
    ppermute x3, waiting for transfers between devices: 0.01 us -> 3.43 us  [flip_both(): return lax.ppermute(v, ('zl', 'zh'), [(i, 3 - i) for i in range(4)])]
    ppermute x26, waiting for transfers between devices: 68.6 us -> 65.7 us  [near_pairs(): return lambda v: lax.ppermute(v, ('c', axis), table)]
    ppermute x3, starting transfers between devices: 5.43 us -> 8.13 us  [flip_core(): return lax.ppermute(v, 'c', [(0, 1), (1, 0)])]
    unnamed x32, local copies, waits for them, and re-layouts: 5.17 us -> 2.94 us
  transfers between devices with their start and end apart: 40 -> 40, of which waited for: 18 -> 19; matrix products, arithmetic and copies ran while one was open for 10% -> 10% of each run, Pallas kernels for 9% -> 9%
where the time goes in v6:
time: 182 us
  waiting for transfers between devices  85.4 us (47%)
  starting transfers between devices  50 us (27%)
  Pallas kernels  23 us (13%)
  other arithmetic  12.1 us (7%)
  local copies, waits for them, and re-layouts  10.7 us (6%)
    ppermute x26, waiting for transfers between devices, near_pairs(): return lambda v: lax.ppermute(v, ('c', axis), table)  65.7 us
    ppermute x26, starting transfers between devices, near_pairs(): return lambda v: lax.ppermute(v, ('c', axis), table)  25.8 us
    pallas_call x1, Pallas kernels, rotate_out(): pl.pallas_call(rotate_out_kernel, out_shape=(shape, shape), in_specs=[pl....  14.7 us
    ppermute x3, waiting for transfers between devices, relay(): return lax.ppermute(v, ('zl', 'c', 'zh'), table)  11.5 us
    ppermute x3, starting transfers between devices, flip_core(): return lax.ppermute(v, 'c', [(0, 1), (1, 0)])  8.13 us
    pallas_call x1, Pallas kernels, product(): pl.pallas_call(product_kernel, out_shape=(shape, shape), in_specs=[pl.Blo...  6.4 us
    concatenate x14, other arithmetic, joined(): return [jnp.concatenate([v[half], w[half]], axis) for half in halves]  5.68 us
    ppermute x3, starting transfers between devices, flip_both(): return lax.ppermute(v, ('zl', 'zh'), [(i, 3 - i) for i in range(4)])  5.08 us
  transfers between devices with their start and end apart: 40, of which 19 were waited for; matrix products, arithmetic and copies ran while one was open for 10% of the time, Pallas kernels for 9%

profile of v6, /device:TPU:1, one launch (start us, length us, event | category | flops | bytes accessed | tf_op | source)
XLA Modules:
  0.0 181.5 jit_solution(2062706040441912195)
XLA Ops:
  1.0 3.6 %collective-permute-start.10 = (bf16[2,8,4096]{2,1,0:T(8,128)(2,1)S(1)}, bf16[2,8,4096]{2,1,0:T(8,128)(2,1)S(1)}, u32[]{:S(2)}, u32[]{:S(2)}) collective-permute-start(bf16[2,8,4096]{2,1,0:T(8,128)(2,1)S(1)} %get-tuple-element.59), channel_id=1, source_target_pairs={{0,4},{4,0},{8,12},{12,8},{32,44},{36,40},{40,36},{44,32},{1,5},{5... | collective-permute-start | bytes 393224 | tf_op jit(solution)/shard_map/ppermute | solution.py:30
  8.2 3.8 %collective-permute-start = (bf16[2048,128]{1,0:T(8,128)(2,1)S(1)}, bf16[2048,128]{1,0:T(8,128)(2,1)S(1)}, u32[]{:S(2)}, u32[]{:S(2)}) collective-permute-start(bf16[2048,128]{1,0:T(8,128)(2,1)S(1)} %constant_dynamic-slice_fusion), channel_id=1, source_target_pairs={{0,80},{16,64},{64,16},{80,0},{1,81},{17,65},{65,17},{81,1},{2,82}... | collective-permute-start | bytes 1572872 | tf_op jit(solution)/shard_map/ppermute | solution.py:47
  13.5 2.9 %dynamic-slice_bitcast_fusion = bf16[176,5504]{1,0:T(8,128)(2,1)} fusion(bf16[11008,344]{0,1:T(8,128)(2,1)} %param.7, s32[]{:T(128)S(6)} %select_n.30, s32[]{:T(128)S(6)} %select_n.31), kind=kLoop, calls=%fused_computation.2 | loop fusion | bytes 3874824 | tf_op jit(solution)/shard_map/dynamic_slice | solution.py:276
  16.8 4.4 %collective-permute-done.4 = bf16[2,8,11008]{2,1,0:T(8,128)(2,1)S(1)} collective-permute-done((bf16[2,8,11008]{2,1,0:T(8,128)(2,1)S(1)}, bf16[2,8,11008]{2,1,0:T(8,128)(2,1)S(1)}, u32[]{:S(2)}, u32[]{:S(2)}) %collective-permute-start.4) | collective-permute-done | bytes 352288 | tf_op jit(solution)/shard_map/ppermute | solution.py:30
  22.2 2.6 %collective-permute-start.12 = (bf16[2,32,4096]{2,1,0:T(8,128)(2,1)S(1)}, bf16[2,32,4096]{2,1,0:T(8,128)(2,1)S(1)}, u32[]{:S(2)}, u32[]{:S(2)}) collective-permute-start(bf16[2,32,4096]{2,1,0:T(8,128)(2,1)S(1)} %pad_maximum_fusion.11), channel_id=1, source_target_pairs={{0,1},{1,0},{2,3},{3,2},{32,35},{33,34},{34,33},{35,32},{4,5},{5,4... | collective-permute-start | bytes 1572872 | tf_op jit(solution)/shard_map/ppermute | solution.py:30
  24.8 2.7 %collective-permute-start.8 = (bf16[2,32,4096]{2,1,0:T(8,128)(2,1)S(1)}, bf16[2,32,4096]{2,1,0:T(8,128)(2,1)S(1)}, u32[]{:S(2)}, u32[]{:S(2)}) collective-permute-start(bf16[2,32,4096]{2,1,0:T(8,128)(2,1)S(1)} %pad_maximum_fusion.10), channel_id=1, source_target_pairs={{0,4},{4,0},{8,12},{12,8},{32,44},{36,40},{40,36},{44,32},{1,5},{5... | collective-permute-start | bytes 1572872 | tf_op jit(solution)/shard_map/ppermute | solution.py:30
  29.2 10.6 %collective-permute-done.8 = bf16[2,32,4096]{2,1,0:T(8,128)(2,1)S(1)} collective-permute-done((bf16[2,32,4096]{2,1,0:T(8,128)(2,1)S(1)}, bf16[2,32,4096]{2,1,0:T(8,128)(2,1)S(1)}, u32[]{:S(2)}, u32[]{:S(2)}) %collective-permute-start.8) | collective-permute-done | bytes 524320 | tf_op jit(solution)/shard_map/ppermute | solution.py:30
  43.5 11.3 %collective-permute-done.9.refs_1_ = bf16[2,64,4096]{2,1,0:T(8,128)(2,1)S(1)} collective-permute-done((bf16[2,64,4096]{2,1,0:T(8,128)(2,1)S(1)}, bf16[2,64,4096]{2,1,0:T(8,128)(2,1)S(1)}, u32[]{:S(2)}, u32[]{:S(2)}) %collective-permute-start.9) | collective-permute-done | bytes 1048608 | tf_op jit(solution)/shard_map/ppermute | solution.py:30
  62.6 3.3 %broadcast_select_fusion.1 = bf16[176,5504]{1,0:T(8,128)(2,1)} fusion(bf16[176,5504]{1,0:T(8,128)(2,1)S(1)} %collective-permute-done.1, pred[]{:T(512)S(6)} %eq.4, bf16[11008,344]{0,1:T(8,128)(2,1)} %param.7, s32[]{:T(128)S(6)} %select_n.30, s32[]{:T(128)S(6)} %select_n.31), kind=kLoop, calls=%fused_computation.4 | loop fusion | flops 968704 | bytes 5812233 | tf_op jit(solution)/shard_map/jit(_where)/select_n | solution.py:300
  69.0 4.7 %collective-permute-done.15.refs_1_ = bf16[2,32,11008]{2,1,0:T(8,128)(2,1)S(1)} collective-permute-done((bf16[2,32,11008]{2,1,0:T(8,128)(2,1)}, bf16[2,32,11008]{2,1,0:T(8,128)(2,1)S(1)}, u32[]{:S(2)}, u32[]{:S(2)}) %collective-permute-start.15) | collective-permute-done | bytes 1409056 | tf_op jit(solution)/shard_map/ppermute | solution.py:30
  75.3 2.7 %collective-permute-start.23 = (bf16[4,256,128]{2,1,0:T(8,128)(2,1)S(1)}, bf16[4,256,128]{2,1,0:T(8,128)(2,1)S(1)}, u32[]{:S(2)}, u32[]{:S(2)}) collective-permute-start(bf16[4,256,128]{2,1,0:T(8,128)(2,1)S(1)} %bitcast.52), channel_id=1, source_target_pairs={{0,4},{4,0},{8,12},{12,8},{32,44},{36,40},{40,36},{44,32},{1,5},{5... | collective-permute-start | bytes 786440 | tf_op jit(solution)/shard_map/ppermute | solution.py:30
  78.8 6.3 %collective-permute-done.23 = bf16[4,256,128]{2,1,0:T(8,128)(2,1)S(1)} collective-permute-done((bf16[4,256,128]{2,1,0:T(8,128)(2,1)S(1)}, bf16[4,256,128]{2,1,0:T(8,128)(2,1)S(1)}, u32[]{:S(2)}, u32[]{:S(2)}) %collective-permute-start.23) | collective-permute-done | bytes 262176 | tf_op jit(solution)/shard_map/ppermute | solution.py:30
  85.2 3.5 %collective-permute-done.20 = bf16[4,256,128]{2,1,0:T(8,128)(2,1)S(1)} collective-permute-done((bf16[4,256,128]{2,1,0:T(8,128)(2,1)}, bf16[4,256,128]{2,1,0:T(8,128)(2,1)S(1)}, u32[]{:S(2)}, u32[]{:S(2)}) %collective-permute-start.20) | collective-permute-done | bytes 262176 | tf_op jit(solution)/shard_map/ppermute | solution.py:30
  92.4 2.5 %collective-permute-start.31 = (bf16[176,5504]{1,0:T(8,128)(2,1)}, bf16[176,5504]{1,0:T(8,128)(2,1)S(1)}, u32[]{:S(2)}, u32[]{:S(2)}) collective-permute-start(bf16[176,5504]{1,0:T(8,128)(2,1)} %collective-permute-done.30.refs_10_), channel_id=1, source_target_pairs={{32,96},{48,112},{96,32},{112,48},{33,97},{49,113},{97,33},{113,49... | collective-permute-start | bytes 5812232 | tf_op jit(solution)/shard_map/ppermute | solution.py:22
  98.2 5.1 %collective-permute-done.21 = bf16[2,4,256,128]{3,2,1,0:T(8,128)(2,1)S(1)} collective-permute-done((bf16[2,4,256,128]{3,2,1,0:T(8,128)(2,1)S(1)}, bf16[2,4,256,128]{3,2,1,0:T(8,128)(2,1)S(1)}, u32[]{:S(2)}, u32[]{:S(2)}) %collective-permute-start.21) | collective-permute-done | bytes 524320 | tf_op jit(solution)/shard_map/ppermute | solution.py:30
  104.3 3.3 %collective-permute-start.25 = (bf16[4,4,256,128]{3,2,1,0:T(8,128)(2,1)S(1)}, bf16[4,4,256,128]{3,2,1,0:T(8,128)(2,1)S(1)}, u32[]{:S(2)}, u32[]{:S(2)}) collective-permute-start(bf16[4,4,256,128]{3,2,1,0:T(8,128)(2,1)S(1)} %pad_maximum_fusion.7), channel_id=1, source_target_pairs={{0,1},{1,0},{2,3},{3,2},{32,35},{33,34},{34,33},{35,32},{4,5},{5,4... | collective-permute-start | bytes 3145736 | tf_op jit(solution)/shard_map/ppermute | solution.py:30
  107.6 10.3 %collective-permute-done.31 = bf16[176,5504]{1,0:T(8,128)(2,1)S(1)} collective-permute-done((bf16[176,5504]{1,0:T(8,128)(2,1)}, bf16[176,5504]{1,0:T(8,128)(2,1)S(1)}, u32[]{:S(2)}, u32[]{:S(2)}) %collective-permute-start.31) | collective-permute-done | bytes 1937440 | tf_op jit(solution)/shard_map/ppermute | solution.py:22
  119.6 10.4 %collective-permute-done.22 = bf16[4,4,256,128]{3,2,1,0:T(8,128)(2,1)S(1)} collective-permute-done((bf16[4,4,256,128]{3,2,1,0:T(8,128)(2,1)S(1)}, bf16[4,4,256,128]{3,2,1,0:T(8,128)(2,1)S(1)}, u32[]{:S(2)}, u32[]{:S(2)}) %collective-permute-start.22) | collective-permute-done | bytes 1048608 | tf_op jit(solution)/shard_map/ppermute | solution.py:30
  135.1 14.7 %rotate_out.1 = (bf16[344,512]{1,0:T(8,128)(2,1)}, bf16[344,512]{1,0:T(8,128)(2,1)}) custom-call(s32[7]{0:T(128)} %stack.121.place_ref, bf16[2,32,11008]{2,1,0:T(8,128)(2,1)} %pad_maximum_fusion.2.refs_0_, bf16[2,32,11008]{2,1,0:T(8,128)(2,1)} %copy-done.10, bf16[2,32,11008]{2,1,0:T(8,128)(2,1)} %collective-permute-done.26.refs_2_, ...), custom_call_target="tpu_custom_call" | custom-call | flops 7845445632 | bytes 26595328 | tf_op jit(solution)/shard_map/rotate_out/pallas_call | solution.py:166
  153.2 5.2 %collective-permute-done.38.refs_7_ = bf16[8,4,256,128]{3,2,1,0:T(8,128)(2,1)} collective-permute-done((bf16[8,4,256,128]{3,2,1,0:T(8,128)(2,1)}, bf16[8,4,256,128]{3,2,1,0:T(8,128)(2,1)}, u32[]{:S(2)}, u32[]{:S(2)}) %collective-permute-start.38) | collective-permute-done | bytes 2097184 | tf_op jit(solution)/shard_map/ppermute | solution.py:30
  158.5 3.4 %collective-permute-done.36.refs_3_ = bf16[344,512]{1,0:T(8,128)(2,1)S(1)} collective-permute-done((bf16[344,512]{1,0:T(8,128)(2,1)}, bf16[344,512]{1,0:T(8,128)(2,1)S(1)}, u32[]{:S(2)}, u32[]{:S(2)}) %collective-permute-start.36) | collective-permute-done | bytes 352288 | tf_op jit(solution)/shard_map/ppermute | solution.py:47
  163.4 6.4 %squares.1 = (f32[344,1024]{1,0:T(8,128)S(1)}, f32[344,1024]{1,0:T(8,128)S(1)}) custom-call(s32[16]{0:T(128)S(1)} %stack.115.place_ref, bf16[344,512]{1,0:T(8,128)(2,1)S(1)} %copy-done.1, bf16[344,512]{1,0:T(8,128)(2,1)S(1)} %collective-permute-done.34.refs_1_, bf16[344,512]{1,0:T(8,128)(2,1)S(1)} %collective-permute-done.35.refs_2_, ...), custom_call_target="tpu_custom_call" | custom-call | flops 2885681152 | bytes 14000000 | tf_op jit(solution)/shard_map/squares/pallas_call | solution.py:242
  169.8 7.7 %collective-permute-start.39 = (f32[344,1024]{1,0:T(8,128)S(1)}, f32[344,1024]{1,0:T(8,128)S(1)}, u32[]{:S(2)}, u32[]{:S(2)}) collective-permute-start(f32[344,1024]{1,0:T(8,128)S(1)} %get-tuple-element.48), channel_id=1, source_target_pairs={{0,32},{32,0},{1,33},{33,1},{2,34},{34,2},{3,35},{35,3},{4,36},{36... | collective-permute-start | bytes 4227080 | tf_op jit(solution)/shard_map/ppermute | solution.py:51
  177.4 2.8 %collective-permute-done.39 = f32[344,1024]{1,0:T(8,128)S(1)} collective-permute-done((f32[344,1024]{1,0:T(8,128)S(1)}, f32[344,1024]{1,0:T(8,128)S(1)}, u32[]{:S(2)}, u32[]{:S(2)}) %collective-permute-start.39) | collective-permute-done | bytes 1409056 | tf_op jit(solution)/shard_map/ppermute | solution.py:51
  (124 shorter events, 46.7 us)
Async XLA Ops:
  1.0 15.6 %collective-permute-start.10 = (bf16[2,8,4096]{2,1,0:T(8,128)(2,1)S(1)}, bf16[2,8,4096]{2,1,0:T(8,128)(2,1)S(1)}, u32[]{:S(2)}, u32[]{:S(2)}) collective-permute-start(bf16[2,8,4096]{2,1,0:T(8,128)(2,1)S(1)} %get-tuple-element.59), channel_id=1, source_target_pairs={{0,4},{4,0},{8,12},{12,8},{32,44},{36,40},{40,36},{44,32},{1,5},{5... | collective-permute-start | bytes 393224 | tf_op jit(solution)/shard_map/ppermute | solution.py:30
  8.2 20.1 %collective-permute-start = (bf16[2048,128]{1,0:T(8,128)(2,1)S(1)}, bf16[2048,128]{1,0:T(8,128)(2,1)S(1)}, u32[]{:S(2)}, u32[]{:S(2)}) collective-permute-start(bf16[2048,128]{1,0:T(8,128)(2,1)S(1)} %constant_dynamic-slice_fusion), channel_id=1, source_target_pairs={{0,80},{16,64},{64,16},{80,0},{1,81},{17,65},{65,17},{81,1},{2,82}... | collective-permute-start | bytes 1572872 | tf_op jit(solution)/shard_map/ppermute | solution.py:47
  13.3 14.2 %collective-permute-start.2 = (bf16[2,8,11008]{2,1,0:T(8,128)(2,1)S(1)}, bf16[2,8,11008]{2,1,0:T(8,128)(2,1)S(1)}, u32[]{:S(2)}, u32[]{:S(2)}) collective-permute-start(bf16[2,8,11008]{2,1,0:T(8,128)(2,1)S(1)} %get-tuple-element.50), channel_id=1, source_target_pairs={{0,1},{1,0},{2,3},{3,2},{32,35},{33,34},{34,33},{35,32},{4,5},{5,4... | collective-permute-start | bytes 1056776 | tf_op jit(solution)/shard_map/ppermute | solution.py:30
  21.3 19.7 %collective-permute-start.5 = (bf16[2,16,11008]{2,1,0:T(8,128)(2,1)S(1)}, bf16[2,16,11008]{2,1,0:T(8,128)(2,1)S(1)}, u32[]{:S(2)}, u32[]{:S(2)}) collective-permute-start(bf16[2,16,11008]{2,1,0:T(8,128)(2,1)S(1)} %pad_maximum_fusion.9), channel_id=1, source_target_pairs={{0,12},{4,8},{8,4},{12,0},{32,36},{36,32},{40,44},{44,40},{1,13},{... | collective-permute-start | bytes 2113544 | tf_op jit(solution)/shard_map/ppermute | solution.py:30
  22.2 18.5 %collective-permute-start.12 = (bf16[2,32,4096]{2,1,0:T(8,128)(2,1)S(1)}, bf16[2,32,4096]{2,1,0:T(8,128)(2,1)S(1)}, u32[]{:S(2)}, u32[]{:S(2)}) collective-permute-start(bf16[2,32,4096]{2,1,0:T(8,128)(2,1)S(1)} %pad_maximum_fusion.11), channel_id=1, source_target_pairs={{0,1},{1,0},{2,3},{3,2},{32,35},{33,34},{34,33},{35,32},{4,5},{5,4... | collective-permute-start | bytes 1572872 | tf_op jit(solution)/shard_map/ppermute | solution.py:30
  24.8 14.9 %collective-permute-start.8 = (bf16[2,32,4096]{2,1,0:T(8,128)(2,1)S(1)}, bf16[2,32,4096]{2,1,0:T(8,128)(2,1)S(1)}, u32[]{:S(2)}, u32[]{:S(2)}) collective-permute-start(bf16[2,32,4096]{2,1,0:T(8,128)(2,1)S(1)} %pad_maximum_fusion.10), channel_id=1, source_target_pairs={{0,4},{4,0},{8,12},{12,8},{32,44},{36,40},{40,36},{44,32},{1,5},{5... | collective-permute-start | bytes 1572872 | tf_op jit(solution)/shard_map/ppermute | solution.py:30
  27.6 14.7 %collective-permute-start.3 = (bf16[2,16,11008]{2,1,0:T(8,128)(2,1)S(1)}, bf16[2,16,11008]{2,1,0:T(8,128)(2,1)S(1)}, u32[]{:S(2)}, u32[]{:S(2)}) collective-permute-start(bf16[2,16,11008]{2,1,0:T(8,128)(2,1)S(1)} %pad_maximum_fusion.8), channel_id=1, source_target_pairs={{0,3},{1,2},{2,1},{3,0},{32,33},{33,32},{34,35},{35,34},{4,7},{5,6... | collective-permute-start | bytes 2113544 | tf_op jit(solution)/shard_map/ppermute | solution.py:30
  28.2 28.5 %collective-permute-start.1 = (bf16[176,5504]{1,0:T(8,128)(2,1)S(1)}, bf16[176,5504]{1,0:T(8,128)(2,1)S(1)}, u32[]{:S(2)}, u32[]{:S(2)}) collective-permute-start(bf16[176,5504]{1,0:T(8,128)(2,1)S(1)} %copy-done.2), channel_id=1, source_target_pairs={{0,80},{16,64},{64,16},{80,0},{1,81},{17,65},{65,17},{81,1},{2,82}... | collective-permute-start | bytes 5812232 | tf_op jit(solution)/shard_map/ppermute | solution.py:22
  39.7 17.1 %collective-permute-start.14 = (bf16[2048,128]{1,0:T(8,128)(2,1)S(1)}, bf16[2048,128]{1,0:T(8,128)(2,1)S(1)}, u32[]{:S(2)}, u32[]{:S(2)}) collective-permute-start(bf16[2048,128]{1,0:T(8,128)(2,1)S(1)} %collective-permute-done.refs_5_), channel_id=1, source_target_pairs={{0,64},{64,0},{1,65},{65,1},{2,66},{66,2},{3,67},{67,3},{4,68},{68... | collective-permute-start | bytes 1572872 | tf_op jit(solution)/shard_map/ppermute | solution.py:43
  40.8 14.0 %collective-permute-start.9 = (bf16[2,64,4096]{2,1,0:T(8,128)(2,1)S(1)}, bf16[2,64,4096]{2,1,0:T(8,128)(2,1)S(1)}, u32[]{:S(2)}, u32[]{:S(2)}) collective-permute-start(bf16[2,64,4096]{2,1,0:T(8,128)(2,1)S(1)} %pad_maximum_fusion.4.refs_0_), channel_id=1, source_target_pairs={{0,12},{4,8},{8,4},{12,0},{32,36},{36,32},{40,44},{44,40},{1,13},{... | collective-permute-start | bytes 3145736 | tf_op jit(solution)/shard_map/ppermute | solution.py:30
  41.0 15.8 %collective-permute-start.13 = (bf16[2,64,4096]{2,1,0:T(8,128)(2,1)S(1)}, bf16[2,64,4096]{2,1,0:T(8,128)(2,1)S(1)}, u32[]{:S(2)}, u32[]{:S(2)}) collective-permute-start(bf16[2,64,4096]{2,1,0:T(8,128)(2,1)S(1)} %pad_maximum_fusion.5.refs_2_), channel_id=1, source_target_pairs={{0,3},{1,2},{2,1},{3,0},{32,33},{33,32},{34,35},{35,34},{4,7},{5,6... | collective-permute-start | bytes 3145736 | tf_op jit(solution)/shard_map/ppermute | solution.py:30
  54.8 18.9 %collective-permute-start.15 = (bf16[2,32,11008]{2,1,0:T(8,128)(2,1)}, bf16[2,32,11008]{2,1,0:T(8,128)(2,1)S(1)}, u32[]{:S(2)}, u32[]{:S(2)}) collective-permute-start(bf16[2,32,11008]{2,1,0:T(8,128)(2,1)} %pad_maximum_fusion.2.refs_0_), channel_id=1, source_target_pairs={{0,4},{4,0},{8,12},{12,8},{32,44},{36,40},{40,36},{44,32},{1,5},{5... | collective-permute-start | bytes 4227080 | tf_op jit(solution)/shard_map/ppermute | solution.py:30
  54.8 18.9 %collective-permute-start.16 = (bf16[2,32,11008]{2,1,0:T(8,128)(2,1)}, bf16[2,32,11008]{2,1,0:T(8,128)(2,1)S(1)}, u32[]{:S(2)}, u32[]{:S(2)}) collective-permute-start(bf16[2,32,11008]{2,1,0:T(8,128)(2,1)} %pad_maximum_fusion.3.refs_4_), channel_id=1, source_target_pairs={{0,1},{1,0},{2,3},{3,2},{32,35},{33,34},{34,33},{35,32},{4,5},{5,4... | collective-permute-start | bytes 4227080 | tf_op jit(solution)/shard_map/ppermute | solution.py:30
  67.4 25.0 %collective-permute-start.30 = (bf16[176,5504]{1,0:T(8,128)(2,1)}, bf16[176,5504]{1,0:T(8,128)(2,1)}, u32[]{:S(2)}, u32[]{:S(2)}) collective-permute-start(bf16[176,5504]{1,0:T(8,128)(2,1)} %broadcast_select_fusion.1), channel_id=1, source_target_pairs={{0,64},{16,80},{64,0},{80,16},{32,112},{48,96},{96,48},{112,32},{1... | collective-permute-start | bytes 5812232 | tf_op jit(solution)/shard_map/ppermute | solution.py:22
  69.0 22.3 %collective-permute-start.26 = (bf16[2,32,11008]{2,1,0:T(8,128)(2,1)}, bf16[2,32,11008]{2,1,0:T(8,128)(2,1)}, u32[]{:S(2)}, u32[]{:S(2)}) collective-permute-start(bf16[2,32,11008]{2,1,0:T(8,128)(2,1)} %pad_maximum_fusion.2.refs_0_), channel_id=1, source_target_pairs={{0,12},{4,8},{8,4},{12,0},{32,36},{36,32},{40,44},{44,40},{1,13},{... | collective-permute-start | bytes 4227080 | tf_op jit(solution)/shard_map/ppermute | solution.py:30
  69.0 22.3 %collective-permute-start.27 = (bf16[2,32,11008]{2,1,0:T(8,128)(2,1)}, bf16[2,32,11008]{2,1,0:T(8,128)(2,1)}, u32[]{:S(2)}, u32[]{:S(2)}) collective-permute-start(bf16[2,32,11008]{2,1,0:T(8,128)(2,1)} %pad_maximum_fusion.3.refs_4_), channel_id=1, source_target_pairs={{0,3},{1,2},{2,1},{3,0},{32,33},{33,32},{34,35},{35,34},{4,7},{5,6... | collective-permute-start | bytes 4227080 | tf_op jit(solution)/shard_map/ppermute | solution.py:30
  92.4 25.6 %collective-permute-start.31 = (bf16[176,5504]{1,0:T(8,128)(2,1)}, bf16[176,5504]{1,0:T(8,128)(2,1)S(1)}, u32[]{:S(2)}, u32[]{:S(2)}) collective-permute-start(bf16[176,5504]{1,0:T(8,128)(2,1)} %collective-permute-done.30.refs_10_), channel_id=1, source_target_pairs={{32,96},{48,112},{96,32},{112,48},{33,97},{49,113},{97,33},{113,49... | collective-permute-start | bytes 5812232 | tf_op jit(solution)/shard_map/ppermute | solution.py:22
  96.8 33.8 %collective-permute-start.28 = (bf16[2,32,11008]{2,1,0:T(8,128)(2,1)S(1)}, bf16[2,32,11008]{2,1,0:T(8,128)(2,1)S(1)}, u32[]{:S(2)}, u32[]{:S(2)}) collective-permute-start(bf16[2,32,11008]{2,1,0:T(8,128)(2,1)S(1)} %copy-done.11), channel_id=1, source_target_pairs={{0,12},{4,8},{8,4},{12,0},{32,36},{36,32},{40,44},{44,40},{1,13},{... | collective-permute-start | bytes 4227080 | tf_op jit(solution)/shard_map/ppermute | solution.py:30
  96.9 33.7 %collective-permute-start.29 = (bf16[2,32,11008]{2,1,0:T(8,128)(2,1)}, bf16[2,32,11008]{2,1,0:T(8,128)(2,1)S(1)}, u32[]{:S(2)}, u32[]{:S(2)}) collective-permute-start(bf16[2,32,11008]{2,1,0:T(8,128)(2,1)} %copy-done.12), channel_id=1, source_target_pairs={{0,3},{1,2},{2,1},{3,0},{32,33},{33,32},{34,35},{35,34},{4,7},{5,6... | collective-permute-start | bytes 4227080 | tf_op jit(solution)/shard_map/ppermute | solution.py:30
  103.4 26.5 %collective-permute-start.22 = (bf16[4,4,256,128]{3,2,1,0:T(8,128)(2,1)S(1)}, bf16[4,4,256,128]{3,2,1,0:T(8,128)(2,1)S(1)}, u32[]{:S(2)}, u32[]{:S(2)}) collective-permute-start(bf16[4,4,256,128]{3,2,1,0:T(8,128)(2,1)S(1)} %pad_maximum_fusion.6), channel_id=1, source_target_pairs={{0,4},{4,0},{8,12},{12,8},{32,44},{36,40},{40,36},{44,32},{1,5},{5... | collective-permute-start | bytes 3145736 | tf_op jit(solution)/shard_map/ppermute | solution.py:30
  104.3 27.1 %collective-permute-start.25 = (bf16[4,4,256,128]{3,2,1,0:T(8,128)(2,1)S(1)}, bf16[4,4,256,128]{3,2,1,0:T(8,128)(2,1)S(1)}, u32[]{:S(2)}, u32[]{:S(2)}) collective-permute-start(bf16[4,4,256,128]{3,2,1,0:T(8,128)(2,1)S(1)} %pad_maximum_fusion.7), channel_id=1, source_target_pairs={{0,1},{1,0},{2,3},{3,2},{32,35},{33,34},{34,33},{35,32},{4,5},{5,4... | collective-permute-start | bytes 3145736 | tf_op jit(solution)/shard_map/ppermute | solution.py:30
  118.0 17.1 %collective-permute-start.32 = (bf16[176,5504]{1,0:T(8,128)(2,1)}, bf16[176,5504]{1,0:T(8,128)(2,1)}, u32[]{:S(2)}, u32[]{:S(2)}) collective-permute-start(bf16[176,5504]{1,0:T(8,128)(2,1)} %collective-permute-done.30.refs_10_), channel_id=1, source_target_pairs={{0,32},{32,0},{1,33},{33,1},{2,34},{34,2},{3,35},{35,3},{4,36},{36... | collective-permute-start | bytes 5812232 | tf_op jit(solution)/shard_map/ppermute | solution.py:51
  133.0 25.5 %collective-permute-start.38 = (bf16[8,4,256,128]{3,2,1,0:T(8,128)(2,1)}, bf16[8,4,256,128]{3,2,1,0:T(8,128)(2,1)}, u32[]{:S(2)}, u32[]{:S(2)}) collective-permute-start(bf16[8,4,256,128]{3,2,1,0:T(8,128)(2,1)} %pad_maximum_fusion.1.refs_6_), channel_id=1, source_target_pairs={{0,3},{1,2},{2,1},{3,0},{32,33},{33,32},{34,35},{35,34},{4,7},{5,6... | collective-permute-start | bytes 6291464 | tf_op jit(solution)/shard_map/ppermute | solution.py:30
  133.2 25.3 %collective-permute-start.37 = (bf16[8,4,256,128]{3,2,1,0:T(8,128)(2,1)S(1)}, bf16[8,4,256,128]{3,2,1,0:T(8,128)(2,1)}, u32[]{:S(2)}, u32[]{:S(2)}) collective-permute-start(bf16[8,4,256,128]{3,2,1,0:T(8,128)(2,1)S(1)} %pad_maximum_fusion.refs_4_), channel_id=1, source_target_pairs={{0,12},{4,8},{8,4},{12,0},{32,36},{36,32},{40,44},{44,40},{1,13},{... | collective-permute-start | bytes 6291464 | tf_op jit(solution)/shard_map/ppermute | solution.py:30
  (31 other events, 241.2 us)

commit v7 on v6

--- a/solution.py
+++ b/solution.py
@@ -301,7 +301,7 @@
     third = relay(after(second, *c1, *g4), (None, "zl"))
 
     c2 = joined(c1, moved(c1, 1), 0)
-    g5 = moved(g3, 3, *g4)
+    g5 = moved(g3, 3, g4[0])
     grads_pieces = [v[half] for half in halves for v in (g2, g3, g4, g5)]
     c3 = joined(c2, moved(c2, 2), 0)
     c4 = moved(c3, 3, *g5)

time: 182 us -> 182 us (level)
  no operation moved by 1% of the time
where the time goes in v7:
time: 182 us
  waiting for transfers between devices  85.4 us (47%)
  starting transfers between devices  50 us (27%)
  Pallas kernels  23 us (13%)
  other arithmetic  12.1 us (7%)
  local copies, waits for them, and re-layouts  10.7 us (6%)
    ppermute x26, waiting for transfers between devices, near_pairs(): return lambda v: lax.ppermute(v, ('c', axis), table)  65.7 us
    ppermute x26, starting transfers between devices, near_pairs(): return lambda v: lax.ppermute(v, ('c', axis), table)  25.8 us
    pallas_call x1, Pallas kernels, rotate_out(): pl.pallas_call(rotate_out_kernel, out_shape=(shape, shape), in_specs=[pl....  14.7 us
    ppermute x3, waiting for transfers between devices, relay(): return lax.ppermute(v, ('zl', 'c', 'zh'), table)  11.5 us
    ppermute x3, starting transfers between devices, flip_core(): return lax.ppermute(v, 'c', [(0, 1), (1, 0)])  8.13 us
    pallas_call x1, Pallas kernels, product(): pl.pallas_call(product_kernel, out_shape=(shape, shape), in_specs=[pl.Blo...  6.4 us
    concatenate x14, other arithmetic, joined(): return [jnp.concatenate([v[half], w[half]], axis) for half in halves]  5.68 us
    ppermute x3, starting transfers between devices, flip_both(): return lax.ppermute(v, ('zl', 'zh'), [(i, 3 - i) for i in range(4)])  5.08 us
  transfers between devices with their start and end apart: 40, of which 19 were waited for; matrix products, arithmetic and copies ran while one was open for 10% of the time, Pallas kernels for 9%

profile of v7, /device:TPU:1, one launch (start us, length us, event | category | flops | bytes accessed | tf_op | source)
XLA Modules:
  0.0 181.5 jit_solution(2062706040441912195)
XLA Ops:
  1.0 3.6 %collective-permute-start.10 = (bf16[2,8,4096]{2,1,0:T(8,128)(2,1)S(1)}, bf16[2,8,4096]{2,1,0:T(8,128)(2,1)S(1)}, u32[]{:S(2)}, u32[]{:S(2)}) collective-permute-start(bf16[2,8,4096]{2,1,0:T(8,128)(2,1)S(1)} %get-tuple-element.59), channel_id=1, source_target_pairs={{0,4},{4,0},{8,12},{12,8},{32,44},{36,40},{40,36},{44,32},{1,5},{5... | collective-permute-start | bytes 393224 | tf_op jit(solution)/shard_map/ppermute | solution.py:30
  8.2 3.8 %collective-permute-start = (bf16[2048,128]{1,0:T(8,128)(2,1)S(1)}, bf16[2048,128]{1,0:T(8,128)(2,1)S(1)}, u32[]{:S(2)}, u32[]{:S(2)}) collective-permute-start(bf16[2048,128]{1,0:T(8,128)(2,1)S(1)} %constant_dynamic-slice_fusion), channel_id=1, source_target_pairs={{0,80},{16,64},{64,16},{80,0},{1,81},{17,65},{65,17},{81,1},{2,82}... | collective-permute-start | bytes 1572872 | tf_op jit(solution)/shard_map/ppermute | solution.py:47
  13.5 2.9 %dynamic-slice_bitcast_fusion = bf16[176,5504]{1,0:T(8,128)(2,1)} fusion(bf16[11008,344]{0,1:T(8,128)(2,1)} %param.7, s32[]{:T(128)S(6)} %select_n.30, s32[]{:T(128)S(6)} %select_n.31), kind=kLoop, calls=%fused_computation.2 | loop fusion | bytes 3874824 | tf_op jit(solution)/shard_map/dynamic_slice | solution.py:276
  16.8 4.4 %collective-permute-done.4 = bf16[2,8,11008]{2,1,0:T(8,128)(2,1)S(1)} collective-permute-done((bf16[2,8,11008]{2,1,0:T(8,128)(2,1)S(1)}, bf16[2,8,11008]{2,1,0:T(8,128)(2,1)S(1)}, u32[]{:S(2)}, u32[]{:S(2)}) %collective-permute-start.4) | collective-permute-done | bytes 352288 | tf_op jit(solution)/shard_map/ppermute | solution.py:30
  22.2 2.6 %collective-permute-start.12 = (bf16[2,32,4096]{2,1,0:T(8,128)(2,1)S(1)}, bf16[2,32,4096]{2,1,0:T(8,128)(2,1)S(1)}, u32[]{:S(2)}, u32[]{:S(2)}) collective-permute-start(bf16[2,32,4096]{2,1,0:T(8,128)(2,1)S(1)} %pad_maximum_fusion.11), channel_id=1, source_target_pairs={{0,1},{1,0},{2,3},{3,2},{32,35},{33,34},{34,33},{35,32},{4,5},{5,4... | collective-permute-start | bytes 1572872 | tf_op jit(solution)/shard_map/ppermute | solution.py:30
  24.8 2.7 %collective-permute-start.8 = (bf16[2,32,4096]{2,1,0:T(8,128)(2,1)S(1)}, bf16[2,32,4096]{2,1,0:T(8,128)(2,1)S(1)}, u32[]{:S(2)}, u32[]{:S(2)}) collective-permute-start(bf16[2,32,4096]{2,1,0:T(8,128)(2,1)S(1)} %pad_maximum_fusion.10), channel_id=1, source_target_pairs={{0,4},{4,0},{8,12},{12,8},{32,44},{36,40},{40,36},{44,32},{1,5},{5... | collective-permute-start | bytes 1572872 | tf_op jit(solution)/shard_map/ppermute | solution.py:30
  29.2 10.6 %collective-permute-done.8 = bf16[2,32,4096]{2,1,0:T(8,128)(2,1)S(1)} collective-permute-done((bf16[2,32,4096]{2,1,0:T(8,128)(2,1)S(1)}, bf16[2,32,4096]{2,1,0:T(8,128)(2,1)S(1)}, u32[]{:S(2)}, u32[]{:S(2)}) %collective-permute-start.8) | collective-permute-done | bytes 524320 | tf_op jit(solution)/shard_map/ppermute | solution.py:30
  43.5 11.3 %collective-permute-done.9.refs_1_ = bf16[2,64,4096]{2,1,0:T(8,128)(2,1)S(1)} collective-permute-done((bf16[2,64,4096]{2,1,0:T(8,128)(2,1)S(1)}, bf16[2,64,4096]{2,1,0:T(8,128)(2,1)S(1)}, u32[]{:S(2)}, u32[]{:S(2)}) %collective-permute-start.9) | collective-permute-done | bytes 1048608 | tf_op jit(solution)/shard_map/ppermute | solution.py:30
  62.6 3.3 %broadcast_select_fusion.1 = bf16[176,5504]{1,0:T(8,128)(2,1)} fusion(bf16[176,5504]{1,0:T(8,128)(2,1)S(1)} %collective-permute-done.1, pred[]{:T(512)S(6)} %eq.4, bf16[11008,344]{0,1:T(8,128)(2,1)} %param.7, s32[]{:T(128)S(6)} %select_n.30, s32[]{:T(128)S(6)} %select_n.31), kind=kLoop, calls=%fused_computation.4 | loop fusion | flops 968704 | bytes 5812233 | tf_op jit(solution)/shard_map/jit(_where)/select_n | solution.py:300
  69.0 4.7 %collective-permute-done.15.refs_1_ = bf16[2,32,11008]{2,1,0:T(8,128)(2,1)S(1)} collective-permute-done((bf16[2,32,11008]{2,1,0:T(8,128)(2,1)}, bf16[2,32,11008]{2,1,0:T(8,128)(2,1)S(1)}, u32[]{:S(2)}, u32[]{:S(2)}) %collective-permute-start.15) | collective-permute-done | bytes 1409056 | tf_op jit(solution)/shard_map/ppermute | solution.py:30
  75.3 2.7 %collective-permute-start.23 = (bf16[4,256,128]{2,1,0:T(8,128)(2,1)S(1)}, bf16[4,256,128]{2,1,0:T(8,128)(2,1)S(1)}, u32[]{:S(2)}, u32[]{:S(2)}) collective-permute-start(bf16[4,256,128]{2,1,0:T(8,128)(2,1)S(1)} %bitcast.52), channel_id=1, source_target_pairs={{0,4},{4,0},{8,12},{12,8},{32,44},{36,40},{40,36},{44,32},{1,5},{5... | collective-permute-start | bytes 786440 | tf_op jit(solution)/shard_map/ppermute | solution.py:30
  78.8 6.3 %collective-permute-done.23 = bf16[4,256,128]{2,1,0:T(8,128)(2,1)S(1)} collective-permute-done((bf16[4,256,128]{2,1,0:T(8,128)(2,1)S(1)}, bf16[4,256,128]{2,1,0:T(8,128)(2,1)S(1)}, u32[]{:S(2)}, u32[]{:S(2)}) %collective-permute-start.23) | collective-permute-done | bytes 262176 | tf_op jit(solution)/shard_map/ppermute | solution.py:30
  85.2 3.5 %collective-permute-done.20 = bf16[4,256,128]{2,1,0:T(8,128)(2,1)S(1)} collective-permute-done((bf16[4,256,128]{2,1,0:T(8,128)(2,1)}, bf16[4,256,128]{2,1,0:T(8,128)(2,1)S(1)}, u32[]{:S(2)}, u32[]{:S(2)}) %collective-permute-start.20) | collective-permute-done | bytes 262176 | tf_op jit(solution)/shard_map/ppermute | solution.py:30
  92.4 2.5 %collective-permute-start.31 = (bf16[176,5504]{1,0:T(8,128)(2,1)}, bf16[176,5504]{1,0:T(8,128)(2,1)S(1)}, u32[]{:S(2)}, u32[]{:S(2)}) collective-permute-start(bf16[176,5504]{1,0:T(8,128)(2,1)} %collective-permute-done.30.refs_10_), channel_id=1, source_target_pairs={{32,96},{48,112},{96,32},{112,48},{33,97},{49,113},{97,33},{113,49... | collective-permute-start | bytes 5812232 | tf_op jit(solution)/shard_map/ppermute | solution.py:22
  98.2 5.1 %collective-permute-done.21 = bf16[2,4,256,128]{3,2,1,0:T(8,128)(2,1)S(1)} collective-permute-done((bf16[2,4,256,128]{3,2,1,0:T(8,128)(2,1)S(1)}, bf16[2,4,256,128]{3,2,1,0:T(8,128)(2,1)S(1)}, u32[]{:S(2)}, u32[]{:S(2)}) %collective-permute-start.21) | collective-permute-done | bytes 524320 | tf_op jit(solution)/shard_map/ppermute | solution.py:30
  104.3 3.3 %collective-permute-start.25 = (bf16[4,4,256,128]{3,2,1,0:T(8,128)(2,1)S(1)}, bf16[4,4,256,128]{3,2,1,0:T(8,128)(2,1)S(1)}, u32[]{:S(2)}, u32[]{:S(2)}) collective-permute-start(bf16[4,4,256,128]{3,2,1,0:T(8,128)(2,1)S(1)} %pad_maximum_fusion.7), channel_id=1, source_target_pairs={{0,1},{1,0},{2,3},{3,2},{32,35},{33,34},{34,33},{35,32},{4,5},{5,4... | collective-permute-start | bytes 3145736 | tf_op jit(solution)/shard_map/ppermute | solution.py:30
  107.6 10.3 %collective-permute-done.31 = bf16[176,5504]{1,0:T(8,128)(2,1)S(1)} collective-permute-done((bf16[176,5504]{1,0:T(8,128)(2,1)}, bf16[176,5504]{1,0:T(8,128)(2,1)S(1)}, u32[]{:S(2)}, u32[]{:S(2)}) %collective-permute-start.31) | collective-permute-done | bytes 1937440 | tf_op jit(solution)/shard_map/ppermute | solution.py:22
  119.6 10.4 %collective-permute-done.22 = bf16[4,4,256,128]{3,2,1,0:T(8,128)(2,1)S(1)} collective-permute-done((bf16[4,4,256,128]{3,2,1,0:T(8,128)(2,1)S(1)}, bf16[4,4,256,128]{3,2,1,0:T(8,128)(2,1)S(1)}, u32[]{:S(2)}, u32[]{:S(2)}) %collective-permute-start.22) | collective-permute-done | bytes 1048608 | tf_op jit(solution)/shard_map/ppermute | solution.py:30
  135.1 14.7 %rotate_out.1 = (bf16[344,512]{1,0:T(8,128)(2,1)}, bf16[344,512]{1,0:T(8,128)(2,1)}) custom-call(s32[7]{0:T(128)} %stack.121.place_ref, bf16[2,32,11008]{2,1,0:T(8,128)(2,1)} %pad_maximum_fusion.2.refs_0_, bf16[2,32,11008]{2,1,0:T(8,128)(2,1)} %copy-done.10, bf16[2,32,11008]{2,1,0:T(8,128)(2,1)} %collective-permute-done.26.refs_2_, ...), custom_call_target="tpu_custom_call" | custom-call | flops 7845445632 | bytes 26595328 | tf_op jit(solution)/shard_map/rotate_out/pallas_call | solution.py:166
  153.2 5.2 %collective-permute-done.38.refs_7_ = bf16[8,4,256,128]{3,2,1,0:T(8,128)(2,1)} collective-permute-done((bf16[8,4,256,128]{3,2,1,0:T(8,128)(2,1)}, bf16[8,4,256,128]{3,2,1,0:T(8,128)(2,1)}, u32[]{:S(2)}, u32[]{:S(2)}) %collective-permute-start.38) | collective-permute-done | bytes 2097184 | tf_op jit(solution)/shard_map/ppermute | solution.py:30
  158.5 3.4 %collective-permute-done.36.refs_3_ = bf16[344,512]{1,0:T(8,128)(2,1)S(1)} collective-permute-done((bf16[344,512]{1,0:T(8,128)(2,1)}, bf16[344,512]{1,0:T(8,128)(2,1)S(1)}, u32[]{:S(2)}, u32[]{:S(2)}) %collective-permute-start.36) | collective-permute-done | bytes 352288 | tf_op jit(solution)/shard_map/ppermute | solution.py:47
  163.4 6.4 %squares.1 = (f32[344,1024]{1,0:T(8,128)S(1)}, f32[344,1024]{1,0:T(8,128)S(1)}) custom-call(s32[16]{0:T(128)S(1)} %stack.115.place_ref, bf16[344,512]{1,0:T(8,128)(2,1)S(1)} %copy-done.1, bf16[344,512]{1,0:T(8,128)(2,1)S(1)} %collective-permute-done.34.refs_1_, bf16[344,512]{1,0:T(8,128)(2,1)S(1)} %collective-permute-done.35.refs_2_, ...), custom_call_target="tpu_custom_call" | custom-call | flops 2885681152 | bytes 14000000 | tf_op jit(solution)/shard_map/squares/pallas_call | solution.py:242
  169.8 7.7 %collective-permute-start.39 = (f32[344,1024]{1,0:T(8,128)S(1)}, f32[344,1024]{1,0:T(8,128)S(1)}, u32[]{:S(2)}, u32[]{:S(2)}) collective-permute-start(f32[344,1024]{1,0:T(8,128)S(1)} %get-tuple-element.48), channel_id=1, source_target_pairs={{0,32},{32,0},{1,33},{33,1},{2,34},{34,2},{3,35},{35,3},{4,36},{36... | collective-permute-start | bytes 4227080 | tf_op jit(solution)/shard_map/ppermute | solution.py:51
  177.4 2.8 %collective-permute-done.39 = f32[344,1024]{1,0:T(8,128)S(1)} collective-permute-done((f32[344,1024]{1,0:T(8,128)S(1)}, f32[344,1024]{1,0:T(8,128)S(1)}, u32[]{:S(2)}, u32[]{:S(2)}) %collective-permute-start.39) | collective-permute-done | bytes 1409056 | tf_op jit(solution)/shard_map/ppermute | solution.py:51
  (124 shorter events, 46.7 us)
Async XLA Ops:
  1.0 15.6 %collective-permute-start.10 = (bf16[2,8,4096]{2,1,0:T(8,128)(2,1)S(1)}, bf16[2,8,4096]{2,1,0:T(8,128)(2,1)S(1)}, u32[]{:S(2)}, u32[]{:S(2)}) collective-permute-start(bf16[2,8,4096]{2,1,0:T(8,128)(2,1)S(1)} %get-tuple-element.59), channel_id=1, source_target_pairs={{0,4},{4,0},{8,12},{12,8},{32,44},{36,40},{40,36},{44,32},{1,5},{5... | collective-permute-start | bytes 393224 | tf_op jit(solution)/shard_map/ppermute | solution.py:30
  8.2 20.1 %collective-permute-start = (bf16[2048,128]{1,0:T(8,128)(2,1)S(1)}, bf16[2048,128]{1,0:T(8,128)(2,1)S(1)}, u32[]{:S(2)}, u32[]{:S(2)}) collective-permute-start(bf16[2048,128]{1,0:T(8,128)(2,1)S(1)} %constant_dynamic-slice_fusion), channel_id=1, source_target_pairs={{0,80},{16,64},{64,16},{80,0},{1,81},{17,65},{65,17},{81,1},{2,82}... | collective-permute-start | bytes 1572872 | tf_op jit(solution)/shard_map/ppermute | solution.py:47
  13.3 14.2 %collective-permute-start.2 = (bf16[2,8,11008]{2,1,0:T(8,128)(2,1)S(1)}, bf16[2,8,11008]{2,1,0:T(8,128)(2,1)S(1)}, u32[]{:S(2)}, u32[]{:S(2)}) collective-permute-start(bf16[2,8,11008]{2,1,0:T(8,128)(2,1)S(1)} %get-tuple-element.50), channel_id=1, source_target_pairs={{0,1},{1,0},{2,3},{3,2},{32,35},{33,34},{34,33},{35,32},{4,5},{5,4... | collective-permute-start | bytes 1056776 | tf_op jit(solution)/shard_map/ppermute | solution.py:30
  21.3 19.7 %collective-permute-start.5 = (bf16[2,16,11008]{2,1,0:T(8,128)(2,1)S(1)}, bf16[2,16,11008]{2,1,0:T(8,128)(2,1)S(1)}, u32[]{:S(2)}, u32[]{:S(2)}) collective-permute-start(bf16[2,16,11008]{2,1,0:T(8,128)(2,1)S(1)} %pad_maximum_fusion.9), channel_id=1, source_target_pairs={{0,12},{4,8},{8,4},{12,0},{32,36},{36,32},{40,44},{44,40},{1,13},{... | collective-permute-start | bytes 2113544 | tf_op jit(solution)/shard_map/ppermute | solution.py:30
  22.2 18.5 %collective-permute-start.12 = (bf16[2,32,4096]{2,1,0:T(8,128)(2,1)S(1)}, bf16[2,32,4096]{2,1,0:T(8,128)(2,1)S(1)}, u32[]{:S(2)}, u32[]{:S(2)}) collective-permute-start(bf16[2,32,4096]{2,1,0:T(8,128)(2,1)S(1)} %pad_maximum_fusion.11), channel_id=1, source_target_pairs={{0,1},{1,0},{2,3},{3,2},{32,35},{33,34},{34,33},{35,32},{4,5},{5,4... | collective-permute-start | bytes 1572872 | tf_op jit(solution)/shard_map/ppermute | solution.py:30
  24.8 14.9 %collective-permute-start.8 = (bf16[2,32,4096]{2,1,0:T(8,128)(2,1)S(1)}, bf16[2,32,4096]{2,1,0:T(8,128)(2,1)S(1)}, u32[]{:S(2)}, u32[]{:S(2)}) collective-permute-start(bf16[2,32,4096]{2,1,0:T(8,128)(2,1)S(1)} %pad_maximum_fusion.10), channel_id=1, source_target_pairs={{0,4},{4,0},{8,12},{12,8},{32,44},{36,40},{40,36},{44,32},{1,5},{5... | collective-permute-start | bytes 1572872 | tf_op jit(solution)/shard_map/ppermute | solution.py:30
  27.6 14.7 %collective-permute-start.3 = (bf16[2,16,11008]{2,1,0:T(8,128)(2,1)S(1)}, bf16[2,16,11008]{2,1,0:T(8,128)(2,1)S(1)}, u32[]{:S(2)}, u32[]{:S(2)}) collective-permute-start(bf16[2,16,11008]{2,1,0:T(8,128)(2,1)S(1)} %pad_maximum_fusion.8), channel_id=1, source_target_pairs={{0,3},{1,2},{2,1},{3,0},{32,33},{33,32},{34,35},{35,34},{4,7},{5,6... | collective-permute-start | bytes 2113544 | tf_op jit(solution)/shard_map/ppermute | solution.py:30
  28.2 28.5 %collective-permute-start.1 = (bf16[176,5504]{1,0:T(8,128)(2,1)S(1)}, bf16[176,5504]{1,0:T(8,128)(2,1)S(1)}, u32[]{:S(2)}, u32[]{:S(2)}) collective-permute-start(bf16[176,5504]{1,0:T(8,128)(2,1)S(1)} %copy-done.2), channel_id=1, source_target_pairs={{0,80},{16,64},{64,16},{80,0},{1,81},{17,65},{65,17},{81,1},{2,82}... | collective-permute-start | bytes 5812232 | tf_op jit(solution)/shard_map/ppermute | solution.py:22
  39.7 17.1 %collective-permute-start.14 = (bf16[2048,128]{1,0:T(8,128)(2,1)S(1)}, bf16[2048,128]{1,0:T(8,128)(2,1)S(1)}, u32[]{:S(2)}, u32[]{:S(2)}) collective-permute-start(bf16[2048,128]{1,0:T(8,128)(2,1)S(1)} %collective-permute-done.refs_5_), channel_id=1, source_target_pairs={{0,64},{64,0},{1,65},{65,1},{2,66},{66,2},{3,67},{67,3},{4,68},{68... | collective-permute-start | bytes 1572872 | tf_op jit(solution)/shard_map/ppermute | solution.py:43
  40.8 14.0 %collective-permute-start.9 = (bf16[2,64,4096]{2,1,0:T(8,128)(2,1)S(1)}, bf16[2,64,4096]{2,1,0:T(8,128)(2,1)S(1)}, u32[]{:S(2)}, u32[]{:S(2)}) collective-permute-start(bf16[2,64,4096]{2,1,0:T(8,128)(2,1)S(1)} %pad_maximum_fusion.4.refs_0_), channel_id=1, source_target_pairs={{0,12},{4,8},{8,4},{12,0},{32,36},{36,32},{40,44},{44,40},{1,13},{... | collective-permute-start | bytes 3145736 | tf_op jit(solution)/shard_map/ppermute | solution.py:30
  41.0 15.8 %collective-permute-start.13 = (bf16[2,64,4096]{2,1,0:T(8,128)(2,1)S(1)}, bf16[2,64,4096]{2,1,0:T(8,128)(2,1)S(1)}, u32[]{:S(2)}, u32[]{:S(2)}) collective-permute-start(bf16[2,64,4096]{2,1,0:T(8,128)(2,1)S(1)} %pad_maximum_fusion.5.refs_2_), channel_id=1, source_target_pairs={{0,3},{1,2},{2,1},{3,0},{32,33},{33,32},{34,35},{35,34},{4,7},{5,6... | collective-permute-start | bytes 3145736 | tf_op jit(solution)/shard_map/ppermute | solution.py:30
  54.8 18.9 %collective-permute-start.15 = (bf16[2,32,11008]{2,1,0:T(8,128)(2,1)}, bf16[2,32,11008]{2,1,0:T(8,128)(2,1)S(1)}, u32[]{:S(2)}, u32[]{:S(2)}) collective-permute-start(bf16[2,32,11008]{2,1,0:T(8,128)(2,1)} %pad_maximum_fusion.2.refs_0_), channel_id=1, source_target_pairs={{0,4},{4,0},{8,12},{12,8},{32,44},{36,40},{40,36},{44,32},{1,5},{5... | collective-permute-start | bytes 4227080 | tf_op jit(solution)/shard_map/ppermute | solution.py:30
  54.8 18.9 %collective-permute-start.16 = (bf16[2,32,11008]{2,1,0:T(8,128)(2,1)}, bf16[2,32,11008]{2,1,0:T(8,128)(2,1)S(1)}, u32[]{:S(2)}, u32[]{:S(2)}) collective-permute-start(bf16[2,32,11008]{2,1,0:T(8,128)(2,1)} %pad_maximum_fusion.3.refs_4_), channel_id=1, source_target_pairs={{0,1},{1,0},{2,3},{3,2},{32,35},{33,34},{34,33},{35,32},{4,5},{5,4... | collective-permute-start | bytes 4227080 | tf_op jit(solution)/shard_map/ppermute | solution.py:30
  67.4 25.0 %collective-permute-start.30 = (bf16[176,5504]{1,0:T(8,128)(2,1)}, bf16[176,5504]{1,0:T(8,128)(2,1)}, u32[]{:S(2)}, u32[]{:S(2)}) collective-permute-start(bf16[176,5504]{1,0:T(8,128)(2,1)} %broadcast_select_fusion.1), channel_id=1, source_target_pairs={{0,64},{16,80},{64,0},{80,16},{32,112},{48,96},{96,48},{112,32},{1... | collective-permute-start | bytes 5812232 | tf_op jit(solution)/shard_map/ppermute | solution.py:22
  69.0 22.3 %collective-permute-start.26 = (bf16[2,32,11008]{2,1,0:T(8,128)(2,1)}, bf16[2,32,11008]{2,1,0:T(8,128)(2,1)}, u32[]{:S(2)}, u32[]{:S(2)}) collective-permute-start(bf16[2,32,11008]{2,1,0:T(8,128)(2,1)} %pad_maximum_fusion.2.refs_0_), channel_id=1, source_target_pairs={{0,12},{4,8},{8,4},{12,0},{32,36},{36,32},{40,44},{44,40},{1,13},{... | collective-permute-start | bytes 4227080 | tf_op jit(solution)/shard_map/ppermute | solution.py:30
  69.0 22.3 %collective-permute-start.28 = (bf16[2,32,11008]{2,1,0:T(8,128)(2,1)}, bf16[2,32,11008]{2,1,0:T(8,128)(2,1)}, u32[]{:S(2)}, u32[]{:S(2)}) collective-permute-start(bf16[2,32,11008]{2,1,0:T(8,128)(2,1)} %pad_maximum_fusion.3.refs_4_), channel_id=1, source_target_pairs={{0,3},{1,2},{2,1},{3,0},{32,33},{33,32},{34,35},{35,34},{4,7},{5,6... | collective-permute-start | bytes 4227080 | tf_op jit(solution)/shard_map/ppermute | solution.py:30
  92.4 25.6 %collective-permute-start.31 = (bf16[176,5504]{1,0:T(8,128)(2,1)}, bf16[176,5504]{1,0:T(8,128)(2,1)S(1)}, u32[]{:S(2)}, u32[]{:S(2)}) collective-permute-start(bf16[176,5504]{1,0:T(8,128)(2,1)} %collective-permute-done.30.refs_10_), channel_id=1, source_target_pairs={{32,96},{48,112},{96,32},{112,48},{33,97},{49,113},{97,33},{113,49... | collective-permute-start | bytes 5812232 | tf_op jit(solution)/shard_map/ppermute | solution.py:22
  96.8 33.8 %collective-permute-start.27 = (bf16[2,32,11008]{2,1,0:T(8,128)(2,1)S(1)}, bf16[2,32,11008]{2,1,0:T(8,128)(2,1)S(1)}, u32[]{:S(2)}, u32[]{:S(2)}) collective-permute-start(bf16[2,32,11008]{2,1,0:T(8,128)(2,1)S(1)} %copy-done.11), channel_id=1, source_target_pairs={{0,12},{4,8},{8,4},{12,0},{32,36},{36,32},{40,44},{44,40},{1,13},{... | collective-permute-start | bytes 4227080 | tf_op jit(solution)/shard_map/ppermute | solution.py:30
  96.9 33.7 %collective-permute-start.29 = (bf16[2,32,11008]{2,1,0:T(8,128)(2,1)}, bf16[2,32,11008]{2,1,0:T(8,128)(2,1)S(1)}, u32[]{:S(2)}, u32[]{:S(2)}) collective-permute-start(bf16[2,32,11008]{2,1,0:T(8,128)(2,1)} %copy-done.12), channel_id=1, source_target_pairs={{0,3},{1,2},{2,1},{3,0},{32,33},{33,32},{34,35},{35,34},{4,7},{5,6... | collective-permute-start | bytes 4227080 | tf_op jit(solution)/shard_map/ppermute | solution.py:30
  103.4 26.5 %collective-permute-start.22 = (bf16[4,4,256,128]{3,2,1,0:T(8,128)(2,1)S(1)}, bf16[4,4,256,128]{3,2,1,0:T(8,128)(2,1)S(1)}, u32[]{:S(2)}, u32[]{:S(2)}) collective-permute-start(bf16[4,4,256,128]{3,2,1,0:T(8,128)(2,1)S(1)} %pad_maximum_fusion.6), channel_id=1, source_target_pairs={{0,4},{4,0},{8,12},{12,8},{32,44},{36,40},{40,36},{44,32},{1,5},{5... | collective-permute-start | bytes 3145736 | tf_op jit(solution)/shard_map/ppermute | solution.py:30
  104.3 27.1 %collective-permute-start.25 = (bf16[4,4,256,128]{3,2,1,0:T(8,128)(2,1)S(1)}, bf16[4,4,256,128]{3,2,1,0:T(8,128)(2,1)S(1)}, u32[]{:S(2)}, u32[]{:S(2)}) collective-permute-start(bf16[4,4,256,128]{3,2,1,0:T(8,128)(2,1)S(1)} %pad_maximum_fusion.7), channel_id=1, source_target_pairs={{0,1},{1,0},{2,3},{3,2},{32,35},{33,34},{34,33},{35,32},{4,5},{5,4... | collective-permute-start | bytes 3145736 | tf_op jit(solution)/shard_map/ppermute | solution.py:30
  118.0 17.1 %collective-permute-start.32 = (bf16[176,5504]{1,0:T(8,128)(2,1)}, bf16[176,5504]{1,0:T(8,128)(2,1)}, u32[]{:S(2)}, u32[]{:S(2)}) collective-permute-start(bf16[176,5504]{1,0:T(8,128)(2,1)} %collective-permute-done.30.refs_10_), channel_id=1, source_target_pairs={{0,32},{32,0},{1,33},{33,1},{2,34},{34,2},{3,35},{35,3},{4,36},{36... | collective-permute-start | bytes 5812232 | tf_op jit(solution)/shard_map/ppermute | solution.py:51
  133.0 25.5 %collective-permute-start.38 = (bf16[8,4,256,128]{3,2,1,0:T(8,128)(2,1)}, bf16[8,4,256,128]{3,2,1,0:T(8,128)(2,1)}, u32[]{:S(2)}, u32[]{:S(2)}) collective-permute-start(bf16[8,4,256,128]{3,2,1,0:T(8,128)(2,1)} %pad_maximum_fusion.1.refs_6_), channel_id=1, source_target_pairs={{0,3},{1,2},{2,1},{3,0},{32,33},{33,32},{34,35},{35,34},{4,7},{5,6... | collective-permute-start | bytes 6291464 | tf_op jit(solution)/shard_map/ppermute | solution.py:30
  133.2 25.3 %collective-permute-start.37 = (bf16[8,4,256,128]{3,2,1,0:T(8,128)(2,1)S(1)}, bf16[8,4,256,128]{3,2,1,0:T(8,128)(2,1)}, u32[]{:S(2)}, u32[]{:S(2)}) collective-permute-start(bf16[8,4,256,128]{3,2,1,0:T(8,128)(2,1)S(1)} %pad_maximum_fusion.refs_4_), channel_id=1, source_target_pairs={{0,12},{4,8},{8,4},{12,0},{32,36},{36,32},{40,44},{44,40},{1,13},{... | collective-permute-start | bytes 6291464 | tf_op jit(solution)/shard_map/ppermute | solution.py:30
  (31 other events, 241.2 us)
